TPU v7x, 512 devices: a whole 4x8x8 slice. The times are simulated.
512 devices in a mesh: lat: 16 (over z_hi, x), lon: 32 (over z_lo, y, core).
Axes of the slice: x: 4, y: 8, z: 8 (z_hi: 4, z_lo: 2; z = z_hi * 2 + z_lo), core: 2. Of those that a mesh axis runs over, the one named last changes fastest.
Arguments:
- state_grid: bfloat16 [1, 384, 768, 256], P(None, 'lat', 'lon'), may hold values from -6 to 6
- spectral_filter: float32 [384, 256], P(None, 'lon'), may hold values from -6 to 6
- up_weight: bfloat16 [256, 512], replicated, may hold values from -0.375 to 0.375
- down_weight: bfloat16 [256, 512], replicated, may hold values from -0.25 to 0.25
- cotangent: bfloat16 [1, 384, 768, 256], P(None, 'lat', 'lon'), may hold values from -6 to 6
Outputs:
- grad_field: bfloat16 [1, 384, 768, 256], P(None, 'lat', 'lon')
- grad_up: float32 [256, 512], P('lat')
- grad_down: float32 [256, 512], P('lat')
All inputs are finite; a program needn't handle non-finite values.
Results may differ from a plain program's by a relative error of at most 0.018.
Values may be sent and summed in bfloat16 or wider, within the bound.
No kernel may reach another device: no remote copies, remote signals or barrier semaphores. Data moves between devices by JAX's collectives and lax.ppermute only.
A program may use at most 64 MiB of HBM per device.

v0:
```python
import math

import jax
import jax.numpy as jnp
from jax import lax
from jax.sharding import PartitionSpec as P

L = 384


def fourier_tables(lon_total, order_total):
    lon_index = jnp.arange(lon_total, dtype=jnp.int32)
    order_index = jnp.arange(order_total, dtype=jnp.int32)
    phases = lon_index[:, None] * order_index[None, :] % lon_total
    angles = phases.astype(jnp.float32) * (2.0 * math.pi / lon_total)
    cosine = jnp.cos(angles)
    sines = jnp.sin(angles)
    forward = jnp.concatenate([cosine, -sines], axis=1).astype(jnp.bfloat16)
    doubling = jnp.where(order_index == 0, 1.0, 2.0).astype(jnp.float32)
    inverse = jnp.concatenate(
        [(cosine * doubling[None, :]).T, (-sines * doubling[None, :]).T], axis=0
    ).astype(jnp.bfloat16)
    return (forward, inverse)


def row_scale(lat_total, lon_total):
    colatitude = (jnp.arange(lat_total, dtype=jnp.float32) + 0.5) * (math.pi / lat_total)
    counter = jnp.arange(1, lat_total // 2 + 1, dtype=jnp.float32)
    series = jnp.sum(
        jnp.cos(2.0 * counter[None, :] * colatitude[:, None])
        / (4.0 * counter * counter - 1.0)[None, :],
        axis=1,
    )
    return 2.0 / lat_total * (1.0 - 2.0 * series) * (2.0 * math.pi / lon_total)


def combine_transfer(early, late):
    e00, e01, e10, e11, early_log = early
    l00, l01, l10, l11, late_log = late
    p00 = l00 * e00 + l01 * e10
    p01 = l00 * e01 + l01 * e11
    p10 = l10 * e00 + l11 * e10
    p11 = l10 * e01 + l11 * e11
    largest = jnp.maximum(
        jnp.maximum(jnp.abs(p00), jnp.abs(p01)), jnp.maximum(jnp.abs(p10), jnp.abs(p11))
    )
    return (
        p00 / largest,
        p01 / largest,
        p10 / largest,
        p11 / largest,
        early_log + jnp.log(largest),
    )


def legendre_table(order_first, order_count, lat_total, degrees):
    half_rows = lat_total // 2
    colatitude = (jnp.arange(half_rows, dtype=jnp.float32) + 0.5) * (math.pi / lat_total)
    cosine = jnp.cos(colatitude)
    log_sine = jnp.log(jnp.sin(colatitude))
    later = jnp.arange(1, degrees, dtype=jnp.float32)
    ratios = jnp.log((2.0 * later - 1.0) / (2.0 * later))
    every_order = jnp.arange(degrees, dtype=jnp.float32)
    partial_logs = jnp.sum(
        jnp.where(later[None, :] <= every_order[:, None], ratios[None, :], 0.0), axis=1
    )
    base_logs = 0.5 * (jnp.log((2.0 * every_order + 1.0) / (4.0 * math.pi)) + partial_logs)
    base_logs = lax.dynamic_slice_in_dim(base_logs, order_first, order_count)
    orders = (order_first + jnp.arange(order_count, dtype=jnp.int32)).astype(jnp.float32)[:, None]
    diag_logs = base_logs[:, None] + orders * log_sine[None, :]
    squares = orders * orders
    full_shape = (order_count, half_rows)
    block_len = 16

    def one_block(carry, block_index):
        outputs = []
        for inner in range(block_len):
            degree_val = (block_index * block_len + inner).astype(jnp.float32)
            spread = jnp.maximum(degree_val * degree_val - squares, 1.0)
            growth = jnp.sqrt(jnp.maximum(4.0 * degree_val * degree_val - 1.0, 1.0) / spread)
            lower_deg = degree_val - 1.0
            damping = jnp.sqrt(
                jnp.maximum(lower_deg * lower_deg - squares, 0.0)
                / jnp.maximum(4.0 * lower_deg * lower_deg - 1.0, 1.0)
            )
            live = jnp.broadcast_to(degree_val > orders, full_shape)
            top_left = jnp.where(live, growth * cosine[None, :], 1.0)
            top_right = jnp.where(live, jnp.broadcast_to(-growth * damping, full_shape), 0.0)
            bottom_left = jnp.where(live, 1.0, 0.0).astype(jnp.float32)
            bottom_right = jnp.where(live, 0.0, 1.0).astype(jnp.float32)
            log_zero = jnp.zeros(full_shape, jnp.float32)
            carry = combine_transfer(
                carry, (top_left, top_right, bottom_left, bottom_right, log_zero)
            )
            values = jnp.exp(diag_logs + carry[4]) * carry[0]
            values = jnp.where(degree_val >= orders, values, 0.0)
            outputs.append(values.astype(jnp.bfloat16))
        return (carry, jnp.stack(outputs))

    ones_init = jnp.ones(full_shape, jnp.float32)
    zeros_init = jnp.zeros(full_shape, jnp.float32)
    start_carry = (ones_init, zeros_init, zeros_init, ones_init, zeros_init)
    _, blocks = lax.scan(one_block, start_carry, jnp.arange(degrees // block_len, dtype=jnp.int32))
    return blocks.reshape(degrees, order_count, half_rows)


def parity_signs(order_first, order_count, degrees):
    degree_index = jnp.arange(degrees, dtype=jnp.int32)
    order_index = order_first + jnp.arange(order_count, dtype=jnp.int32)
    return (1 - 2 * ((degree_index[:, None] + order_index[None, :]) % 2)).astype(jnp.float32)


def analysis(fourier_modes, legendre, parity):
    half_rows = legendre.shape[2]
    northern = fourier_modes[:, :half_rows]
    southern = jnp.flip(fourier_modes[:, half_rows:], axis=1)
    north_sum = jnp.einsum(
        "lmk,bkcpm->bcplm", legendre, northern, preferred_element_type=jnp.float32
    )
    south_sum = jnp.einsum(
        "lmk,bkcpm->bcplm", legendre, southern, preferred_element_type=jnp.float32
    )
    return north_sum + parity * south_sum


def synthesis(coefs, legendre, parity_low):
    north_sum = jnp.einsum("lmk,bcplm->bkcpm", legendre, coefs, preferred_element_type=jnp.float32)
    mirrored = coefs * parity_low
    south_sum = jnp.einsum(
        "lmk,bcplm->bkcpm", legendre, mirrored, preferred_element_type=jnp.float32
    )
    return jnp.concatenate([north_sum, jnp.flip(south_sum, axis=1)], axis=1)


def gelu_slope(values):
    normal_cdf = 0.5 * (1.0 + lax.erf(values / math.sqrt(2.0)))
    return normal_cdf + values * jnp.exp(-0.5 * values * values) / math.sqrt(2.0 * math.pi)


def to_spectral(grid_vals, fourier_table, einsum_form, weights_rows, legendre, parity):
    whole_rows = lax.all_to_all(grid_vals, "lon", split_axis=3, concat_axis=2, tiled=True)
    fourier_modes = jnp.einsum(
        einsum_form, whole_rows, fourier_table, preferred_element_type=jnp.float32
    )
    if weights_rows is not None:
        fourier_modes = fourier_modes * weights_rows[None, :, None, None]
    fourier_modes = fourier_modes.astype(jnp.bfloat16)
    dims_now = fourier_modes.shape
    fourier_modes = fourier_modes.reshape(
        dims_now[0], dims_now[1], dims_now[2], 2, dims_now[3] // 2
    )
    turned = lax.all_to_all(fourier_modes, "lat", split_axis=4, concat_axis=1, tiled=True)
    return analysis(turned, legendre, parity)


def to_grid(coefs, fourier_table, einsum_form, weights_rows, legendre, parity_low):
    wave_rows = synthesis(coefs, legendre, parity_low).astype(jnp.bfloat16)
    returned = lax.all_to_all(wave_rows, "lat", split_axis=1, concat_axis=4, tiled=True)
    dims_now = returned.shape
    flat_waves = returned.reshape(dims_now[0], dims_now[1], dims_now[2], dims_now[3] * dims_now[4])
    grid_vals = jnp.einsum(
        einsum_form, flat_waves, fourier_table, preferred_element_type=jnp.float32
    )
    if weights_rows is not None:
        grid_vals = grid_vals * weights_rows[None, :, None, None]
    return lax.all_to_all(
        grid_vals.astype(jnp.bfloat16), "lon", split_axis=2, concat_axis=3, tiled=True
    )


def body(state_grid, spectral_filter, up_weight, down_weight, cotangent):
    members, lat_rows, lon_cols, channels = state_grid.shape
    lat_count = lax.axis_size("lat")
    lat_pos = lax.axis_index("lat")
    lat_total = lat_rows * lat_count
    lon_total = lon_cols * lax.axis_size("lon")
    order_count = L // lat_count
    order_first = lat_pos * order_count
    forward_table, inverse_table = fourier_tables(lon_total, L)
    weights_all = row_scale(lat_total, lon_total)
    row_weights = lax.dynamic_slice_in_dim(weights_all, lat_pos * lat_rows, lat_rows)
    legendre = legendre_table(order_first, order_count, lat_total, L)
    parity = parity_signs(order_first, order_count, L)
    parity_low = parity.astype(jnp.bfloat16)
    filter_gains = spectral_filter.T[None, :, None, :, None]
    spectrum = to_spectral(
        state_grid, forward_table, "bkjc,jn->bkcn", row_weights, legendre, parity
    )
    filtered = (spectrum * filter_gains).astype(jnp.bfloat16)
    smooth = to_grid(filtered, inverse_table, "bkcn,nj->bkjc", None, legendre, parity_low)
    mixed_grid = (state_grid.astype(jnp.float32) + smooth.astype(jnp.float32)).astype(jnp.bfloat16)
    flat_mixed = mixed_grid.reshape(-1, channels)
    pre_active = jnp.dot(flat_mixed, up_weight, preferred_element_type=jnp.float32)
    active = jax.nn.gelu(pre_active, approximate=False).astype(jnp.bfloat16)
    flat_cotangent = cotangent.reshape(-1, channels)
    back_active = jnp.dot(flat_cotangent, down_weight, preferred_element_type=jnp.float32)
    back_pre = (back_active * gelu_slope(pre_active)).astype(jnp.bfloat16)
    back_mixed = flat_cotangent.astype(jnp.float32) + jnp.einsum(
        "ph,ch->pc", back_pre, up_weight, preferred_element_type=jnp.float32
    )
    back_round = back_mixed.astype(jnp.bfloat16).reshape(state_grid.shape)
    back_spectrum = to_spectral(back_round, inverse_table, "bkjc,nj->bkcn", None, legendre, parity)
    back_filtered = (back_spectrum * filter_gains).astype(jnp.bfloat16)
    back_field = to_grid(
        back_filtered, forward_table, "bkcn,jn->bkjc", row_weights, legendre, parity_low
    )
    grad_field = (back_mixed.reshape(state_grid.shape) + back_field.astype(jnp.float32)).astype(
        jnp.bfloat16
    )
    grad_scale = 1.0 / math.sqrt(members * lat_total * lon_total)
    kept_count = channels // lat_count
    up_part = jnp.einsum("pc,ph->ch", flat_mixed, back_pre, preferred_element_type=jnp.float32)
    down_part = jnp.einsum("pc,ph->ch", flat_cotangent, active, preferred_element_type=jnp.float32)
    summed_all = lax.psum(
        jnp.concatenate([up_part, down_part], axis=1) * grad_scale, ("lat", "lon")
    )
    kept_rows = lax.dynamic_slice_in_dim(summed_all, lat_pos * kept_count, kept_count, 0)
    hidden_units = up_weight.shape[1]
    return (grad_field, kept_rows[:, :hidden_units], kept_rows[:, hidden_units:])


def solution(mesh):
    placed = (P(None, "lat", "lon", None), P(None, "lon"), P(), P(), P(None, "lat", "lon", None))
    return jax.shard_map(
        body,
        mesh=mesh,
        in_specs=placed,
        out_specs=(P(None, "lat", "lon", None), P("lat", None), P("lat", None)),
        check_vma=False,
    )
```

profile of v0, /device:TPU:1, one launch (start us, length us, event | category | flops | bytes accessed | tf_op | source)
XLA Modules:
  0.0 644.5 jit_solution(16409379368668702964)
XLA Ops:
  9.0 2.9 reshape.1396
  11.9 10.9 %all-to-all-start = ((bf16[32,2,2304]{2,1,0:T(2,128)(2,1)}), bf16[32,2,2304]{2,1,0:T(2,128)(2,1)S(1)}, u32[]{:S(2)}, u32[]{:S(2)}) async-start(bf16[32,2,2304]{2,1,0:T(2,128)(2,1)} %reshape.1396), calls=%async_computation | async-start | bytes 589824 | tf_op jit(solution)/shard_map/all_to_all | solution.py:141
  24.4 5.0 negate_convert_fusion
  29.5 5.7 all-to-all-done
  35.1 2.2 reshape.1397
  38.0 2.9 reshape.1395
  43.0 2.9 reshape.1398
  45.8 11.9 %all-to-all-start.1 = ((bf16[16,2,4608]{2,1,0:T(2,128)(2,1)}), bf16[16,2,4608]{2,1,0:T(2,128)(2,1)S(1)}, u32[]{:S(2)}, u32[]{:S(2)}) async-start(bf16[16,2,4608]{2,1,0:T(2,128)(2,1)} %reshape.1398), calls=%async_computation.1 | async-start | bytes 589824 | tf_op jit(solution)/shard_map/all_to_all | solution.py:152
  57.8 115.2 %while.27 = (s32[]{:T(128)}, f32[24,192]{1,0:T(8,128)S(1)}, f32[24,192]{1,0:T(8,128)S(1)}, f32[24,192]{1,0:T(8,128)S(1)}, f32[24,192]{1,0:T(8,128)S(1)}, /*index...) while((s32[]{:T(128)}, f32[24,192]{1,0:T(8,128)S(1)}, ...), condition=%wide.region_3.4_spmd.clone.clone.clone.clone, body=%wide.region_2.3_spmd.clone.clone.clone.clone.sunk | while | flops 2568594 | bytes 5267075 | solution.py:103
  173.0 6.8 %copy.211 = bf16[384,24,192,1]{0,2,3,1:T(8,128)(2,1)} copy(bf16[384,24,192,1]{2,1,0,3:T(8,128)(2,1)} %bitcast.589) | data formatting | bytes 7077888 | tf_op jit(solution)/shard_map/reshape | solution.py:104
  179.9 2.2 reshape.1399
  186.0 2.7 convolution_bitcast_fusion.3
  189.0 2.9 fusion.148
  197.0 2.9 reshape.1400
  199.9 9.2 %all-to-all-start.2 = ((bf16[16,2,4608]{2,1,0:T(2,128)(2,1)}), bf16[16,2,4608]{2,1,0:T(2,128)(2,1)S(1)}, u32[]{:S(2)}, u32[]{:S(2)}) async-start(bf16[16,2,4608]{2,1,0:T(2,128)(2,1)} %reshape.1400), calls=%async_computation.2 | async-start | bytes 589824 | tf_op jit(solution)/shard_map/all_to_all | solution.py:158
  209.1 5.8 multiply_convert_fusion.1
  214.9 4.4 all-to-all-done.2
  219.3 2.3 reshape.1401
  222.6 2.9 reshape.1370
  226.9 2.2 reshape.1402
  229.2 19.9 %all_to_all.114 = bf16[32,2,2304]{2,1,0:T(2,128)(2,1)S(1)} all-to-all(bf16[32,2,2304]{2,1,0:T(2,128)(2,1)S(1)} %reshape.1402), channel_id=1, replica_groups=mesh['lat'=16,'lon'=32] {'lon'}, dimensions={0} | all-to-all | bytes 589824 | tf_op jit(solution)/shard_map/all_to_all | solution.py:166
  249.0 2.3 reshape.1403
  253.0 3.3 reshape.1383
  256.3 4.4 copy.246
  260.6 2.4 copy.193
  267.3 2.2 reshape.1404
  269.5 17.1 %all_to_all.115 = bf16[32,2,2304]{2,1,0:T(2,128)(2,1)S(1)} all-to-all(bf16[32,2,2304]{2,1,0:T(2,128)(2,1)S(1)} %reshape.1404), channel_id=1, replica_groups=mesh['lat'=16,'lon'=32] {'lon'}, dimensions={0} | all-to-all | bytes 589824 | tf_op jit(solution)/shard_map/all_to_all | solution.py:141
  286.6 2.3 reshape.1405
  289.5 2.9 reshape.1374
  293.7 2.3 copy.197
  298.2 14.0 %all_to_all.116 = bf16[16,2,4608]{2,1,0:T(2,128)(2,1)S(1)} all-to-all(bf16[16,2,4608]{2,1,0:T(2,128)(2,1)S(1)} %reshape.1406), channel_id=1, replica_groups=mesh['lat'=16,'lon'=32] {'lat'}, dimensions={0} | all-to-all | bytes 589824 | tf_op jit(solution)/shard_map/all_to_all | solution.py:152
  312.1 2.3 reshape.1407
  318.0 2.7 convolution_bitcast_fusion.1
  321.2 2.9 fusion.149
  328.8 2.9 reshape.1408
  331.7 6.7 %all-to-all-start.6 = ((bf16[16,2,4608]{2,1,0:T(2,128)(2,1)}), bf16[16,2,4608]{2,1,0:T(2,128)(2,1)S(1)}, u32[]{:S(2)}, u32[]{:S(2)}) async-start(bf16[16,2,4608]{2,1,0:T(2,128)(2,1)} %reshape.1408), calls=%async_computation.6 | async-start | bytes 589824 | tf_op jit(solution)/shard_map/all_to_all | solution.py:158
  338.6 3.8 convolution_bitcast_fusion.5
  343.9 6.2 all-to-all-done.6
  350.1 2.3 reshape.1409
  353.4 2.9 reshape.1380
  357.9 2.9 reshape.1410
  360.9 6.6 %all-to-all-start.7 = ((bf16[32,2,2304]{2,1,0:T(2,128)(2,1)}), bf16[32,2,2304]{2,1,0:T(2,128)(2,1)}, u32[]{:S(2)}, u32[]{:S(2)}) async-start(bf16[32,2,2304]{2,1,0:T(2,128)(2,1)} %reshape.1410), calls=%async_computation.7 | async-start | bytes 589824 | tf_op jit(solution)/shard_map/all_to_all | solution.py:166
  369.4 246.5 %all-reduce.2.cloned.1.call-done = f32[256,1024]{1,0:T(8,128)} async-done(((f32[256,1024]{1,0:T(8,128)}), f32[256,1024]{1,0:T(8,128)}) %all-reduce.2.cloned.1.call-update) | async-done | bytes 1048592 | tf_op jit(solution)/shard_map/psum | solution.py:214
  617.3 4.4 reshape.1411
  621.8 2.9 copy.206
  624.6 4.4 reshape.1384
  629.0 6.1 fusion.137
  635.1 2.3 copy.210
  (1554 shorter events, 130.6 us)
Async XLA Ops:
  7.2 256.6 %copy-start = (bf16[256,512]{1,0:T(8,128)(2,1)S(1)}, bf16[256,512]{1,0:T(8,128)(2,1)}, u32[]{:S(2)}) copy-start(bf16[256,512]{1,0:T(8,128)(2,1)} %param.9) | copy-start | bytes 786436
  11.9 23.2 %all-to-all-start = ((bf16[32,2,2304]{2,1,0:T(2,128)(2,1)}), bf16[32,2,2304]{2,1,0:T(2,128)(2,1)S(1)}, u32[]{:S(2)}, u32[]{:S(2)}) async-start(bf16[32,2,2304]{2,1,0:T(2,128)(2,1)} %reshape.1396), calls=%async_computation | async-start | bytes 589824 | tf_op jit(solution)/shard_map/all_to_all | solution.py:141
  29.5 11.4 %copy-start.11 = (bf16[768,384]{1,0:T(8,128)(2,1)}, bf16[768,384]{1,0:T(8,128)(2,1)S(1)}, u32[]{:S(2)}) copy-start(bf16[768,384]{1,0:T(8,128)(2,1)S(1)} %get-tuple-element.707) | copy-start | bytes 1769476
  29.5 11.4 %copy-start.13 = (bf16[768,384]{1,0:T(8,128)(2,1)}, bf16[768,384]{1,0:T(8,128)(2,1)S(1)}, u32[]{:S(2)}) copy-start(bf16[768,384]{1,0:T(8,128)(2,1)S(1)} %get-tuple-element.708) | copy-start | bytes 1769476
  45.8 134.1 %all-to-all-start.1 = ((bf16[16,2,4608]{2,1,0:T(2,128)(2,1)}), bf16[16,2,4608]{2,1,0:T(2,128)(2,1)S(1)}, u32[]{:S(2)}, u32[]{:S(2)}) async-start(bf16[16,2,4608]{2,1,0:T(2,128)(2,1)} %reshape.1398), calls=%async_computation.1 | async-start | bytes 589824 | tf_op jit(solution)/shard_map/all_to_all | solution.py:152
  185.9 3.1 copy-start.20
  189.0 3.1 copy-start.2
  199.9 19.4 %all-to-all-start.2 = ((bf16[16,2,4608]{2,1,0:T(2,128)(2,1)}), bf16[16,2,4608]{2,1,0:T(2,128)(2,1)S(1)}, u32[]{:S(2)}, u32[]{:S(2)}) async-start(bf16[16,2,4608]{2,1,0:T(2,128)(2,1)} %reshape.1400), calls=%async_computation.2 | async-start | bytes 589824 | tf_op jit(solution)/shard_map/all_to_all | solution.py:158
  222.6 2.9 copy-start.15
  222.6 2.9 copy-start.17
  260.6 2.4 copy-start.8
  263.0 1.2 copy-start.19
  263.0 1.1 copy-start.21
  263.1 0.7 copy-start.4
  264.1 1.0 copy-start.9
  265.2 1.2 copy-start.6
  289.5 2.9 copy-start.16
  289.5 2.9 copy-start.18
  321.2 3.1 copy-start.3
  328.8 9.8 %copy-start.10 = (f32[576,512]{1,0:T(8,128)S(1)}, f32[576,512]{1,0:T(8,128)}, u32[]{:S(2)}) copy-start(f32[576,512]{1,0:T(8,128)} %copy-done.9) | copy-start | bytes 3538948
  331.7 18.4 %all-to-all-start.6 = ((bf16[16,2,4608]{2,1,0:T(2,128)(2,1)}), bf16[16,2,4608]{2,1,0:T(2,128)(2,1)S(1)}, u32[]{:S(2)}, u32[]{:S(2)}) async-start(bf16[16,2,4608]{2,1,0:T(2,128)(2,1)} %reshape.1408), calls=%async_computation.6 | async-start | bytes 589824 | tf_op jit(solution)/shard_map/all_to_all | solution.py:158
  338.4 4.0 copy-start.5
  338.4 4.0 copy-start.7
  338.4 277.5 %all-reduce.2.cloned.1.call-start = ((), (), s32[]{:S(2)}) async-start(), calls=%async_computation.8 | async-start | bytes 2097152 | tf_op jit(solution)/shard_map/psum | solution.py:214
  353.4 2.9 copy-start.12
  353.4 2.9 copy-start.14
  360.9 256.5 %all-to-all-start.7 = ((bf16[32,2,2304]{2,1,0:T(2,128)(2,1)}), bf16[32,2,2304]{2,1,0:T(2,128)(2,1)}, u32[]{:S(2)}, u32[]{:S(2)}) async-start(bf16[32,2,2304]{2,1,0:T(2,128)(2,1)} %reshape.1410), calls=%async_computation.7 | async-start | bytes 589824 | tf_op jit(solution)/shard_map/all_to_all | solution.py:166
  629.0 8.4 %copy-start.1 = (bf16[256,512]{1,0:T(8,128)(2,1)S(1)}, bf16[256,512]{1,0:T(8,128)(2,1)}, u32[]{:S(2)}) copy-start(bf16[256,512]{1,0:T(8,128)(2,1)} %param.9) | copy-start | bytes 786436
Sparse Core Ops, SparseCore 0:
  344.3 271.5 all-reduce.1
where the time goes:
time: 649 us; the launch traced here: 645 us
  waiting for transfers between devices  263 us (41%)
  local copies, waits for them, and re-layouts  141 us (22%)
  other arithmetic  75.4 us (12%)
  blocking collectives  50.9 us (8%)
  starting transfers between devices  45.4 us (7%)
  loops' own time  28.6 us (4%)
  matrix products  25.5 us (4%)
  between operations  15 us (2%)
    psum x1, waiting for transfers between devices, body(): lax.psum(jnp.concatenate([up_part, down_part], axis=1) * grad_scale, ('la...  246 us
    unnamed x68, local copies, waits for them, and re-layouts  48.2 us
    while x360, other arithmetic  41.3 us
    another operation x1, loops' own time, legendre_table(): lax.scan(one_block, start_carry, jnp.arange(degrees // block_len, dtype=j...  28.6 us
    all_to_all x1, blocking collectives, to_grid(): lax.all_to_all(grid_vals.astype(jnp.bfloat16), 'lon', split_axis=2, conca...  19.9 us
    all_to_all x1, blocking collectives, to_spectral(): lax.all_to_all(grid_vals, 'lon', split_axis=3, concat_axis=2, tiled=True)  17.1 us
    dynamic_update_slice x24, local copies, waits for them, and re-layouts, legendre_table(): lax.scan(one_block, start_carry, jnp.arange(degrees // block_len, dtype=j...  16.8 us
    all_to_all x2, starting transfers between devices, to_grid(): lax.all_to_all(wave_rows, 'lat', split_axis=1, concat_axis=4, tiled=True)  15.8 us
  transfers between devices with their start and end apart: 6, of which 4 were waited for; matrix products, arithmetic and copies ran while one was open for 19% of the time, Pallas kernels for 0%

commit v1 on v0

v1 whole, which is shorter than its diff:
```python
import functools
import math

import jax
import jax.numpy as jnp
from jax import lax
from jax.experimental import pallas as pl
from jax.experimental.pallas import tpu as pltpu
from jax.sharding import Mesh, PartitionSpec as P

L = 384
ROW_GROUPS = 4
TILE = 8
F32 = jnp.float32
BF16 = jnp.bfloat16
VMEM_LIMIT = 48 * 1024 * 1024


def dot(a, b, dims=((1,), (0,))):
    return lax.dot_general(a, b, (dims, ((), ())), preferred_element_type=F32)


def call(kernel, outs, *args, scratch=(), cost=None):
    single = not isinstance(outs, (list, tuple))
    shapes = [outs] if single else list(outs)
    result = pl.pallas_call(
        kernel,
        out_shape=shapes,
        in_specs=[pl.BlockSpec(memory_space=pltpu.VMEM)] * len(args),
        out_specs=[pl.BlockSpec(memory_space=pltpu.VMEM)] * len(shapes),
        scratch_shapes=list(scratch),
        compiler_params=pltpu.CompilerParams(vmem_limit_bytes=VMEM_LIMIT),
        cost_estimate=cost,
    )(*args)
    return result[0] if single else result


def shaped(shape, dtype):
    return jax.ShapeDtypeStruct(shape, dtype)


def tiles_of(rows, width):
    return pltpu.VMEM((-(-width // 128), rows, 128), F32)


def pick(ref, width, start=0, size=None, stride=1, lead=()):
    tiles = -(-width // 128)
    at = slice(None) if size is None else pl.ds(start, size, stride=stride)
    value = jnp.concatenate([ref[(*lead, i, at, slice(None))] for i in range(tiles)], axis=1)
    return value[:, :width] if tiles * 128 > width else value


def place(ref, value, start=0, size=None, stride=1, lead=()):
    pad = -value.shape[1] % 128
    if pad:
        value = jnp.concatenate([value, jnp.zeros((value.shape[0], pad), value.dtype)], axis=1)
    at = slice(None) if size is None else pl.ds(start, size, stride=stride)
    for i in range(value.shape[1] // 128):
        ref[(*lead, i, at, slice(None))] = value[:, i * 128 : (i + 1) * 128]


def row_scale(lat_total, lon_total):
    colatitude = (jnp.arange(lat_total, dtype=F32) + 0.5) * (math.pi / lat_total)
    counter = jnp.arange(1, lat_total // 2 + 1, dtype=F32)
    series = jnp.sum(
        jnp.cos(2.0 * counter[None, :] * colatitude[:, None])
        / (4.0 * counter * counter - 1.0)[None, :],
        axis=1,
    )
    return 2.0 / lat_total * (1.0 - 2.0 * series) * (2.0 * math.pi / lon_total)


def fourier_tables(lon_total, groups, per_group):
    row = jnp.arange(groups * TILE, dtype=jnp.int32)
    order = row // TILE * per_group + row % TILE
    live = row % TILE < per_group
    lon_index = jnp.arange(lon_total, dtype=jnp.int32)
    angles = (order[:, None] * lon_index[None, :] % lon_total).astype(F32) * (
        2.0 * math.pi / lon_total
    )
    tables = jnp.stack([jnp.cos(angles), -jnp.sin(angles)])
    tables = jnp.where(live[None, :, None], tables, 0.0).astype(BF16)
    return tables, jnp.swapaxes(tables, 1, 2)


def legendre_kernel(orders, degrees, m_ref, cos_ref, diag_ref, p_ref, pt_ref, table):
    m = m_ref[...]
    squares = m * m
    cosine = cos_ref[...]
    diag = diag_ref[...]

    def block(index, carry):
        here, before, scale = carry
        level = jnp.exp(diag + scale)
        for inner in range(TILE):
            degree = index * TILE + inner
            lv = jnp.full(m.shape, degree, jnp.int32).astype(F32)
            spread = jnp.maximum(lv * lv - squares, 1.0)
            growth = jnp.sqrt(jnp.maximum(4.0 * lv * lv - 1.0, 1.0) / spread)
            low = lv - 1.0
            damping = jnp.sqrt(
                jnp.maximum(low * low - squares, 0.0) / jnp.maximum(4.0 * low * low - 1.0, 1.0)
            )
            ahead = growth * cosine * here - growth * damping * before
            live = lv > m
            here, before = jnp.where(live, ahead, here), jnp.where(live, here, before)
            values = jnp.where(lv >= m, level * here, 0.0)
            place(table, values, pl.multiple_of(degree * TILE, TILE), TILE)
        largest = jnp.maximum(jnp.abs(here), jnp.abs(before))
        return here / largest, before / largest, scale + jnp.log(largest)

    ones = jnp.ones(m.shape, F32)
    zeros = jnp.zeros(m.shape, F32)
    lax.fori_loop(0, degrees // TILE, block, (ones, zeros, zeros))
    for r in range(orders):
        rows = pick(table, m.shape[1], r, degrees, TILE)
        p_ref[r] = rows.astype(BF16)
        pt_ref[r] = rows.T.astype(BF16)


def legendre_tables(first_order, orders, lat_total, groups, degrees):
    per = lat_total // groups
    half = lat_total // 2
    position = jnp.arange(lat_total, dtype=jnp.int32)
    row = position % groups * per + position // groups
    north = jnp.minimum(row, lat_total - 1 - row)
    colatitude = (north.astype(F32) + 0.5) * (math.pi / lat_total)
    cosine = jnp.where(row < half, 1.0, -1.0) * jnp.cos(colatitude)
    log_sine = jnp.log(jnp.sin(colatitude))
    later = jnp.arange(1, degrees, dtype=F32)
    ratios = jnp.log((2.0 * later - 1.0) / (2.0 * later))
    order = (first_order + jnp.arange(TILE, dtype=jnp.int32)).astype(F32)
    partial_logs = jnp.sum(jnp.where(later[None, :] <= order[:, None], ratios[None, :], 0.0), axis=1)
    base_logs = 0.5 * (jnp.log((2.0 * order + 1.0) / (4.0 * math.pi)) + partial_logs)
    shape = (TILE, lat_total)
    diag = base_logs[:, None] + order[:, None] * log_sine[None, :]
    return call(
        functools.partial(legendre_kernel, orders, degrees),
        [
            shaped((orders, degrees, lat_total), BF16),
            shaped((orders, lat_total, degrees), BF16),
        ],
        jnp.broadcast_to(order[:, None], shape),
        jnp.broadcast_to(cosine[None, :], shape),
        diag,
        scratch=[tiles_of(degrees * TILE, lat_total)],
        cost=pl.CostEstimate(flops=40_000_000, bytes_accessed=4_000_000, transcendentals=1_000_000),
    )


def put_tile(row_groups, load, store):
    first = load(0)
    cols, channels = first.shape
    store_row_groups, rows, chunk_count = row_groups
    channel_groups = chunk_count // store_row_groups
    wide = channels // channel_groups
    per = rows // store_row_groups
    pad = -(per * wide) % 128
    for q in range(store_row_groups):
        lines = [load(q * per + k).astype(F32) for k in range(per)]
        for g in range(channel_groups):
            parts = [line[:, g * wide : (g + 1) * wide] for line in lines]
            if pad:
                parts.append(jnp.zeros((cols, pad), F32))
            store(g * store_row_groups + q, jnp.concatenate(parts, axis=1).astype(BF16))


def take_row(row_groups, load_chunk, k):
    count, rows, chunk_count, wide = row_groups
    per = rows // count
    q, inner = k // per, k % per
    parts = [
        load_chunk(g * count + q)[:, inner * wide : (inner + 1) * wide].astype(F32)
        for g in range(chunk_count // count)
    ]
    return jnp.concatenate(parts, axis=1)


def split_kernel(row_groups, x_ref, out_ref):
    def store(chunk, value):
        out_ref[chunk] = value

    put_tile((row_groups, x_ref.shape[0], out_ref.shape[0]), lambda k: x_ref[k], store)


def forward_kernel(width, doubled, scaled, skip, *refs):
    if scaled:
        x_ref, table_ref, scale_ref, out_ref, x_all, out_all = refs
    else:
        x_ref, table_ref, out_ref, x_all, out_all = refs
    chunks, rows, _ = x_ref.shape
    cols = rows - skip
    for b in range(chunks):
        x_all[pl.ds(b * cols, cols), :] = x_ref[b, skip:, :].astype(F32)
    x = x_all[...].astype(BF16)
    halves = [dot(table_ref[p], x)[:, :width] for p in range(2)]
    value = jnp.concatenate(halves, axis=1)
    if scaled:
        value = value * scale_ref[...]
    if doubled:
        order_row = lax.broadcasted_iota(jnp.int32, value.shape, 0)
        value = value * jnp.where(order_row == 0, 1.0, 2.0)
    place(out_all, value)
    if skip:
        total = x_ref[0, :skip, :].astype(F32)
        for b in range(1, chunks):
            total = total + x_ref[b, :skip, :].astype(F32)
        bands = skip // 2
        lanes = total.shape[1]
        groups = value.shape[0] // TILE
        for q in range(groups // bands):
            for half in range(2):
                place(
                    out_all,
                    total[half * bands : (half + 1) * bands, :lanes],
                    q * TILE + TILE - 2 + half,
                    bands,
                    groups // bands * TILE,
                )
    out_ref[...] = pick(out_all, value.shape[1]).astype(BF16)


def spectral_kernel(orders, per, wide, x_ref, p_ref, pt_ref, gain_ref, out_ref, x_all, out_all):
    groups = x_ref.shape[0] // TILE
    place(x_all, x_ref[...].astype(F32))
    gains = jnp.concatenate([gain_ref[...], gain_ref[...]], axis=1)
    half = per * wide
    for r in range(orders):
        rows = pick(x_all, 2 * half, r, groups, TILE)
        modes = jnp.concatenate(
            [
                jnp.concatenate(
                    [rows[:, p * half + k * wide : p * half + (k + 1) * wide] for p in range(2)],
                    axis=1,
                )
                for k in range(per)
            ],
            axis=0,
        ).astype(BF16)
        spectrum = dot(p_ref[r], modes)
        filtered = (spectrum * gains).astype(BF16)
        waves = dot(pt_ref[r], filtered)
        parts = []
        for p in range(2):
            for k in range(per):
                parts.append(waves[k * groups : (k + 1) * groups, p * wide : (p + 1) * wide])
        place(out_all, jnp.concatenate(parts, axis=1), r, groups, TILE)
    for r in range(orders, TILE):
        place(out_all, jnp.zeros((groups, 2 * half), F32), r, groups, TILE)
    out_ref[...] = pick(out_all, 2 * half).astype(BF16)


def inverse_kernel(width, doubled, scaled, *refs):
    if scaled:
        x_ref, table_ref, scale_ref, out_ref = refs
    else:
        x_ref, table_ref, out_ref = refs
    x = x_ref[...]
    if doubled:
        wide = x.astype(F32)
        order_row = lax.broadcasted_iota(jnp.int32, wide.shape, 0)
        x = (wide * jnp.where(order_row == 0, 1.0, 2.0)).astype(BF16)
    value = dot(table_ref[0], x[:, :width]) + dot(table_ref[1], x[:, width:])
    if scaled:
        value = value * scale_ref[...]
    pad = out_ref.shape[2] - width
    if pad:
        value = jnp.concatenate([value, jnp.zeros((value.shape[0], pad), F32)], axis=1)
    chunks, cols, _ = out_ref.shape
    for b in range(chunks):
        out_ref[b] = value[b * cols : (b + 1) * cols].astype(BF16)


def erf(values):
    return lax.erf(values)


def mlp_kernel(
    row_groups, wide, block, grad_scale,
    recv_ref, state_ref, cot_ref, up_ref, down_ref,
    send_ref, back_ref,
    mixed, cots, active_all, back_pre_all, grads,
):
    rows, cols, channels = state_ref.shape
    chunks = recv_ref.shape[0]
    plan = (row_groups, rows, chunks, wide)
    for k in range(rows):
        smooth = take_row(plan, lambda b: recv_ref[b], k)
        mixed[pl.ds(k * cols, cols), :] = state_ref[k].astype(F32) + smooth
        cots[pl.ds(k * cols, cols), :] = cot_ref[k].astype(F32)

    def step(index, _):
        at = pl.ds(pl.multiple_of(index * block, block), block)
        up = up_ref[...]
        pre = dot(mixed[at, :].astype(BF16), up)
        back_active = dot(cots[at, :].astype(BF16), down_ref[...])
        cdf = 0.5 * (1.0 + erf(pre * (1.0 / math.sqrt(2.0))))
        density = jnp.exp(-0.5 * pre * pre) * (1.0 / math.sqrt(2.0 * math.pi))
        active_all[at, :] = (pre * cdf).astype(BF16)
        back_pre = (back_active * (cdf + pre * density)).astype(BF16)
        back_pre_all[at, :] = back_pre
        back_ref[at, :] = cots[at, :] + dot(back_pre, up, ((1,), (1,)))
        return 0

    lax.fori_loop(0, rows * cols // block, step, 0)
    up_part = dot(mixed[...].astype(BF16), back_pre_all[...], ((0,), (0,)))
    down_part = dot(cots[...].astype(BF16), active_all[...], ((0,), (0,)))
    place(grads, up_part * grad_scale, lead=(0,))
    place(grads, down_part * grad_scale, lead=(1,))

    per_band = chunks // 2
    bands = channels // per_band
    lanes = up_ref.shape[1] // 2
    for b in range(chunks):
        line = pick(grads, 2 * lanes, b // 2, bands, per_band, lead=(b % 2,)).astype(BF16)
        for half in range(2):
            send_ref[b, half * bands : (half + 1) * bands, :lanes] = line[
                :, half * lanes : (half + 1) * lanes
            ]

    def store(chunk, value):
        send_ref[chunk, 2 * bands :, :] = value

    put_tile(
        (row_groups, rows, chunks), lambda k: back_ref[pl.ds(k * cols, cols), :], store
    )


def join_kernel(row_groups, wide, recv_ref, back_ref, out_ref):
    rows, cols, _ = out_ref.shape
    plan = (row_groups, rows, recv_ref.shape[0], wide)
    for k in range(rows):
        field = take_row(plan, lambda b: recv_ref[b], k)
        out_ref[k] = (back_ref[pl.ds(k * cols, cols), :] + field).astype(BF16)


def body(state_grid, spectral_filter, up_weight, down_weight, cotangent):
    _, rows, cols, channels = state_grid.shape
    bands = lax.axis_size("lat")
    row_groups = lax.axis_size("rows")
    channel_groups = lax.axis_size("chans")
    chunks = row_groups * channel_groups
    degrees = spectral_filter.shape[0]
    hidden = up_weight.shape[1]
    lat_total, lon_total = rows * bands, cols * chunks
    groups = bands * row_groups
    orders = degrees // groups
    per = rows // row_groups
    wide = channels // channel_groups
    width = per * wide
    lanes = -(-width // 128) * 128
    lon_axes = ("chans", "rows")
    lat_axes = ("lat", "rows")
    me = lax.axis_index("lat") * row_groups + lax.axis_index("rows")

    state = state_grid.reshape(rows, cols, channels)
    cot = cotangent.reshape(rows, cols, channels)

    sent = call(
        functools.partial(split_kernel, row_groups), shaped((chunks, cols, lanes), BF16), state
    )
    whole = lax.all_to_all(sent, lon_axes, 0, 0, tiled=True)

    gains = lax.all_gather(spectral_filter, "rows", axis=1, tiled=True)
    table, table_t = fourier_tables(lon_total, groups, orders)
    p_table, pt_table = legendre_tables(me * orders, orders, lat_total, groups, degrees)
    own = lax.dynamic_slice_in_dim(row_scale(lat_total, lon_total), me * per, per)
    scale_one = jnp.broadcast_to(own[:, None], (per, wide)).reshape(1, width)
    scale_two = jnp.concatenate([scale_one, scale_one], axis=1)

    def forward(x, doubled, scale, skip):
        extra = [] if scale is None else [scale]
        return call(
            functools.partial(forward_kernel, width, doubled, scale is not None, skip),
            shaped((groups * TILE, 2 * width), BF16),
            x, table, *extra,
            scratch=[
                pltpu.VMEM((lon_total, lanes), F32),
                tiles_of(groups * TILE, 2 * width),
            ],
        )

    def turn(x):
        moved = lax.all_to_all(
            x.reshape(groups, TILE, 2 * width), lat_axes, 0, 0, tiled=True
        )
        return moved.reshape(groups * TILE, 2 * width)

    def spectral(x):
        return call(
            functools.partial(spectral_kernel, orders, per, wide),
            shaped((groups * TILE, 2 * width), BF16),
            x, p_table, pt_table, gains,
            scratch=[
                tiles_of(groups * TILE, 2 * width),
                tiles_of(groups * TILE, 2 * width),
            ],
        )

    def inverse(x, doubled, scale):
        extra = [] if scale is None else [scale]
        return call(
            functools.partial(inverse_kernel, width, doubled, scale is not None),
            shaped((chunks, cols, lanes), BF16),
            x, table_t, *extra,
        )

    modes = turn(forward(whole, False, scale_two, 0))
    waves = turn(spectral(modes))
    smooth = lax.all_to_all(inverse(waves, True, None), lon_axes, 0, 0, tiled=True)

    points = rows * cols
    grad_rows = 2 * (channels // (chunks // 2))
    sent, back_mixed = call(
        functools.partial(
            mlp_kernel, row_groups, wide, points // 6, 1.0 / math.sqrt(lat_total * lon_total)
        ),
        [shaped((chunks, grad_rows + cols, lanes), BF16), shaped((points, channels), F32)],
        smooth, state, cot, up_weight, down_weight,
        scratch=[
            pltpu.VMEM((points, channels), F32),
            pltpu.VMEM((points, channels), F32),
            pltpu.VMEM((points, hidden), BF16),
            pltpu.VMEM((points, hidden), BF16),
            pltpu.VMEM((2, -(-hidden // 128), channels, 128), F32),
        ],
    )
    whole = lax.all_to_all(sent, lon_axes, 0, 0, tiled=True)
    back_modes = turn(forward(whole, True, None, grad_rows))

    parts = back_modes.reshape(bands, row_groups, TILE, 2 * width)
    parts = lax.dynamic_index_in_dim(parts, lax.axis_index("rows"), 1, keepdims=False)
    piece = jnp.sum(parts[:, TILE - 2 :, : hidden // 2].astype(F32), axis=0)
    pieces = lax.all_gather(piece, lon_axes, axis=0, tiled=False)
    pieces = pieces.reshape(chunks // 2, 2, hidden)

    back_waves = turn(spectral(back_modes))
    field = lax.all_to_all(inverse(back_waves, False, scale_one), lon_axes, 0, 0, tiled=True)
    grad_field = call(
        functools.partial(join_kernel, row_groups, wide),
        shaped((rows, cols, channels), BF16),
        field, back_mixed,
    )
    return grad_field.reshape(state_grid.shape), pieces[:, 0], pieces[:, 1]


def solution(mesh):
    bands, tiles = mesh.shape["lat"], mesh.shape["lon"]
    fine = Mesh(
        mesh.devices.reshape(bands, tiles // ROW_GROUPS, ROW_GROUPS), ("lat", "chans", "rows")
    )
    lon = ("chans", "rows")
    placed = (P(None, "lat", lon, None), P(None, lon), P(), P(), P(None, "lat", lon, None))
    return jax.shard_map(
        body,
        mesh=fine,
        in_specs=placed,
        out_specs=(P(None, "lat", lon, None), P("lat", None), P("lat", None)),
        check_vma=False,
    )
```

time: 649 us -> 240 us (0.37)
  waiting for transfers between devices: 263 us -> 20.2 us
  local copies, waits for them, and re-layouts: 141 us -> 8.79 us
  blocking collectives: 50.9 us -> 138 us
  other arithmetic: 75.4 us -> 11.5 us
  loops' own time: 28.6 us -> 0 us
  matrix products: 25.5 us -> 0 us
  Pallas kernels: 0 us -> 24.5 us
  between operations: 15 us -> 0.92 us
  starting transfers between devices: 45.4 us -> 35.1 us
    psum x1 -> x0, waiting for transfers between devices: 246 us -> none  [body(): lax.psum(jnp.concatenate([up_part, down_part], axis=1) * grad_scale, ('la...]
    all_gather x0 -> x2, blocking collectives: none -> 44.1 us  [the longest x1 38.8 us: body(): pieces = lax.all_gather(piece, lon_axes, axis=0, tiled=False)]
    all_to_all x3 -> x4, blocking collectives: 50.9 us -> 94.2 us  [the longest x2 44.5 us: turn(): lax.all_to_all(x.reshape(groups, TILE, 2 * width), lat_axes, 0, 0, tiled=...]
    unnamed x68 -> x34, local copies, waits for them, and re-layouts: 48.2 us -> 6.51 us
    while x360 -> x0, other arithmetic: 41.3 us -> none
    another operation x1 -> x0, loops' own time: 28.6 us -> none  [legendre_table(): lax.scan(one_block, start_carry, jnp.arange(degrees // block_len, dtype=j...]
    dot_general x17 -> x0, matrix products: 25.5 us -> none  [the longest x2 5.89 us: analysis(): jnp.einsum('lmk,bkcpm->bcplm', legendre, southern, preferred_element_type...]
    pallas_call x0 -> x10, Pallas kernels: none -> 24.5 us  [call(): pl.pallas_call(kernel, out_shape=shapes, in_specs=[pl.BlockSpec(memory_sp...]
  transfers between devices with their start and end apart: 6 -> 4, of which waited for: 4 -> 2; matrix products, arithmetic and copies ran while one was open for 19% -> 6% of each run, Pallas kernels for 0% -> 3%
where the time goes in v1:
time: 240 us; the launch traced here: 239 us
  blocking collectives  138 us (58%)
  starting transfers between devices  35.1 us (15%)
  Pallas kernels  24.5 us (10%)
  waiting for transfers between devices  20.2 us (8%)
  other arithmetic  11.5 us (5%)
  local copies, waits for them, and re-layouts  8.79 us (4%)
    all_to_all x2, blocking collectives, turn(): lax.all_to_all(x.reshape(groups, TILE, 2 * width), lat_axes, 0, 0, tiled=...  44.5 us
    all_gather x1, blocking collectives, body(): pieces = lax.all_gather(piece, lon_axes, axis=0, tiled=False)  38.8 us
    all_to_all x1, blocking collectives, body(): whole = lax.all_to_all(sent, lon_axes, 0, 0, tiled=True)  28.4 us
    pallas_call x10, Pallas kernels, call(): pl.pallas_call(kernel, out_shape=shapes, in_specs=[pl.BlockSpec(memory_sp...  24.5 us
    all_to_all x1, blocking collectives, body(): lax.all_to_all(inverse(waves, True, None), lon_axes, 0, 0, tiled=True)  21.3 us
    all_to_all x2, starting transfers between devices, turn(): lax.all_to_all(x.reshape(groups, TILE, 2 * width), lat_axes, 0, 0, tiled=...  20.4 us
    all_to_all x2, waiting for transfers between devices, turn(): lax.all_to_all(x.reshape(groups, TILE, 2 * width), lat_axes, 0, 0, tiled=...  20.2 us
    all_to_all x1, starting transfers between devices, body(): whole = lax.all_to_all(sent, lon_axes, 0, 0, tiled=True)  10.6 us
  transfers between devices with their start and end apart: 4, of which 2 were waited for; matrix products, arithmetic and copies ran while one was open for 6% of the time, Pallas kernels for 3%

profile of v1, /device:TPU:1, one launch (start us, length us, event | category | flops | bytes accessed | tf_op | source)
XLA Modules:
  0.0 239.2 jit_solution(5718312050835577865)
XLA Ops:
  0.6 0.0 copy-start.6
  0.6 1.0 copy-done.6
  1.6 1.1 shard_map.76
  2.7 10.6 %all-to-all-start = ((bf16[32,24,256]{2,1,0:T(8,128)(2,1)}), bf16[32,24,256]{2,1,0:T(8,128)(2,1)S(1)}, u32[]{:S(2)}, u32[]{:S(2)}) async-start(bf16[32,24,256]{2,1,0:T(8,128)(2,1)} %shard_map.76), calls=%async_computation | async-start | bytes 786432 | tf_op jit(solution)/shard_map/all_to_all | solution.py:362
  13.3 6.7 %fusion.5 = (bf16[1,512,768]{1,2,0:T(8,128)(2,1)S(1)}, bf16[1,512,768]{1,2,0:T(8,128)(2,1)S(1)}) fusion(s32[512]{0:T(512)S(1)} %fusion.14), kind=kLoop, calls=%fused_computation.9 | loop fusion | flops 4718592 | bytes 1574912 | tf_op jit(solution)/shard_map/cos | solution.py:81
  20.0 1.1 fusion.7
  21.1 0.1 dynamic_slice.7
  21.2 0.1 broadcast_in_dim.38
  21.3 0.1 reshape.240.refs_2_
  21.4 5.3 %all_gather.9 = f32[384,32]{0,1:T(8,128)S(1)} all-gather(f32[384,8]{0,1:T(8,128)S(1)} %copy-done.15), channel_id=1, replica_groups=mesh['lat'=16,'chans'=8,'rows'=4] {'rows'}, dimensions={1}, use_global_device_ids=true | all-gather | bytes 61440 | tf_op jit(solution)/shard_map/all_gather | solution.py:364
  26.7 0.1 copy.19.gain_ref
  26.8 1.5 fusion
  28.3 1.7 copy.18.refs_1_
  30.0 0.1 pad_maximum_fusion.refs_2_
  30.2 0.1 sine_log_fusion
  30.2 0.0 all-to-all-done.refs_0_
  30.2 1.4 shard_map.77
  31.6 14.0 %all-to-all-start.1 = ((bf16[64,8,384]{2,1,0:T(8,128)(2,1)}), bf16[64,8,384]{2,1,0:T(8,128)(2,1)}, u32[]{:S(2)}, u32[]{:S(2)}) async-start(bf16[64,8,384]{2,1,0:T(8,128)(2,1)} %bitcast.1), calls=%async_computation.1 | async-start | bytes 786432 | tf_op jit(solution)/shard_map/all_to_all | solution.py:384
  45.7 0.2 select_reduce_fusion
  45.9 0.1 multiply_add_fusion.diag_ref
  45.9 0.1 broadcast_in_dim.39.m_ref
  46.0 7.5 %shard_map.78 = (bf16[6,384,384]{2,1,0:T(8,128)(2,1)S(1)}, bf16[6,384,384]{2,1,0:T(8,128)(2,1)S(1)}) custom-call(f32[8,384]{1,0:T(8,128)S(1)} %broadcast_in_dim.39.m_ref, f32[8,384]{1,0:T(8,128)S(1)} %broadcast_in_dim.41.cos_ref, f32[8,384]{1,0:T(8,128)S(1)} %multiply_add_fusion.diag_ref), custom_call_target="tpu_custom_call" | custom-call | flops 40000000 | bytes 4000000 | tf_op jit(solution)/shard_map/pallas_call | solution.py:26
  53.5 1.2 copy-done.2
  54.7 6.4 %all-to-all-done.1 = bf16[64,8,384]{2,1,0:T(8,128)(2,1)} async-done(((bf16[64,8,384]{2,1,0:T(8,128)(2,1)}), bf16[64,8,384]{2,1,0:T(8,128)(2,1)}, u32[]{:S(2)}, u32[]{:S(2)}) %all-to-all-start.1) | async-done | bytes 393248 | tf_op jit(solution)/shard_map/all_to_all | solution.py:384
  61.2 1.5 copy-done.3
  62.6 3.2 %shard_map.79 = bf16[512,384]{1,0:T(8,128)(2,1)S(1)} custom-call(bf16[512,384]{1,0:T(8,128)(2,1)} %bitcast.2.x_ref, bf16[6,384,384]{2,1,0:T(8,128)(2,1)S(1)} %get-tuple-element.7.p_ref, bf16[6,384,384]{2,1,0:T(8,128)(2,1)S(1)} %copy-done.3, f32[384,32]{1,0:T(8,128)S(1)} %copy.19.gain_ref), custom_call_target="tpu_custom_call" | custom-call | tf_op jit(solution)/shard_map/pallas_call | solution.py:26
  65.8 0.7 copy-done.5
  66.6 6.4 %all-to-all-start.2 = ((bf16[64,8,384]{2,1,0:T(8,128)(2,1)}), bf16[64,8,384]{2,1,0:T(8,128)(2,1)}, u32[]{:S(2)}, u32[]{:S(2)}) async-start(bf16[64,8,384]{2,1,0:T(8,128)(2,1)} %bitcast.25), calls=%async_computation.2 | async-start | bytes 786432 | tf_op jit(solution)/shard_map/all_to_all | solution.py:384
  73.0 1.6 fusion.32.refs_1_
  74.6 13.7 %all-to-all-done.2 = bf16[64,8,384]{2,1,0:T(8,128)(2,1)} async-done(((bf16[64,8,384]{2,1,0:T(8,128)(2,1)}), bf16[64,8,384]{2,1,0:T(8,128)(2,1)}, u32[]{:S(2)}, u32[]{:S(2)}) %all-to-all-start.2) | async-done | bytes 393248 | tf_op jit(solution)/shard_map/all_to_all | solution.py:384
  88.3 1.7 shard_map.80
  90.1 21.3 %all_to_all.40.recv_ref = bf16[32,24,256]{2,1,0:T(8,128)(2,1)S(1)} all-to-all(bf16[32,24,256]{2,1,0:T(8,128)(2,1)S(1)} %shard_map.80), channel_id=1, replica_groups=mesh['lat'=16,'chans'=8,'rows'=4] {'chans','rows'}, dimensions={0} | all-to-all | bytes 786432 | tf_op jit(solution)/shard_map/all_to_all | solution.py:410
  111.4 4.0 %shard_map.81 = (bf16[32,56,256]{2,1,0:T(8,128)(2,1)S(1)}, f32[576,256]{1,0:T(8,128)S(1)}) custom-call(bf16[32,24,256]{2,1,0:T(8,128)(2,1)S(1)} %all_to_all.40.recv_ref, bf16[24,24,256]{2,1,0:T(8,128)(2,1)S(1)} %bitcast.30, bf16[24,24,256]{2,1,0:T(8,128)(2,1)S(1)} %bitcast.31, bf16[256,512]{1,0:T(8,128)(2,1)S(1)} %copy-done.11, bf16[256,512]{1,0:T(8,128)(2,1)S(1)} %copy-done.12), custom_call_target="tpu_custom_call" | custom-call | tf_op jit(solution)/shard_map/pallas_call | solution.py:26
  115.4 0.8 copy-done.8
  116.2 28.4 %all_to_all.41.refs_0_ = bf16[32,56,256]{2,1,0:T(8,128)(2,1)S(1)} all-to-all(bf16[32,56,256]{2,1,0:T(8,128)(2,1)S(1)} %get-tuple-element.9), channel_id=1, replica_groups=mesh['lat'=16,'chans'=8,'rows'=4] {'chans','rows'}, dimensions={0} | all-to-all | bytes 1835008 | tf_op jit(solution)/shard_map/all_to_all | solution.py:428
  144.6 0.7 shard_map.82
  145.4 23.2 %all_to_all.42 = bf16[64,8,384]{2,1,0:T(8,128)(2,1)S(1)} all-to-all(bf16[64,8,384]{2,1,0:T(8,128)(2,1)S(1)} %bitcast.28), channel_id=1, replica_groups=mesh['lat'=16,'chans'=8,'rows'=4] {'lat','rows'}, dimensions={0} | all-to-all | bytes 786432 | tf_op jit(solution)/shard_map/all_to_all | solution.py:384
  168.5 2.2 shard_map.83
  170.7 21.3 %all_to_all.43 = bf16[64,8,384]{2,1,0:T(8,128)(2,1)S(1)} all-to-all(bf16[64,8,384]{2,1,0:T(8,128)(2,1)S(1)} %bitcast.26), channel_id=1, replica_groups=mesh['lat'=16,'chans'=8,'rows'=4] {'lat','rows'}, dimensions={0} | all-to-all | bytes 786432 | tf_op jit(solution)/shard_map/all_to_all | solution.py:384
  192.0 1.4 shard_map.84
  193.4 4.2 %all-to-all-start.7 = ((bf16[32,24,256]{2,1,0:T(8,128)(2,1)}), bf16[32,24,256]{2,1,0:T(8,128)(2,1)S(1)}, u32[]{:S(2)}, u32[]{:S(2)}) async-start(bf16[32,24,256]{2,1,0:T(8,128)(2,1)} %shard_map.84), calls=%async_computation.7 | async-start | bytes 786432 | tf_op jit(solution)/shard_map/all_to_all | solution.py:438
  197.7 38.8 %all-gather.1 = f32[32,2,256]{2,1,0:T(2,128)S(1)} all-gather(f32[1,2,256]{2,1,0:T(2,128)S(1)} %bitcast.35), channel_id=2, replica_groups=mesh['lat'=16,'chans'=8,'rows'=4] {'chans','rows'}, dimensions={0}, use_global_device_ids=true | all-gather | bytes 67584 | tf_op jit(solution)/shard_map/all_gather | solution.py:434
  236.5 0.1 reshape.251
  236.6 0.1 fusion.31
  236.6 0.6 copy.26
  237.3 0.6 copy.27
  237.9 0.0 all-to-all-done.7.recv_ref
  237.9 1.3 shard_map.85
  (38 shorter events, 0.2 us)
Async XLA Ops:
  0.6 1.0 copy-start.6
  1.6 19.8 %copy-start.15 = (f32[384,8]{0,1:T(8,128)S(1)}, f32[384,8]{0,1:T(8,128)}, u32[]{:S(2)}) copy-start(f32[384,8]{0,1:T(8,128)} %param.6) | copy-start | bytes 36868
  2.7 27.6 %all-to-all-start = ((bf16[32,24,256]{2,1,0:T(8,128)(2,1)}), bf16[32,24,256]{2,1,0:T(8,128)(2,1)S(1)}, u32[]{:S(2)}, u32[]{:S(2)}) async-start(bf16[32,24,256]{2,1,0:T(8,128)(2,1)} %shard_map.76), calls=%async_computation | async-start | bytes 786432 | tf_op jit(solution)/shard_map/all_to_all | solution.py:362
  20.0 6.8 %copy-start.13 = (bf16[1,512,768]{1,2,0:T(8,128)(2,1)}, bf16[1,512,768]{1,2,0:T(8,128)(2,1)S(1)}, u32[]{:S(2)}) copy-start(bf16[1,512,768]{1,2,0:T(8,128)(2,1)S(1)} %get-tuple-element.13) | copy-start | bytes 2359300
  20.0 6.8 %copy-start.14 = (bf16[1,512,768]{1,2,0:T(8,128)(2,1)}, bf16[1,512,768]{1,2,0:T(8,128)(2,1)S(1)}, u32[]{:S(2)}) copy-start(bf16[1,512,768]{1,2,0:T(8,128)(2,1)S(1)} %get-tuple-element.14) | copy-start | bytes 2359300
  31.6 29.5 %all-to-all-start.1 = ((bf16[64,8,384]{2,1,0:T(8,128)(2,1)}), bf16[64,8,384]{2,1,0:T(8,128)(2,1)}, u32[]{:S(2)}, u32[]{:S(2)}) async-start(bf16[64,8,384]{2,1,0:T(8,128)(2,1)} %bitcast.1), calls=%async_computation.1 | async-start | bytes 786432 | tf_op jit(solution)/shard_map/all_to_all | solution.py:384
  53.5 1.2 copy-start.2
  54.7 11.1 %copy-start = (bf16[6,384,384]{2,1,0:T(8,128)(2,1)}, bf16[6,384,384]{2,1,0:T(8,128)(2,1)S(1)}, u32[]{:S(2)}) copy-start(bf16[6,384,384]{2,1,0:T(8,128)(2,1)S(1)} %get-tuple-element.7.p_ref) | copy-start | bytes 5308420
  61.2 1.5 copy-start.3
  65.8 0.8 copy-start.5
  66.6 21.7 %all-to-all-start.2 = ((bf16[64,8,384]{2,1,0:T(8,128)(2,1)}), bf16[64,8,384]{2,1,0:T(8,128)(2,1)}, u32[]{:S(2)}, u32[]{:S(2)}) async-start(bf16[64,8,384]{2,1,0:T(8,128)(2,1)} %bitcast.25), calls=%async_computation.2 | async-start | bytes 786432 | tf_op jit(solution)/shard_map/all_to_all | solution.py:384
  88.3 23.0 %copy-start.7 = (bf16[1,24,24,256]{3,2,1,0:T(8,128)(2,1)S(1)}, bf16[1,24,24,256]{3,2,1,0:T(8,128)(2,1)}, u32[]{:S(2)}) copy-start(bf16[1,24,24,256]{3,2,1,0:T(8,128)(2,1)} %param.5) | copy-start | bytes 884740
  88.3 23.0 %copy-start.10 = (bf16[1,24,24,256]{3,2,1,0:T(8,128)(2,1)S(1)}, bf16[1,24,24,256]{3,2,1,0:T(8,128)(2,1)}, u32[]{:S(2)}) copy-start(bf16[1,24,24,256]{3,2,1,0:T(8,128)(2,1)} %param.9) | copy-start | bytes 884740
  88.3 23.0 %copy-start.11 = (bf16[256,512]{1,0:T(8,128)(2,1)S(1)}, bf16[256,512]{1,0:T(8,128)(2,1)}, u32[]{:S(2)}) copy-start(bf16[256,512]{1,0:T(8,128)(2,1)} %up_ref.1) | copy-start | bytes 786436
  88.3 23.0 %copy-start.12 = (bf16[256,512]{1,0:T(8,128)(2,1)S(1)}, bf16[256,512]{1,0:T(8,128)(2,1)}, u32[]{:S(2)}) copy-start(bf16[256,512]{1,0:T(8,128)(2,1)} %down_ref.1) | copy-start | bytes 786436
  115.4 0.8 copy-start.8
  144.6 23.9 %copy-start.1 = (bf16[6,384,384]{2,1,0:T(8,128)(2,1)S(1)}, bf16[6,384,384]{2,1,0:T(8,128)(2,1)}, u32[]{:S(2)}) copy-start(bf16[6,384,384]{2,1,0:T(8,128)(2,1)} %copy-done) | copy-start | bytes 5308420
  144.6 23.9 %copy-start.4 = (bf16[6,384,384]{2,1,0:T(8,128)(2,1)S(1)}, bf16[6,384,384]{2,1,0:T(8,128)(2,1)}, u32[]{:S(2)}) copy-start(bf16[6,384,384]{2,1,0:T(8,128)(2,1)} %copy-done.2) | copy-start | bytes 5308420
  193.4 44.4 %copy-start.9 = (f32[576,256]{1,0:T(8,128)S(1)}, f32[576,256]{1,0:T(8,128)}, u32[]{:S(2)}) copy-start(f32[576,256]{1,0:T(8,128)} %copy-done.8) | copy-start | bytes 1769476
  193.4 44.4 %all-to-all-start.7 = ((bf16[32,24,256]{2,1,0:T(8,128)(2,1)}), bf16[32,24,256]{2,1,0:T(8,128)(2,1)S(1)}, u32[]{:S(2)}, u32[]{:S(2)}) async-start(bf16[32,24,256]{2,1,0:T(8,128)(2,1)} %shard_map.84), calls=%async_computation.7 | async-start | bytes 786432 | tf_op jit(solution)/shard_map/all_to_all | solution.py:438

commit v2 on v1

v2 whole, which is shorter than its diff:
```python
import functools
import math

import jax
import jax.numpy as jnp
from jax import lax
from jax.experimental import pallas as pl
from jax.experimental.pallas import tpu as pltpu
from jax.sharding import Mesh, PartitionSpec as P

L = 384
ROW_GROUPS = 4
TILE = 8
F32 = jnp.float32
BF16 = jnp.bfloat16
VMEM_LIMIT = 24 * 1024 * 1024


def dot(a, b, dims=((1,), (0,))):
    return lax.dot_general(a, b, (dims, ((), ())), preferred_element_type=F32)


def call(kernel, outs, *args, scratch=(), cost=None, in_hbm=()):
    single = not isinstance(outs, (list, tuple))
    shapes = [outs] if single else list(outs)
    result = pl.pallas_call(
        kernel,
        out_shape=shapes,
        in_specs=[pl.BlockSpec(memory_space=pltpu.VMEM)] * len(args),
        out_specs=[
            pl.BlockSpec(memory_space=pltpu.HBM if i in in_hbm else pltpu.VMEM)
            for i in range(len(shapes))
        ],
        scratch_shapes=list(scratch),
        compiler_params=pltpu.CompilerParams(vmem_limit_bytes=VMEM_LIMIT),
        cost_estimate=cost,
    )(*args)
    return result[0] if single else result


def shaped(shape, dtype):
    return jax.ShapeDtypeStruct(shape, dtype)


def tiles_of(rows, width):
    return pltpu.VMEM((-(-width // 128), rows, 128), F32)


def pick(ref, width, start=0, size=None, stride=1, lead=()):
    tiles = -(-width // 128)
    at = slice(None) if size is None else pl.ds(start, size, stride=stride)
    value = jnp.concatenate([ref[(*lead, i, at, slice(None))] for i in range(tiles)], axis=1)
    return value[:, :width] if tiles * 128 > width else value


def place(ref, value, start=0, size=None, stride=1, lead=()):
    pad = -value.shape[1] % 128
    if pad:
        value = jnp.concatenate([value, jnp.zeros((value.shape[0], pad), value.dtype)], axis=1)
    at = slice(None) if size is None else pl.ds(start, size, stride=stride)
    for i in range(value.shape[1] // 128):
        ref[(*lead, i, at, slice(None))] = value[:, i * 128 : (i + 1) * 128]


def row_scale(lat_total, lon_total):
    colatitude = (jnp.arange(lat_total, dtype=F32) + 0.5) * (math.pi / lat_total)
    counter = jnp.arange(1, lat_total // 2 + 1, dtype=F32)
    series = jnp.sum(
        jnp.cos(2.0 * counter[None, :] * colatitude[:, None])
        / (4.0 * counter * counter - 1.0)[None, :],
        axis=1,
    )
    return 2.0 / lat_total * (1.0 - 2.0 * series) * (2.0 * math.pi / lon_total)


def wave_pair(product, lon_total):
    quarter = lon_total // 4
    turns = jnp.floor(product * (1.0 / quarter) + 0.5)
    angle = (product - turns * quarter) * (2.0 * math.pi / lon_total)
    square = angle * angle
    sine = angle * (
        1.0 + square * (-1.0 / 6 + square * (1.0 / 120 + square * (-1.0 / 5040 + square / 362880)))
    )
    cosine = 1.0 + square * (
        -0.5 + square * (1.0 / 24 + square * (-1.0 / 720 + square / 40320))
    )
    quadrant = turns - 4.0 * jnp.floor(turns * 0.25)
    odd = (quadrant == 1.0) | (quadrant == 3.0)
    first = jnp.where(odd, sine, cosine)
    second = jnp.where(odd, cosine, sine)
    first = jnp.where((quadrant == 1.0) | (quadrant == 2.0), -first, first)
    second = jnp.where(quadrant >= 2.0, -second, second)
    return first, second


def fourier_kernel(per_group, table_out, turned_out, table_ref, turned_ref, sems):
    _, padded, lon_total = table_ref.shape

    def fill(ref, start, turn, live):
        here = wave_pair(start, lon_total)
        turn_cos, turn_sin = wave_pair(turn, lon_total)

        def ahead(pair):
            cosine, sine = pair
            return cosine * turn_cos - sine * turn_sin, sine * turn_cos + cosine * turn_sin

        def step(index, pair):
            later = ahead(pair)
            at = pl.ds(pl.multiple_of(index * 2 * TILE, 2 * TILE), 2 * TILE)
            for p, sign in enumerate((1.0, -1.0)):
                both = jnp.concatenate([pair[p], later[p]], axis=0)
                ref[p, at, :] = jnp.where(live, sign * both, 0.0).astype(BF16)
            return ahead(later)

        lax.fori_loop(0, ref.shape[1] // (2 * TILE), step, here)

    def whole(shape, axis):
        return lax.broadcasted_iota(jnp.int32, shape, axis)

    shape = (TILE, lon_total)
    lon_index = whole(shape, 1).astype(F32)
    rank = whole((2 * TILE, lon_total), 0) % TILE
    fill(table_ref, whole(shape, 0).astype(F32) * lon_index, per_group * lon_index, rank < per_group)
    first = pltpu.make_async_copy(table_ref, table_out, sems.at[0])
    first.start()

    shape = (TILE, padded)
    column = whole(shape, 1)
    order = (column // TILE * per_group + column % TILE).astype(F32)
    rank = whole((2 * TILE, padded), 1) % TILE
    fill(turned_ref, whole(shape, 0).astype(F32) * order, TILE * order, rank < per_group)
    second = pltpu.make_async_copy(turned_ref, turned_out, sems.at[1])
    second.start()
    first.wait()
    second.wait()


def fourier_tables(lon_total, groups, per_group):
    padded = groups * TILE
    shapes = [(2, padded, lon_total), (2, lon_total, padded)]
    return call(
        functools.partial(fourier_kernel, per_group),
        [shaped(shape, BF16) for shape in shapes],
        scratch=[pltpu.VMEM(shape, BF16) for shape in shapes] + [pltpu.SemaphoreType.DMA((2,))],
        cost=pl.CostEstimate(
            flops=30 * padded * lon_total, bytes_accessed=8 * padded * lon_total, transcendentals=0
        ),
        in_hbm=(0, 1),
    )


def legendre_kernel(
    orders, degrees, m_ref, cos_ref, diag_ref, p_out, pt_out, table, p_ref, pt_ref, sems
):
    m = m_ref[...]
    squares = m * m
    cosine = cos_ref[...]
    diag = diag_ref[...]

    def block(index, carry):
        here, before, scale = carry
        level = jnp.exp(diag + scale)
        for inner in range(TILE):
            degree = index * TILE + inner
            lv = jnp.full(m.shape, degree, jnp.int32).astype(F32)
            spread = jnp.maximum(lv * lv - squares, 1.0)
            growth = jnp.sqrt(jnp.maximum(4.0 * lv * lv - 1.0, 1.0) / spread)
            low = lv - 1.0
            damping = jnp.sqrt(
                jnp.maximum(low * low - squares, 0.0) / jnp.maximum(4.0 * low * low - 1.0, 1.0)
            )
            ahead = growth * cosine * here - growth * damping * before
            live = lv > m
            here, before = jnp.where(live, ahead, here), jnp.where(live, here, before)
            values = jnp.where(lv >= m, level * here, 0.0)
            place(table, values, pl.multiple_of(degree * TILE, TILE), TILE)
        largest = jnp.maximum(jnp.abs(here), jnp.abs(before))
        return here / largest, before / largest, scale + jnp.log(largest)

    ones = jnp.ones(m.shape, F32)
    zeros = jnp.zeros(m.shape, F32)
    lax.fori_loop(0, degrees // TILE, block, (ones, zeros, zeros))
    copies = []
    for r in range(orders):
        rows = pick(table, m.shape[1], r, degrees, TILE)
        p_ref[r] = rows.astype(BF16)
        pt_ref[r] = rows.T.astype(BF16)
        copies += [
            pltpu.make_async_copy(p_ref.at[r], p_out.at[r], sems.at[0, r]),
            pltpu.make_async_copy(pt_ref.at[r], pt_out.at[r], sems.at[1, r]),
        ]
        copies[-2].start()
        copies[-1].start()
    for copy in copies:
        copy.wait()


def legendre_tables(first_order, orders, lat_total, groups, degrees):
    per = lat_total // groups
    half = lat_total // 2
    position = jnp.arange(lat_total, dtype=jnp.int32)
    row = position % groups * per + position // groups
    north = jnp.minimum(row, lat_total - 1 - row)
    colatitude = (north.astype(F32) + 0.5) * (math.pi / lat_total)
    cosine = jnp.where(row < half, 1.0, -1.0) * jnp.cos(colatitude)
    log_sine = jnp.log(jnp.sin(colatitude))
    later = jnp.arange(1, degrees, dtype=F32)
    ratios = jnp.log((2.0 * later - 1.0) / (2.0 * later))
    order = (first_order + jnp.arange(TILE, dtype=jnp.int32)).astype(F32)
    partial_logs = jnp.sum(jnp.where(later[None, :] <= order[:, None], ratios[None, :], 0.0), axis=1)
    base_logs = 0.5 * (jnp.log((2.0 * order + 1.0) / (4.0 * math.pi)) + partial_logs)
    shape = (TILE, lat_total)
    diag = base_logs[:, None] + order[:, None] * log_sine[None, :]
    return call(
        functools.partial(legendre_kernel, orders, degrees),
        [
            shaped((orders, degrees, lat_total), BF16),
            shaped((orders, lat_total, degrees), BF16),
        ],
        jnp.broadcast_to(order[:, None], shape),
        jnp.broadcast_to(cosine[None, :], shape),
        diag,
        scratch=[
            tiles_of(degrees * TILE, lat_total),
            pltpu.VMEM((orders, degrees, lat_total), BF16),
            pltpu.VMEM((orders, lat_total, degrees), BF16),
            pltpu.SemaphoreType.DMA((2, orders)),
        ],
        in_hbm=(0, 1),
        cost=pl.CostEstimate(flops=40_000_000, bytes_accessed=4_000_000, transcendentals=1_000_000),
    )


def chunk_lanes(cols, width):
    return -(-(cols // TILE * width) // 128) * 128


def put_tile(plan, load, store):
    row_groups, rows, chunks, wide = plan
    per = rows // row_groups
    for q in range(row_groups):
        lines = [load(q * per + k).astype(F32) for k in range(per)]
        cols = lines[0].shape[0]
        used = cols // TILE * per * wide
        pad = chunk_lanes(cols, per * wide) - used
        for g in range(chunks // row_groups):
            parts = [
                line[j : j + TILE, g * wide : (g + 1) * wide]
                for j in range(0, cols, TILE)
                for line in lines
            ]
            if pad:
                parts.append(jnp.zeros((TILE, pad), F32))
            store(g * row_groups + q, jnp.concatenate(parts, axis=1).astype(BF16))


def take_row(plan, cols, load_chunk, k):
    row_groups, rows, chunks, wide = plan
    per = rows // row_groups
    q, inner = k // per, k % per
    held = [load_chunk(g * row_groups + q) for g in range(chunks // row_groups)]
    lines = []
    for j in range(cols // TILE):
        at = (j * per + inner) * wide
        lines.append(jnp.concatenate([one[:, at : at + wide] for one in held], axis=1))
    return jnp.concatenate(lines, axis=0)


def split_kernel(plan, x_ref, out_ref):
    def store(chunk, value):
        out_ref[chunk] = value

    put_tile(plan, lambda k: x_ref[k], store)


def forward_kernel(width, cols, doubled, scaled, skip, *refs):
    if scaled:
        x_ref, table_ref, scale_ref, filter_ref, out_ref, x_all, out_all = refs
    else:
        x_ref, table_ref, out_ref, x_all, out_all = refs
    chunks = x_ref.shape[0]
    used = chunk_lanes(cols, width)
    for b in range(chunks):
        chunk = x_ref[b, :, :used].astype(F32)
        for j in range(cols // TILE):
            x_all[pl.ds(b * cols + j * TILE, TILE), :] = chunk[:, j * width : (j + 1) * width]
    x = x_all[...].astype(BF16)
    value = jnp.concatenate([dot(table_ref[p], x) for p in range(2)], axis=1)
    if scaled:
        value = value * scale_ref[...]
    if doubled:
        order_row = lax.broadcasted_iota(jnp.int32, value.shape, 0)
        value = value * jnp.where(order_row == 0, 1.0, 2.0)
    place(out_all, value)
    if scaled:
        gains = filter_ref[...]
        parts = []
        for _ in range(3):
            parts.append(gains.astype(BF16).astype(F32))
            gains = gains - parts[-1]
        groups = value.shape[0] // TILE
        shape = (groups, value.shape[1])
        upper = jnp.concatenate(parts[:2], axis=1)
        lower = jnp.concatenate([parts[2], jnp.zeros_like(parts[2])], axis=1)
        place(out_all, jnp.broadcast_to(upper, shape), TILE - 2, groups, TILE)
        place(out_all, jnp.broadcast_to(lower, shape), TILE - 1, groups, TILE)
    if skip:
        lanes, bands = skip
        total = x_ref[0, :, used:].astype(F32)
        for b in range(1, chunks):
            total = total + x_ref[b, :, used:].astype(F32)
        groups = value.shape[0] // TILE
        per = bands // (total.shape[1] // (2 * lanes))
        for high in range(bands // per):
            for half in range(2):
                at = (2 * high + half) * lanes
                for q in range(groups // bands):
                    place(
                        out_all,
                        total[:per, at : at + lanes],
                        (high * per * (groups // bands) + q) * TILE + TILE - 2 + half,
                        per,
                        groups // bands * TILE,
                    )
    out_ref[...] = pick(out_all, value.shape[1]).astype(BF16)


def gather_gains(x_all, bands, width):
    groups = x_all.shape[1] // TILE
    row_groups = groups // bands
    parts = []
    for q in range(row_groups):
        upper = pick(x_all, 2 * width, q * TILE + TILE - 2, bands, row_groups * TILE)
        lower = pick(x_all, width, q * TILE + TILE - 1, bands, row_groups * TILE)
        parts.append(upper[:, :width] + upper[:, width:] + lower)
    return parts


def spectral_kernel(orders, per, wide, bands, first, *refs):
    if first:
        x_ref, p_ref, pt_ref, out_ref, gain_ref, x_all, out_all = refs
    else:
        x_ref, p_ref, pt_ref, gain_ref, out_ref, piece_ref, x_all, out_all = refs
    groups = x_ref.shape[0] // TILE
    place(x_all, x_ref[...].astype(F32))
    row_groups = groups // bands
    if first:
        parts = gather_gains(x_all, bands, per * wide)
        own = wide // row_groups
        rows = []
        for at in range(0, per * wide, own):
            line = [part[:, at : at + own] for part in parts]
            rows.append(jnp.concatenate(line + line, axis=1))
        gains = jnp.concatenate(rows, axis=0)
        gain_ref[...] = gains
    else:
        gains = gain_ref[...]
        mine = lax.axis_index("rows")
        lanes = piece_ref.shape[1]
        for half in range(2):
            sums = pick(x_all, lanes, mine * TILE + TILE - 2 + half, bands, row_groups * TILE)
            piece_ref[half : half + 1, :] = jnp.sum(sums, axis=0, keepdims=True)
    half = per * wide
    for r in range(orders):
        rows = pick(x_all, 2 * half, r, groups, TILE)
        modes = jnp.concatenate(
            [
                jnp.concatenate(
                    [rows[:, p * half + k * wide : p * half + (k + 1) * wide] for p in range(2)],
                    axis=1,
                )
                for k in range(per)
            ],
            axis=0,
        ).astype(BF16)
        spectrum = dot(p_ref[r], modes)
        filtered = (spectrum * gains).astype(BF16)
        waves = dot(pt_ref[r], filtered)
        parts = []
        for p in range(2):
            for k in range(per):
                parts.append(waves[k * groups : (k + 1) * groups, p * wide : (p + 1) * wide])
        place(out_all, jnp.concatenate(parts, axis=1), r, groups, TILE)
    for r in range(orders, TILE):
        place(out_all, jnp.zeros((groups, 2 * half), F32), r, groups, TILE)
    out_ref[...] = pick(out_all, 2 * half).astype(BF16)


def inverse_kernel(width, cols, doubled, scaled, *refs):
    if scaled:
        x_ref, table_ref, scale_ref, piece_ref, out_ref = refs
    else:
        x_ref, table_ref, out_ref = refs
    x = x_ref[...]
    if doubled:
        wide = x.astype(F32)
        order_row = lax.broadcasted_iota(jnp.int32, wide.shape, 0)
        x = (wide * jnp.where(order_row == 0, 1.0, 2.0)).astype(BF16)
    value = dot(table_ref[0], x[:, :width]) + dot(table_ref[1], x[:, width:])
    chunks, _, lanes = out_ref.shape
    pad = lanes - cols // TILE * width
    rest = jnp.zeros((TILE, pad), F32)
    if scaled:
        value = value * scale_ref[...]
        piece = piece_ref[...]
        share = 2 * piece.shape[1] // TILE
        rest = jnp.concatenate(
            [piece[i * share // piece.shape[1] : i * share // piece.shape[1] + 1,
                   i * share % piece.shape[1] : i * share % piece.shape[1] + share]
             for i in range(TILE)],
            axis=0,
        )
        if pad > share:
            rest = jnp.concatenate([rest, jnp.zeros((TILE, pad - share), F32)], axis=1)
    for b in range(chunks):
        lines = [
            value[b * cols + j * TILE : b * cols + (j + 1) * TILE] for j in range(cols // TILE)
        ]
        out_ref[b] = jnp.concatenate(lines + [rest], axis=1).astype(BF16)


def erf(values):
    return lax.erf(values)


def mlp_kernel(
    row_groups, wide, block, grad_scale,
    recv_ref, state_ref, cot_ref, up_ref, down_ref,
    send_ref, back_out,
    mixed, cots, active_all, back_pre_all, grads, back_ref, sem,
):
    rows, cols, channels = state_ref.shape
    chunks = recv_ref.shape[0]
    plan = (row_groups, rows, chunks, wide)
    for k in range(rows):
        smooth = take_row(plan, cols, lambda b: recv_ref[b].astype(F32), k)
        mixed[pl.ds(k * cols, cols), :] = state_ref[k].astype(F32) + smooth
        cots[pl.ds(k * cols, cols), :] = cot_ref[k].astype(F32)

    def step(index, _):
        at = pl.ds(pl.multiple_of(index * block, block), block)
        up = up_ref[...]
        pre = dot(mixed[at, :].astype(BF16), up)
        back_active = dot(cots[at, :].astype(BF16), down_ref[...])
        cdf = 0.5 * (1.0 + erf(pre * (1.0 / math.sqrt(2.0))))
        density = jnp.exp(-0.5 * pre * pre) * (1.0 / math.sqrt(2.0 * math.pi))
        active_all[at, :] = (pre * cdf).astype(BF16)
        back_pre = (back_active * (cdf + pre * density)).astype(BF16)
        back_pre_all[at, :] = back_pre
        back_ref[at, :] = cots[at, :] + dot(back_pre, up, ((1,), (1,)))
        return 0

    lax.fori_loop(0, rows * cols // block, step, 0)
    kept = pltpu.make_async_copy(back_ref, back_out, sem)
    kept.start()
    up_part = dot(mixed[...].astype(BF16), back_pre_all[...], ((0,), (0,)))
    down_part = dot(cots[...].astype(BF16), active_all[...], ((0,), (0,)))
    place(grads, up_part * grad_scale, lead=(0,))
    place(grads, down_part * grad_scale, lead=(1,))

    per_band = chunks // 2
    bands = channels // per_band
    lanes = up_ref.shape[1] // 2
    used = chunk_lanes(cols, rows // row_groups * wide)
    for b in range(chunks):
        line = pick(grads, 2 * lanes, b // 2, bands, per_band, lead=(b % 2,)).astype(BF16)
        for high in range(0, bands, TILE):
            send_ref[b, : min(TILE, bands), used + high // TILE * 2 * lanes : used + (high // TILE + 1) * 2 * lanes] = line[
                high : high + TILE
            ]

    def store(chunk, value):
        send_ref[chunk, :, :used] = value

    put_tile(plan, lambda k: back_ref[pl.ds(k * cols, cols), :], store)
    kept.wait()


def join_kernel(row_groups, wide, recv_ref, back_ref, out_ref, up_ref, down_ref, held):
    rows, cols, _ = out_ref.shape
    chunks = recv_ref.shape[0]
    plan = (row_groups, rows, chunks, wide)
    for k in range(rows):
        field = take_row(plan, cols, lambda b: recv_ref[b].astype(F32), k)
        out_ref[k] = (back_ref[pl.ds(k * cols, cols), :] + field).astype(BF16)
    used = cols // TILE * (rows // row_groups) * wide
    lines, hidden = up_ref.shape
    share = hidden // TILE
    for b in range(chunks):
        held[pl.ds(b * TILE, TILE), :] = jnp.concatenate(
            [recv_ref[b, :, used : used + share].astype(F32), jnp.zeros((TILE, 128 - share), F32)],
            axis=1,
        )
    for parity, ref in enumerate((up_ref, down_ref)):
        ref[...] = jnp.concatenate(
            [
                held[pl.ds(parity * TILE + i, lines, stride=2 * TILE), :][:, :share]
                for i in range(TILE)
            ],
            axis=1,
        )


def body(state_grid, spectral_filter, up_weight, down_weight, cotangent):
    _, rows, cols, channels = state_grid.shape
    bands = lax.axis_size("lat")
    row_groups = lax.axis_size("rows")
    channel_groups = lax.axis_size("chans")
    chunks = row_groups * channel_groups
    degrees = spectral_filter.shape[0]
    hidden = up_weight.shape[1]
    lat_total, lon_total = rows * bands, cols * chunks
    groups = bands * row_groups
    orders = degrees // groups
    per = rows // row_groups
    wide = channels // channel_groups
    width = per * wide
    lanes = chunk_lanes(cols, width)
    plan = (row_groups, rows, chunks, wide)
    lon_axes = ("chans", "rows")
    lat_axes = ("lat", "rows")
    me = lax.axis_index("lat") * row_groups + lax.axis_index("rows")

    state = state_grid.reshape(rows, cols, channels)
    cot = cotangent.reshape(rows, cols, channels)

    sent = call(
        functools.partial(split_kernel, plan), shaped((chunks, TILE, lanes), BF16), state
    )
    whole = lax.all_to_all(sent, lon_axes, 0, 0, tiled=True)

    shared = lax.dynamic_index_in_dim(
        spectral_filter.reshape(degrees // bands, bands, channels // chunks),
        lax.axis_index("lat"), 1, keepdims=False,
    ).reshape(1, width)
    table, table_t = fourier_tables(lon_total, groups, orders)
    p_table, pt_table = legendre_tables(me * orders, orders, lat_total, groups, degrees)
    own = lax.dynamic_slice_in_dim(row_scale(lat_total, lon_total), me * per, per)
    scale_one = jnp.broadcast_to(own[:, None], (per, wide)).reshape(1, width)
    scale_two = jnp.concatenate([scale_one, scale_one], axis=1)

    def forward(x, doubled, skip, *extra):
        return call(
            functools.partial(forward_kernel, width, cols, doubled, bool(extra), skip),
            shaped((groups * TILE, 2 * width), BF16),
            x, table, *extra,
            scratch=[
                pltpu.VMEM((lon_total, width), F32),
                tiles_of(groups * TILE, 2 * width),
            ],
        )

    def turn(x):
        moved = lax.all_to_all(
            x.reshape(groups, TILE, 2 * width), lat_axes, 0, 0, tiled=True
        )
        return moved.reshape(groups * TILE, 2 * width)

    def spectral(x, *gains):
        extra = shaped((2, hidden // 2), F32) if gains else shaped((degrees, 2 * wide), F32)
        return call(
            functools.partial(spectral_kernel, orders, per, wide, bands, not gains),
            [shaped((groups * TILE, 2 * width), BF16), extra],
            x, p_table, pt_table, *gains,
            scratch=[
                tiles_of(groups * TILE, 2 * width),
                tiles_of(groups * TILE, 2 * width),
            ],
        )

    def inverse(x, doubled, *extra):
        return call(
            functools.partial(inverse_kernel, width, cols, doubled, bool(extra)),
            shaped((chunks, TILE, lanes), BF16),
            x, table_t, *extra,
        )

    modes = turn(forward(whole, False, None, scale_two, shared))
    filtered, gains = spectral(modes)
    waves = turn(filtered)
    smooth = lax.all_to_all(inverse(waves, True), lon_axes, 0, 0, tiled=True)

    points = rows * cols
    grad_lanes = hidden * -(-bands // TILE)
    sent, back_mixed = call(
        functools.partial(
            mlp_kernel, row_groups, wide, points // 6, 1.0 / math.sqrt(lat_total * lon_total)
        ),
        [shaped((chunks, TILE, lanes + grad_lanes), BF16), shaped((points, channels), F32)],
        smooth, state, cot, up_weight, down_weight,
        in_hbm=(1,),
        scratch=[
            pltpu.VMEM((points, channels), F32),
            pltpu.VMEM((points, channels), F32),
            pltpu.VMEM((points, hidden), BF16),
            pltpu.VMEM((points, hidden), BF16),
            pltpu.VMEM((2, -(-hidden // 128), channels, 128), F32),
            pltpu.VMEM((points, channels), F32),
            pltpu.SemaphoreType.DMA,
        ],
    )
    whole = lax.all_to_all(sent, lon_axes, 0, 0, tiled=True)
    back_modes = turn(forward(whole, True, (hidden // 2, bands)))
    filtered, piece = spectral(back_modes, gains)
    back_waves = turn(filtered)
    field = lax.all_to_all(
        inverse(back_waves, False, scale_one, piece), lon_axes, 0, 0, tiled=True
    )
    grad_field, grad_up, grad_down = call(
        functools.partial(join_kernel, row_groups, wide),
        [
            shaped((rows, cols, channels), BF16),
            shaped((chunks // 2, hidden), F32),
            shaped((chunks // 2, hidden), F32),
        ],
        field, back_mixed,
        scratch=[pltpu.VMEM((chunks * TILE, 128), F32)],
    )
    return grad_field.reshape(state_grid.shape), grad_up, grad_down


def solution(mesh):
    bands, tiles = mesh.shape["lat"], mesh.shape["lon"]
    fine = Mesh(
        mesh.devices.reshape(bands, tiles // ROW_GROUPS, ROW_GROUPS), ("lat", "chans", "rows")
    )
    lon = ("chans", "rows")
    placed = (P(None, "lat", lon, None), P(None, lon), P(), P(), P(None, "lat", lon, None))
    return jax.shard_map(
        body,
        mesh=fine,
        in_specs=placed,
        out_specs=(P(None, "lat", lon, None), P("lat", None), P("lat", None)),
        check_vma=False,
    )
```

time: 240 us -> 197 us (0.82)
  blocking collectives: 138 us -> 126 us
  other arithmetic: 11.5 us -> 1.57 us
  starting transfers between devices: 35.1 us -> 25.2 us
  waiting for transfers between devices: 20.2 us -> 13.5 us
  local copies, waits for them, and re-layouts: 8.79 us -> 3.66 us
    all_gather x2 -> x0, blocking collectives: 44.1 us -> none  [the longest x1 38.8 us: body(): pieces = lax.all_gather(piece, lon_axes, axis=0, tiled=False)]
    all_to_all x2 -> x3, blocking collectives: 44.5 us -> 66.1 us  [turn(): lax.all_to_all(x.reshape(groups, TILE, 2 * width), lat_axes, 0, 0, tiled=...]
    all_to_all x2 -> x1, waiting for transfers between devices: 20.2 us -> 6.01 us  [turn(): lax.all_to_all(x.reshape(groups, TILE, 2 * width), lat_axes, 0, 0, tiled=...]
    all_to_all x1 -> x2, blocking collectives: 21.3 us -> 33.4 us  [the longest x1 16.8 us: body(): smooth = lax.all_to_all(inverse(waves, True), lon_axes, 0, 0, tiled=True)]
    all_to_all x1, waiting for transfers between devices: 0.01 us -> 7.44 us  [body(): whole = lax.all_to_all(sent, lon_axes, 0, 0, tiled=True)]
    cos x1 -> x0, other arithmetic: 6.74 us -> none  [fourier_tables(): tables = jnp.stack([jnp.cos(angles), -jnp.sin(angles)])]
    all_to_all x2 -> x1, starting transfers between devices: 20.4 us -> 14.6 us  [turn(): lax.all_to_all(x.reshape(groups, TILE, 2 * width), lat_axes, 0, 0, tiled=...]
    unnamed x34 -> x18, local copies, waits for them, and re-layouts: 6.51 us -> 2.15 us
  transfers between devices with their start and end apart: 4 -> 2, of which waited for: 2 -> 2; matrix products, arithmetic and copies ran while one was open for 6% -> 2% of each run, Pallas kernels for 3% -> 5%
where the time goes in v2:
time: 197 us
  blocking collectives  126 us (64%)
  Pallas kernels  25.7 us (13%)
  starting transfers between devices  25.2 us (13%)
  waiting for transfers between devices  13.5 us (7%)
  local copies, waits for them, and re-layouts  3.66 us (2%)
    all_to_all x3, blocking collectives, turn(): lax.all_to_all(x.reshape(groups, TILE, 2 * width), lat_axes, 0, 0, tiled=...  66.1 us
    all_to_all x1, blocking collectives, body(): whole = lax.all_to_all(sent, lon_axes, 0, 0, tiled=True)  27 us
    pallas_call x11, Pallas kernels, call(): pl.pallas_call(kernel, out_shape=shapes, in_specs=[pl.BlockSpec(memory_sp...  25.7 us
    all_to_all x1, blocking collectives, body(): smooth = lax.all_to_all(inverse(waves, True), lon_axes, 0, 0, tiled=True)  16.8 us
    all_to_all x1, blocking collectives, body(): lax.all_to_all(inverse(back_waves, False, scale_one, piece), lon_axes, 0,...  16.6 us
    all_to_all x1, starting transfers between devices, turn(): lax.all_to_all(x.reshape(groups, TILE, 2 * width), lat_axes, 0, 0, tiled=...  14.6 us
    all_to_all x1, starting transfers between devices, body(): whole = lax.all_to_all(sent, lon_axes, 0, 0, tiled=True)  10.6 us
    all_to_all x1, waiting for transfers between devices, body(): whole = lax.all_to_all(sent, lon_axes, 0, 0, tiled=True)  7.44 us
  transfers between devices with their start and end apart: 2, of which 2 were waited for; matrix products, arithmetic and copies ran while one was open for 2% of the time, Pallas kernels for 5%

profile of v2, /device:TPU:1, one launch (start us, length us, event | category | flops | bytes accessed | tf_op | source)
XLA Modules:
  0.0 196.8 jit_solution(1367414845202921926)
XLA Ops:
  0.6 0.0 copy-start.4
  0.6 1.0 copy-done.4
  1.6 1.0 shard_map.76
  2.6 10.6 %all-to-all-start = ((bf16[32,8,640]{2,1,0:T(8,128)(2,1)}), bf16[32,8,640]{2,1,0:T(8,128)(2,1)S(1)}, u32[]{:S(2)}, u32[]{:S(2)}) async-start(bf16[32,8,640]{2,1,0:T(8,128)(2,1)} %shard_map.76), calls=%async_computation | async-start | bytes 655360 | tf_op jit(solution)/shard_map/all_to_all | solution.py:530
  13.2 1.1 fusion
  14.3 0.1 dynamic_slice.7
  14.4 0.1 broadcast_in_dim.24
  14.5 0.1 reshape.127.refs_2_
  14.6 0.8 reshape.128
  15.4 0.1 constant_dynamic-slice_fusion
  15.5 0.2 copy.10
  15.7 0.1 reshape.129.refs_3_
  15.8 1.6 shard_map.77
  17.4 0.0 copy-start
  17.4 1.2 copy-done
  18.5 0.1 pad_maximum_fusion.refs_2_
  18.7 0.1 sine_log_fusion
  18.7 7.4 %all-to-all-done.refs_0_ = bf16[32,8,640]{2,1,0:T(8,128)(2,1)S(1)} async-done(((bf16[32,8,640]{2,1,0:T(8,128)(2,1)}), bf16[32,8,640]{2,1,0:T(8,128)(2,1)S(1)}, u32[]{:S(2)}, u32[]{:S(2)}) %all-to-all-start) | async-done | bytes 327712 | tf_op jit(solution)/shard_map/all_to_all | solution.py:530
  26.2 1.6 shard_map.78
  27.7 14.6 %all-to-all-start.1 = ((bf16[64,8,384]{2,1,0:T(8,128)(2,1)}), bf16[64,8,384]{2,1,0:T(8,128)(2,1)}, u32[]{:S(2)}, u32[]{:S(2)}) async-start(bf16[64,8,384]{2,1,0:T(8,128)(2,1)} %bitcast.1), calls=%async_computation.1 | async-start | bytes 786432 | tf_op jit(solution)/shard_map/all_to_all | solution.py:554
  42.4 0.2 select_reduce_fusion
  42.6 0.1 multiply_add_fusion.diag_ref
  42.7 0.0 copy-done.2
  42.7 0.1 broadcast_in_dim.25.m_ref
  42.7 8.9 %shard_map.79 = (bf16[6,384,384]{2,1,0:T(8,128)(2,1)S(1)}, bf16[6,384,384]{2,1,0:T(8,128)(2,1)S(1)}) custom-call(f32[8,384]{1,0:T(8,128)S(1)} %broadcast_in_dim.25.m_ref, f32[8,384]{1,0:T(8,128)S(1)} %broadcast_in_dim.27.cos_ref, f32[8,384]{1,0:T(8,128)S(1)} %multiply_add_fusion.diag_ref), custom_call_target="tpu_custom_call" | custom-call | flops 40000000 | bytes 4000000 | tf_op jit(solution)/shard_map/pallas_call | solution.py:26
  51.6 6.0 %all-to-all-done.1 = bf16[64,8,384]{2,1,0:T(8,128)(2,1)} async-done(((bf16[64,8,384]{2,1,0:T(8,128)(2,1)}), bf16[64,8,384]{2,1,0:T(8,128)(2,1)}, u32[]{:S(2)}, u32[]{:S(2)}) %all-to-all-start.1) | async-done | bytes 393248 | tf_op jit(solution)/shard_map/all_to_all | solution.py:554
  57.7 3.3 %shard_map.80 = (bf16[512,384]{1,0:T(8,128)(2,1)S(1)}, f32[384,64]{1,0:T(8,128)S(1)}) custom-call(bf16[512,384]{1,0:T(8,128)(2,1)} %bitcast.2.refs_0_, bf16[6,384,384]{2,1,0:T(8,128)(2,1)S(1)} %get-tuple-element.17.refs_1_, bf16[6,384,384]{2,1,0:T(8,128)(2,1)S(1)} %get-tuple-element.18.refs_2_), custom_call_target="tpu_custom_call" | custom-call | tf_op jit(solution)/shard_map/pallas_call | solution.py:26
  61.0 0.0 copy-start.5
  61.0 0.0 copy-start.6
  61.0 0.0 copy-start.7
  61.0 0.0 copy-start.8
  61.1 21.4 %all_to_all.40 = bf16[64,8,384]{2,1,0:T(8,128)(2,1)S(1)} all-to-all(bf16[64,8,384]{2,1,0:T(8,128)(2,1)S(1)} %bitcast.22), channel_id=1, replica_groups=mesh['lat'=16,'chans'=8,'rows'=4] {'lat','rows'}, dimensions={0} | all-to-all | bytes 786432 | tf_op jit(solution)/shard_map/all_to_all | solution.py:554
  82.5 0.0 copy-done.1
  82.5 0.7 shard_map.81
  83.2 16.8 %all_to_all.41.recv_ref = bf16[32,8,640]{2,1,0:T(8,128)(2,1)S(1)} all-to-all(bf16[32,8,640]{2,1,0:T(8,128)(2,1)S(1)} %shard_map.81), channel_id=1, replica_groups=mesh['lat'=16,'chans'=8,'rows'=4] {'chans','rows'}, dimensions={0} | all-to-all | bytes 655360 | tf_op jit(solution)/shard_map/all_to_all | solution.py:581
  99.9 0.0 copy-done.5
  99.9 0.0 copy-done.6
  99.9 0.0 copy-done.7
  100.0 0.0 copy-done.8
  100.0 3.8 %shard_map.82 = (bf16[32,8,1664]{2,1,0:T(8,128)(2,1)S(1)}, f32[576,256]{1,0:T(8,128)S(1)}) custom-call(bf16[32,8,640]{2,1,0:T(8,128)(2,1)S(1)} %all_to_all.41.recv_ref, bf16[24,24,256]{2,1,0:T(8,128)(2,1)S(1)} %bitcast.20, bf16[24,24,256]{2,1,0:T(8,128)(2,1)S(1)} %bitcast.23, bf16[256,512]{1,0:T(8,128)(2,1)S(1)} %copy-done.7, bf16[256,512]{1,0:T(8,128)(2,1)S(1)} %copy-done.8), custom_call_target="tpu_custom_call" | custom-call | tf_op jit(solution)/shard_map/pallas_call | solution.py:26
  103.8 27.0 %all_to_all.42.refs_0_ = bf16[32,8,1664]{2,1,0:T(8,128)(2,1)S(1)} all-to-all(bf16[32,8,1664]{2,1,0:T(8,128)(2,1)S(1)} %get-tuple-element.21), channel_id=1, replica_groups=mesh['lat'=16,'chans'=8,'rows'=4] {'chans','rows'}, dimensions={0} | all-to-all | bytes 1703936 | tf_op jit(solution)/shard_map/all_to_all | solution.py:602
  130.8 0.8 shard_map.83
  131.6 23.3 %all_to_all.43 = bf16[64,8,384]{2,1,0:T(8,128)(2,1)S(1)} all-to-all(bf16[64,8,384]{2,1,0:T(8,128)(2,1)S(1)} %bitcast.17), channel_id=1, replica_groups=mesh['lat'=16,'chans'=8,'rows'=4] {'lat','rows'}, dimensions={0} | all-to-all | bytes 786432 | tf_op jit(solution)/shard_map/all_to_all | solution.py:554
  154.9 2.2 %shard_map.84 = (bf16[512,384]{1,0:T(8,128)(2,1)S(1)}, f32[2,256]{1,0:T(2,128)S(1)}) custom-call(bf16[512,384]{1,0:T(8,128)(2,1)S(1)} %bitcast.18, bf16[6,384,384]{2,1,0:T(8,128)(2,1)S(1)} %get-tuple-element.17.refs_1_, bf16[6,384,384]{2,1,0:T(8,128)(2,1)S(1)} %get-tuple-element.18.refs_2_, f32[384,64]{1,0:T(8,128)S(1)} %get-tuple-element.22.refs_3_), custom_call_target="tpu_custom_call" | custom-call | tf_op jit(solution)/shard_map/pallas_call | solution.py:26
  157.2 21.3 %all_to_all.44 = bf16[64,8,384]{2,1,0:T(8,128)(2,1)S(1)} all-to-all(bf16[64,8,384]{2,1,0:T(8,128)(2,1)S(1)} %bitcast.21), channel_id=1, replica_groups=mesh['lat'=16,'chans'=8,'rows'=4] {'lat','rows'}, dimensions={0} | all-to-all | bytes 786432 | tf_op jit(solution)/shard_map/all_to_all | solution.py:554
  178.5 0.7 shard_map.85
  179.2 16.6 %all_to_all.45.recv_ref = bf16[32,8,640]{2,1,0:T(8,128)(2,1)S(1)} all-to-all(bf16[32,8,640]{2,1,0:T(8,128)(2,1)S(1)} %shard_map.85), channel_id=1, replica_groups=mesh['lat'=16,'chans'=8,'rows'=4] {'chans','rows'}, dimensions={0} | all-to-all | bytes 655360 | tf_op jit(solution)/shard_map/all_to_all | solution.py:606
  195.8 1.0 shard_map.86
  (12 shorter events, 0.1 us)
Async XLA Ops:
  0.6 1.0 copy-start.4
  2.6 23.5 %all-to-all-start = ((bf16[32,8,640]{2,1,0:T(8,128)(2,1)}), bf16[32,8,640]{2,1,0:T(8,128)(2,1)S(1)}, u32[]{:S(2)}, u32[]{:S(2)}) async-start(bf16[32,8,640]{2,1,0:T(8,128)(2,1)} %shard_map.76), calls=%async_computation | async-start | bytes 655360 | tf_op jit(solution)/shard_map/all_to_all | solution.py:530
  17.4 1.2 copy-start
  18.5 24.1 %copy-start.2 = (bf16[2,512,768]{2,1,0:T(8,128)(2,1)}, bf16[2,512,768]{2,1,0:T(8,128)(2,1)S(1)}, u32[]{:S(2)}) copy-start(bf16[2,512,768]{2,1,0:T(8,128)(2,1)S(1)} %get-tuple-element.16.refs_1_) | copy-start | bytes 4718596
  27.7 29.9 %all-to-all-start.1 = ((bf16[64,8,384]{2,1,0:T(8,128)(2,1)}), bf16[64,8,384]{2,1,0:T(8,128)(2,1)}, u32[]{:S(2)}, u32[]{:S(2)}) async-start(bf16[64,8,384]{2,1,0:T(8,128)(2,1)} %bitcast.1), calls=%async_computation.1 | async-start | bytes 786432 | tf_op jit(solution)/shard_map/all_to_all | solution.py:554
  57.7 24.8 %copy-start.1 = (bf16[2,768,512]{2,1,0:T(8,128)(2,1)S(1)}, bf16[2,768,512]{2,1,0:T(8,128)(2,1)}, u32[]{:S(2)}) copy-start(bf16[2,768,512]{2,1,0:T(8,128)(2,1)} %copy-done) | copy-start | bytes 4718596
  61.0 38.9 %copy-start.5 = (bf16[1,24,24,256]{3,2,1,0:T(8,128)(2,1)S(1)}, bf16[1,24,24,256]{3,2,1,0:T(8,128)(2,1)}, u32[]{:S(2)}) copy-start(bf16[1,24,24,256]{3,2,1,0:T(8,128)(2,1)} %param.5) | copy-start | bytes 884740
  61.0 38.9 %copy-start.6 = (bf16[1,24,24,256]{3,2,1,0:T(8,128)(2,1)S(1)}, bf16[1,24,24,256]{3,2,1,0:T(8,128)(2,1)}, u32[]{:S(2)}) copy-start(bf16[1,24,24,256]{3,2,1,0:T(8,128)(2,1)} %param.9) | copy-start | bytes 884740
  61.0 38.9 %copy-start.7 = (bf16[256,512]{1,0:T(8,128)(2,1)S(1)}, bf16[256,512]{1,0:T(8,128)(2,1)}, u32[]{:S(2)}) copy-start(bf16[256,512]{1,0:T(8,128)(2,1)} %up_ref.1) | copy-start | bytes 786436
  61.0 38.9 %copy-start.8 = (bf16[256,512]{1,0:T(8,128)(2,1)S(1)}, bf16[256,512]{1,0:T(8,128)(2,1)}, u32[]{:S(2)}) copy-start(bf16[256,512]{1,0:T(8,128)(2,1)} %down_ref.1) | copy-start | bytes 786436
  83.2 47.6 %copy-start.3 = (bf16[2,512,768]{2,1,0:T(8,128)(2,1)S(1)}, bf16[2,512,768]{2,1,0:T(8,128)(2,1)}, u32[]{:S(2)}) copy-start(bf16[2,512,768]{2,1,0:T(8,128)(2,1)} %copy-done.2) | copy-start | bytes 4718596

commit v3 on v1

v3 whole, which is shorter than its diff:
```python
import functools
import math

import jax
import jax.numpy as jnp
from jax import lax
from jax.experimental import pallas as pl
from jax.experimental.pallas import tpu as pltpu
from jax.sharding import PartitionSpec as P

TILE = 8
F32 = jnp.float32
BF16 = jnp.bfloat16
VMEM_LIMIT = 24 * 1024 * 1024


def dot(a, b, dims=((1,), (0,))):
    return lax.dot_general(a, b, (dims, ((), ())), preferred_element_type=F32)


def call(kernel, outs, *args, scratch=(), cost=None, in_hbm=()):
    single = not isinstance(outs, (list, tuple))
    shapes = [outs] if single else list(outs)
    result = pl.pallas_call(
        kernel,
        out_shape=shapes,
        in_specs=[pl.BlockSpec(memory_space=pltpu.VMEM)] * len(args),
        out_specs=[
            pl.BlockSpec(memory_space=pltpu.HBM if i in in_hbm else pltpu.VMEM)
            for i in range(len(shapes))
        ],
        scratch_shapes=list(scratch),
        compiler_params=pltpu.CompilerParams(vmem_limit_bytes=VMEM_LIMIT),
        cost_estimate=cost,
    )(*args)
    return result[0] if single else result


def shaped(shape, dtype):
    return jax.ShapeDtypeStruct(shape, dtype)


def tiles_of(rows, width):
    return pltpu.VMEM((-(-width // 128), rows, 128), F32)


def pick(ref, width, start=0, size=None, stride=1, lead=()):
    tiles = -(-width // 128)
    at = slice(None) if size is None else pl.ds(start, size, stride=stride)
    value = jnp.concatenate([ref[(*lead, i, at, slice(None))] for i in range(tiles)], axis=1)
    return value[:, :width] if tiles * 128 > width else value


def place(ref, value, start=0, size=None, stride=1, lead=()):
    pad = -value.shape[1] % 128
    if pad:
        value = jnp.concatenate([value, jnp.zeros((value.shape[0], pad), value.dtype)], axis=1)
    at = slice(None) if size is None else pl.ds(start, size, stride=stride)
    for i in range(value.shape[1] // 128):
        ref[(*lead, i, at, slice(None))] = value[:, i * 128 : (i + 1) * 128]


def row_scale(lat_total, lon_total):
    colatitude = (jnp.arange(lat_total, dtype=F32) + 0.5) * (math.pi / lat_total)
    counter = jnp.arange(1, lat_total // 2 + 1, dtype=F32)
    series = jnp.sum(
        jnp.cos(2.0 * counter[None, :] * colatitude[:, None])
        / (4.0 * counter * counter - 1.0)[None, :],
        axis=1,
    )
    return 2.0 / lat_total * (1.0 - 2.0 * series) * (2.0 * math.pi / lon_total)


def wave_pair(product, lon_total):
    quarter = lon_total // 4
    turns = jnp.floor(product * (1.0 / quarter) + 0.5)
    angle = (product - turns * quarter) * (2.0 * math.pi / lon_total)
    square = angle * angle
    sine = angle * (
        1.0 + square * (-1.0 / 6 + square * (1.0 / 120 + square * (-1.0 / 5040 + square / 362880)))
    )
    cosine = 1.0 + square * (
        -0.5 + square * (1.0 / 24 + square * (-1.0 / 720 + square / 40320))
    )
    quadrant = turns - 4.0 * jnp.floor(turns * 0.25)
    odd = (quadrant == 1.0) | (quadrant == 3.0)
    first = jnp.where(odd, sine, cosine)
    second = jnp.where(odd, cosine, sine)
    first = jnp.where((quadrant == 1.0) | (quadrant == 2.0), -first, first)
    second = jnp.where(quadrant >= 2.0, -second, second)
    return first, second


def rotate(pair, turn):
    cosine, sine = pair
    turn_cos, turn_sin = turn
    return cosine * turn_cos - sine * turn_sin, sine * turn_cos + cosine * turn_sin


def phased(product, part, lon_total):
    cosine, sine = wave_pair(product, lon_total)
    return jnp.where(part == 1, -sine, cosine), jnp.where(part == 1, cosine, sine)


def fourier_kernel(bands, orders, table_out, turned_out, table_ref, turned_ref, sems):
    lon_total, modes = table_ref.shape
    per = 2 * orders

    shape = (TILE, modes)
    column = lax.broadcasted_iota(jnp.int32, shape, 1)
    group = column // per
    rank = column - group * per
    order = (bands * (rank // 2) + group).astype(F32)
    row = lax.broadcasted_iota(jnp.int32, shape, 0).astype(F32)
    turn = wave_pair(TILE * order, lon_total)

    def step(index, pair):
        later = rotate(pair, turn)
        at = pl.ds(pl.multiple_of(index * 2 * TILE, 2 * TILE), 2 * TILE)
        table_ref[at, :] = jnp.concatenate([pair[0], later[0]], axis=0).astype(BF16)
        return rotate(later, turn)

    lax.fori_loop(0, lon_total // (2 * TILE), step, phased(row * order, rank % 2, lon_total))
    first = pltpu.make_async_copy(table_ref, table_out, sems.at[0])
    first.start()

    shape = (TILE, lon_total)
    lon_index = lax.broadcasted_iota(jnp.int32, shape, 1).astype(F32)
    row = lax.broadcasted_iota(jnp.int32, shape, 0)
    start = phased((bands * (row // 2)).astype(F32) * lon_index, row % 2, lon_total)
    inner = wave_pair(TILE // 2 * bands * lon_index, lon_total)
    outer = wave_pair(lon_index, lon_total)

    def group_step(t, pair):
        now = pair
        for i in range(per // (2 * TILE)):
            later = rotate(now, inner)
            at = pl.ds(pl.multiple_of(t * per + i * 2 * TILE, 2 * TILE), 2 * TILE)
            turned_ref[at, :] = jnp.concatenate([now[0], later[0]], axis=0).astype(BF16)
            now = rotate(later, inner)
        return rotate(pair, outer)

    lax.fori_loop(0, modes // per, group_step, start)
    second = pltpu.make_async_copy(turned_ref, turned_out, sems.at[1])
    second.start()
    first.wait()
    second.wait()


def fourier_tables(lon_total, bands, orders):
    modes = 2 * bands * orders
    shapes = [(lon_total, modes), (modes, lon_total)]
    return call(
        functools.partial(fourier_kernel, bands, orders),
        [shaped(shape, BF16) for shape in shapes],
        scratch=[pltpu.VMEM(shape, BF16) for shape in shapes] + [pltpu.SemaphoreType.DMA((2,))],
        cost=pl.CostEstimate(
            flops=30 * modes * lon_total, bytes_accessed=8 * modes * lon_total, transcendentals=0
        ),
        in_hbm=(0, 1),
    )


def legendre_kernel(bands, degrees, cos_ref, diag_ref, out_ref, *tables):
    tiles = diag_ref.shape[0] // TILE
    band = lax.axis_index("lat")
    cosine = cos_ref[...]
    width = cosine.shape[1]
    shape = (TILE, 128)
    rank = lax.broadcasted_iota(jnp.int32, shape, 0)
    orders = [(bands * (TILE * g + rank) + band).astype(F32) for g in range(tiles)]
    diags = [diag_ref[g * TILE : (g + 1) * TILE, :] for g in range(tiles)]

    def spread(value):
        return jnp.concatenate([value] * (-(-width // 128)), axis=1)[:, :width]

    def block(active, index, carry):
        carry = list(carry)
        for g in range(active):
            here, before, scale, inverse = carry[g]
            order = orders[g]
            square = order * order
            wide_order = spread(order)
            level = jnp.exp(diags[g] + scale)
            for inner in range(TILE):
                degree = index * TILE + inner
                lv = jnp.full(shape, degree, jnp.int32).astype(F32)
                now = jnp.sqrt(jnp.maximum(lv * lv - square, 0.0) / jnp.maximum(4.0 * lv * lv - 1.0, 1.0))
                live = lv > order
                growth = 1.0 / jnp.where(live, now, 1.0)
                ahead = spread(growth) * cosine * here - spread(growth * inverse) * before
                wide_live = spread(lv) > wide_order
                here, before = jnp.where(wide_live, ahead, here), jnp.where(wide_live, here, before)
                values = jnp.where(spread(lv) >= wide_order, level * here, 0.0)
                at = pl.multiple_of((degree - bands * TILE * g) * TILE, TILE)
                place(tables[g], values, at, TILE)
                inverse = now
            largest = jnp.maximum(jnp.abs(here), jnp.abs(before))
            carry[g] = (here / largest, before / largest, scale + jnp.log(largest), inverse)
        return tuple(carry)

    ones = jnp.ones((TILE, width), F32)
    zeros = jnp.zeros((TILE, width), F32)
    carry = tuple((ones, zeros, zeros, jnp.zeros(shape, F32)) for _ in range(tiles))
    for g in range(tiles):
        last = bands * (g + 1) if g + 1 < tiles else degrees // TILE
        carry = lax.fori_loop(bands * g, last, functools.partial(block, g + 1), carry)
    at = 0
    for g in range(tiles):
        depth = degrees - bands * TILE * g
        for r in range(TILE):
            rows = pick(tables[g], width, r, depth, TILE)
            out_ref[:, at : at + depth] = rows.T.astype(BF16)
            at += depth


def legendre_tables(bands, orders, lat_total, degrees):
    half = lat_total // 2
    colatitude = (jnp.arange(half, dtype=F32) + 0.5) * (math.pi / lat_total)
    cosine = jnp.cos(colatitude)
    log_sine = jnp.log(jnp.sin(colatitude))
    later = jnp.arange(1, degrees, dtype=F32)
    ratios = jnp.log((2.0 * later - 1.0) / (2.0 * later))
    order = (bands * jnp.arange(orders, dtype=jnp.int32) + lax.axis_index("lat")).astype(F32)
    partial_logs = jnp.sum(jnp.where(later[None, :] <= order[:, None], ratios[None, :], 0.0), axis=1)
    base_logs = 0.5 * (jnp.log((2.0 * order + 1.0) / (4.0 * math.pi)) + partial_logs)
    diag = base_logs[:, None] + order[:, None] * log_sine[None, :]
    depths = [degrees - bands * TILE * g for g in range(orders // TILE)]
    return call(
        functools.partial(legendre_kernel, bands, degrees),
        shaped((half, TILE * sum(depths)), BF16),
        jnp.broadcast_to(cosine[None, :], (TILE, half)),
        diag,
        scratch=[tiles_of(depth * TILE, half) for depth in depths],
        cost=pl.CostEstimate(flops=40_000_000, bytes_accessed=6_000_000, transcendentals=1_000_000),
    )


def slot_row(slot, rows):
    south = lax.axis_index("lat") * 2 >= lax.axis_size("lat")
    return jnp.where(south, rows - 1 - slot, slot)


def padded(count):
    return -(-count // 128) * 128


def send_tile(ref, grid, used):
    turned = grid.T
    pad = used - turned.shape[1]
    if pad:
        turned = jnp.concatenate([turned, jnp.zeros((turned.shape[0], pad), F32)], axis=1)
    for b in range(ref.shape[0]):
        ref[b, :, :used] = turned[b * TILE : (b + 1) * TILE].astype(BF16)


def take_tile(ref, points):
    chunks = [ref[b].astype(F32) for b in range(ref.shape[0])]
    return jnp.concatenate(chunks, axis=0).T[:points]


def split_kernel(x_ref, out_ref, grid):
    rows, cols, _ = x_ref.shape
    for s in range(rows):
        grid[pl.ds(s * cols, cols), :] = x_ref[slot_row(s, rows)].astype(F32)
    send_tile(out_ref, grid[...], out_ref.shape[2])


def forward_kernel(rows, cols, doubled, scaled, skip, *refs):
    if scaled:
        x_ref, table_ref, scale_ref, out_ref, x_all, out_all = refs
    else:
        x_ref, table_ref, out_ref, x_all, out_all = refs
    chunks = x_ref.shape[0]
    used = padded(rows * cols)
    held = [x_ref[b, :, :used].astype(F32) for b in range(chunks)]
    for s in range(rows):
        x_all[pl.ds(s * TILE, TILE), :] = jnp.concatenate(
            [one[:, s * cols : (s + 1) * cols] for one in held], axis=1
        )
    value = dot(x_all[...].astype(BF16), table_ref[...])
    if scaled:
        value = value * scale_ref[...]
    if doubled:
        column = lax.broadcasted_iota(jnp.int32, value.shape, 1)
        value = value * jnp.where(column < 2, 1.0, 2.0)
    modes = value.shape[1]
    place(out_all, value)
    lines = [pick(out_all, modes, c, rows, TILE) for c in range(TILE)]
    bands = out_ref.shape[0]
    per = modes // bands
    share = 2 * TILE
    for t in range(bands):
        for g in range(per // share):
            at = t * per + g * share
            tile = jnp.concatenate([line[:, at : at + share] for line in lines], axis=1).astype(BF16)
            for i in range(rows // TILE):
                lane = i * TILE * per + g * 128
                out_ref[t, :, lane : lane + 128] = tile[i * TILE : (i + 1) * TILE]
    if skip:
        total = x_ref[0, :, used:].astype(F32)
        for b in range(1, chunks):
            total = total + x_ref[b, :, used:].astype(F32)
        lane = TILE * per * (rows // TILE)
        for t in range(bands):
            at = t // TILE * skip
            parts = [
                total[t % TILE : t % TILE + 1, at + i * 128 : at + (i + 1) * 128]
                for i in range(skip // 128)
            ]
            parts.append(jnp.zeros((TILE - skip // 128, 128), F32))
            out_ref[t, :, lane : lane + 128] = jnp.concatenate(parts, axis=0).astype(BF16)


def spectral_kernel(rows, tiles, has_piece, x_ref, filter_ref, table_ref, out_ref, *refs):
    x_all, out_all = refs[-2:]
    bands = x_ref.shape[0]
    blocks = rows // TILE
    stride = tiles * 128
    degrees = filter_ref.shape[1]
    half = table_ref.shape[0]
    if has_piece:
        total = x_ref[0, :, blocks * stride :].astype(F32)
        for t in range(1, bands):
            total = total + x_ref[t, :, blocks * stride :].astype(F32)
        refs[0][...] = total
    shape = (2 * TILE, degrees)
    odd = (lax.broadcasted_iota(jnp.int32, shape, 1) + lax.axis_index("lat")) % 2
    signs = (1 - 2 * odd).astype(F32)
    gains = jnp.concatenate([filter_ref[...], filter_ref[...]], axis=0)
    north = list(range(bands // 2))
    south = [bands - 1 - t for t in north]
    at = 0
    for g in range(tiles):
        depth = degrees - bands * TILE * g
        for h, order in enumerate((north, south)):
            parts = [
                x_ref[t, :, i * stride + g * 128 : i * stride + (g + 1) * 128].astype(F32)
                for t in order
                for i in range(blocks)
            ]
            place(x_all, jnp.concatenate(parts, axis=0).T, h * 128, 128)
        sign, gain = signs[:, degrees - depth :], gains[:, degrees - depth :]
        for r in range(TILE):
            starts = [h * 128 + 2 * r + p for h in range(2) for p in range(2)]
            modes = [pick(x_all, half, start, TILE, 2 * TILE) for start in starts]
            table = table_ref[:, at : at + depth]
            at += depth
            both = dot(jnp.concatenate(modes, axis=0).astype(BF16), table)
            spectrum = both[: 2 * TILE] + sign * both[2 * TILE :]
            filtered = spectrum * gain
            filtered = jnp.concatenate([filtered, sign * filtered], axis=0).astype(BF16)
            waves = dot(filtered, table, ((1,), (1,)))
            for i, start in enumerate(starts):
                place(out_all, waves[i * TILE : (i + 1) * TILE], start, TILE, 2 * TILE)
        for h, order in enumerate((north, south)):
            waves = pick(out_all, half, h * 128, 128).T.astype(BF16)
            for n, t in enumerate(order):
                for i in range(blocks):
                    lane = i * stride + g * 128
                    row = (n * blocks + i) * TILE
                    out_ref[t, :, lane : lane + 128] = waves[row : row + TILE]


def inverse_kernel(rows, cols, doubled, scaled, *refs):
    if scaled:
        x_ref, table_ref, scale_ref, piece_ref, out_ref, x_all = refs
    else:
        x_ref, table_ref, out_ref, x_all = refs
    bands = x_ref.shape[0]
    blocks = rows // TILE
    stride = x_ref.shape[2] // blocks
    share = 2 * TILE
    held = [
        [
            jnp.concatenate(
                [
                    x_ref[t, :, i * stride + g * 128 : i * stride + (g + 1) * 128].astype(F32)
                    for i in range(blocks)
                ],
                axis=0,
            )
            for g in range(stride // 128)
        ]
        for t in range(bands)
    ]
    for c in range(TILE):
        line = jnp.concatenate(
            [tile[:, c * share : (c + 1) * share] for one in held for tile in one], axis=1
        )
        place(x_all, line, c, rows, TILE)
    modes = table_ref.shape[0]
    x = pick(x_all, modes)
    if doubled:
        column = lax.broadcasted_iota(jnp.int32, x.shape, 1)
        x = x * jnp.where(column < 2, 1.0, 2.0)
    value = dot(x.astype(BF16), table_ref[...])
    chunks, _, lanes = out_ref.shape
    pad = lanes - rows * cols
    rest = jnp.zeros((TILE, pad), F32)
    if scaled:
        value = value * scale_ref[...]
        piece = piece_ref[...]
        rest = jnp.concatenate(
            [piece[i // 2 : i // 2 + 1, i % 2 * 64 : i % 2 * 64 + 64] for i in range(TILE)], axis=0
        )
    lines = [value[s * TILE : (s + 1) * TILE] for s in range(rows)]
    for b in range(chunks):
        parts = [line[:, b * cols : (b + 1) * cols] for line in lines]
        out_ref[b] = jnp.concatenate(parts + [rest], axis=1).astype(BF16)


def erf(values):
    return lax.erf(values)


def mlp_kernel(
    block, grad_scale,
    recv_ref, state_ref, cot_ref, up_ref, down_ref,
    send_ref, back_out,
    mixed, cots, active_all, back_pre_all, grads, back_ref, sem,
):
    rows, cols, channels = state_ref.shape
    chunks = recv_ref.shape[0]
    points = rows * cols
    mixed[...] = take_tile(recv_ref, points)
    for s in range(rows):
        at = pl.ds(s * cols, cols)
        row = slot_row(s, rows)
        mixed[at, :] = mixed[at, :] + state_ref[row].astype(F32)
        cots[at, :] = cot_ref[row].astype(F32)

    def step(index, _):
        at = pl.ds(pl.multiple_of(index * block, block), block)
        up = up_ref[...]
        pre = dot(mixed[at, :].astype(BF16), up)
        back_active = dot(cots[at, :].astype(BF16), down_ref[...])
        cdf = 0.5 * (1.0 + erf(pre * (1.0 / math.sqrt(2.0))))
        density = jnp.exp(-0.5 * pre * pre) * (1.0 / math.sqrt(2.0 * math.pi))
        active_all[at, :] = (pre * cdf).astype(BF16)
        back_pre = (back_active * (cdf + pre * density)).astype(BF16)
        back_pre_all[at, :] = back_pre
        back_ref[at, :] = cots[at, :] + dot(back_pre, up, ((1,), (1,)))
        return 0

    lax.fori_loop(0, points // block, step, 0)
    kept = pltpu.make_async_copy(back_ref, back_out, sem)
    kept.start()
    up_part = dot(mixed[...].astype(BF16), back_pre_all[...], ((0,), (0,)))
    down_part = dot(cots[...].astype(BF16), active_all[...], ((0,), (0,)))
    place(grads, up_part * grad_scale, lead=(0,))
    place(grads, down_part * grad_scale, lead=(1,))

    used = padded(points)
    per_band = chunks // 2
    bands = channels // per_band
    hidden = up_ref.shape[1]
    for b in range(chunks):
        line = pick(grads, hidden, b // 2, bands, per_band, lead=(b % 2,)).astype(BF16)
        for i in range(bands // TILE):
            send_ref[b, :, used + i * hidden : used + (i + 1) * hidden] = line[
                i * TILE : (i + 1) * TILE
            ]
    send_tile(send_ref, back_ref[...], used)
    kept.wait()


def join_kernel(recv_ref, back_ref, out_ref, up_ref, down_ref, held):
    rows, cols, _ = out_ref.shape
    points = rows * cols
    total = back_ref[...] + take_tile(recv_ref, points)
    for s in range(rows):
        out_ref[slot_row(s, rows)] = total[s * cols : (s + 1) * cols].astype(BF16)
    lines, hidden = up_ref.shape
    share = hidden // TILE
    for b in range(recv_ref.shape[0]):
        held[pl.ds(b * TILE, TILE), :] = jnp.concatenate(
            [recv_ref[b, :, points : points + share].astype(F32), jnp.zeros((TILE, 128 - share), F32)],
            axis=1,
        )
    for parity, ref in enumerate((up_ref, down_ref)):
        ref[...] = jnp.concatenate(
            [
                held[pl.ds(parity * TILE + i, lines, stride=2 * TILE), :][:, :share]
                for i in range(TILE)
            ],
            axis=1,
        )


def body(state_grid, spectral_filter, up_weight, down_weight, cotangent):
    _, rows, cols, channels = state_grid.shape
    bands, chunks = lax.axis_size("lat"), lax.axis_size("lon")
    band = lax.axis_index("lat")
    degrees = spectral_filter.shape[0]
    hidden = up_weight.shape[1]
    lat_total, lon_total = rows * bands, cols * chunks
    orders = degrees // bands
    points = rows * cols
    used = padded(points)
    modes = 2 * degrees
    line = TILE * 2 * orders
    wide = rows // TILE * line
    tiles = orders // TILE

    state = state_grid.reshape(rows, cols, channels)
    cot = cotangent.reshape(rows, cols, channels)

    sent = call(
        split_kernel,
        shaped((chunks, TILE, used), BF16),
        state,
        scratch=[pltpu.VMEM((points, channels), F32)],
    )
    whole = lax.all_to_all(sent, "lon", 0, 0, tiled=True)

    table, turned = fourier_tables(lon_total, bands, orders)
    legendre = legendre_tables(bands, orders, lat_total, degrees)
    gains = spectral_filter.T
    own = lax.dynamic_slice_in_dim(row_scale(lat_total, lon_total), band * rows, rows)
    own = jnp.where(band * 2 >= bands, jnp.flip(own), own)
    scale = jnp.repeat(own, TILE)[:, None]

    def forward(x, doubled, skip, *extra):
        return call(
            functools.partial(forward_kernel, rows, cols, doubled, bool(extra), skip),
            shaped((bands, TILE, wide + (128 if skip else 0)), BF16),
            x, table, *extra,
            scratch=[
                pltpu.VMEM((rows * TILE, lon_total), F32),
                tiles_of(rows * TILE, modes),
            ],
        )

    def turn(x):
        return lax.all_to_all(x, "lat", 0, 0, tiled=True)

    def spectral(x, has_piece):
        outs = [shaped((bands, TILE, wide), BF16)]
        if has_piece:
            outs.append(shaped((TILE, 128), F32))
        return call(
            functools.partial(spectral_kernel, rows, tiles, has_piece),
            outs,
            x, gains, legendre,
            scratch=[tiles_of(256, lat_total // 2)] * 2,
        )

    def inverse(x, doubled, *extra):
        return call(
            functools.partial(inverse_kernel, rows, cols, doubled, bool(extra)),
            shaped((chunks, TILE, used), BF16),
            x, turned, *extra,
            scratch=[tiles_of(rows * TILE, modes)],
        )

    spread = turn(forward(whole, False, 0, scale))
    waves = turn(spectral(spread, False)[0])
    smooth = lax.all_to_all(inverse(waves, True), "lon", 0, 0, tiled=True)

    sent, back_mixed = call(
        functools.partial(mlp_kernel, points // 6, 1.0 / math.sqrt(lat_total * lon_total)),
        [
            shaped((chunks, TILE, used + bands // TILE * hidden), BF16),
            shaped((points, channels), F32),
        ],
        smooth, state, cot, up_weight, down_weight,
        in_hbm=(1,),
        scratch=[
            pltpu.VMEM((points, channels), F32),
            pltpu.VMEM((points, channels), F32),
            pltpu.VMEM((points, hidden), BF16),
            pltpu.VMEM((points, hidden), BF16),
            pltpu.VMEM((2, hidden // 128, channels, 128), F32),
            pltpu.VMEM((points, channels), F32),
            pltpu.SemaphoreType.DMA,
        ],
    )
    whole = lax.all_to_all(sent, "lon", 0, 0, tiled=True)
    filtered, piece = spectral(turn(forward(whole, True, hidden)), True)
    back_waves = turn(filtered)
    field = lax.all_to_all(inverse(back_waves, False, scale, piece), "lon", 0, 0, tiled=True)
    grad_field, grad_up, grad_down = call(
        join_kernel,
        [
            shaped((rows, cols, channels), BF16),
            shaped((chunks // 2, hidden), F32),
            shaped((chunks // 2, hidden), F32),
        ],
        field, back_mixed,
        scratch=[pltpu.VMEM((chunks * TILE, 128), F32)],
    )
    return grad_field.reshape(state_grid.shape), grad_up, grad_down


def solution(mesh):
    placed = (P(None, "lat", "lon", None), P(None, "lon"), P(), P(), P(None, "lat", "lon", None))
    return jax.shard_map(
        body,
        mesh=mesh,
        in_specs=placed,
        out_specs=(P(None, "lat", "lon", None), P("lat", None), P("lat", None)),
        check_vma=False,
    )
```

time: 240 us -> 182 us (0.76)
  blocking collectives: 138 us -> 117 us
  starting transfers between devices: 35.1 us -> 22.3 us
  other arithmetic: 11.5 us -> 1.58 us
  local copies, waits for them, and re-layouts: 8.79 us -> 1.33 us
  waiting for transfers between devices: 20.2 us -> 13.4 us
    all_gather x2 -> x0, blocking collectives: 44.1 us -> none  [the longest x1 38.8 us: body(): pieces = lax.all_gather(piece, lon_axes, axis=0, tiled=False)]
    all_to_all x4 -> x6, blocking collectives: 94.2 us -> 117 us  [the longest x3 44.7 us: turn(): return lax.all_to_all(x, 'lat', 0, 0, tiled=True)]
    all_to_all x4 -> x2, starting transfers between devices: 35.1 us -> 22.3 us  [the longest x1 11.7 us: turn(): return lax.all_to_all(x, 'lat', 0, 0, tiled=True)]
    all_to_all x4 -> x2, waiting for transfers between devices: 20.2 us -> 13.4 us  [the longest x1 9.29 us: body(): whole = lax.all_to_all(sent, 'lon', 0, 0, tiled=True)]
    cos x1, other arithmetic: 6.74 us -> 0.05 us  [legendre_tables(): cosine = jnp.cos(colatitude)]
    unnamed x34 -> x20, local copies, waits for them, and re-layouts: 6.51 us -> 0.99 us
    pallas_call x10 -> x11, Pallas kernels: 24.5 us -> 25.1 us  [call(): pl.pallas_call(kernel, out_shape=shapes, in_specs=[pl.BlockSpec(memory_sp...]
  transfers between devices with their start and end apart: 4 -> 2, of which waited for: 2 -> 2; matrix products, arithmetic and copies ran while one was open for 6% -> 1% of each run, Pallas kernels for 3% -> 4%
where the time goes in v3:
time: 182 us; the launch traced here: 181 us
  blocking collectives  117 us (64%)
  Pallas kernels  25.1 us (14%)
  starting transfers between devices  22.3 us (12%)
  waiting for transfers between devices  13.4 us (7%)
    all_to_all x3, blocking collectives, turn(): return lax.all_to_all(x, 'lat', 0, 0, tiled=True)  44.7 us
    all_to_all x1, blocking collectives, body(): whole = lax.all_to_all(sent, 'lon', 0, 0, tiled=True)  27.1 us
    pallas_call x11, Pallas kernels, call(): pl.pallas_call(kernel, out_shape=shapes, in_specs=[pl.BlockSpec(memory_sp...  25.1 us
    all_to_all x1, blocking collectives, body(): lax.all_to_all(inverse(back_waves, False, scale, piece), 'lon', 0, 0, til...  22.8 us
    all_to_all x1, blocking collectives, body(): smooth = lax.all_to_all(inverse(waves, True), 'lon', 0, 0, tiled=True)  22 us
    all_to_all x1, starting transfers between devices, turn(): return lax.all_to_all(x, 'lat', 0, 0, tiled=True)  11.7 us
    all_to_all x1, starting transfers between devices, body(): whole = lax.all_to_all(sent, 'lon', 0, 0, tiled=True)  10.6 us
    all_to_all x1, waiting for transfers between devices, body(): whole = lax.all_to_all(sent, 'lon', 0, 0, tiled=True)  9.29 us
  transfers between devices with their start and end apart: 2, of which 2 were waited for; matrix products, arithmetic and copies ran while one was open for 1% of the time, Pallas kernels for 4%

profile of v3, /device:TPU:1, one launch (start us, length us, event | category | flops | bytes accessed | tf_op | source)
XLA Modules:
  0.0 181.2 jit_solution(8171758943377281495)
XLA Ops:
  0.6 0.0 copy-start.2
  0.6 1.0 copy-done.2
  1.6 0.9 shard_map.76
  2.5 10.6 %all-to-all-start = ((bf16[32,8,640]{2,1,0:T(8,128)(2,1)}), bf16[32,8,640]{2,1,0:T(8,128)(2,1)S(1)}, u32[]{:S(2)}, u32[]{:S(2)}) async-start(bf16[32,8,640]{2,1,0:T(8,128)(2,1)} %shard_map.76), calls=%async_computation | async-start | bytes 655360 | tf_op jit(solution)/shard_map/all_to_all | solution.py:515
  13.1 1.1 fusion
  14.2 0.1 dynamic_slice.3
  14.3 0.1 rev.4
  14.4 0.1 broadcast_select_fusion
  14.5 0.1 broadcast_in_dim.16
  14.5 0.1 broadcast_in_dim_reshape.4.refs_2_
  14.6 0.0 copy-start.4
  14.6 1.8 %shard_map.77 = (bf16[768,768]{1,0:T(8,128)(2,1)S(1)}, bf16[768,768]{1,0:T(8,128)(2,1)S(1)}) custom-call(), custom_call_target="tpu_custom_call" | custom-call | flops 17694720 | bytes 4718592 | tf_op jit(solution)/shard_map/pallas_call | solution.py:24
  16.5 0.0 copy-start
  16.6 0.2 select_reduce_fusion
  16.8 9.3 %all-to-all-done.refs_0_ = bf16[32,8,640]{2,1,0:T(8,128)(2,1)S(1)} async-done(((bf16[32,8,640]{2,1,0:T(8,128)(2,1)}), bf16[32,8,640]{2,1,0:T(8,128)(2,1)S(1)}, u32[]{:S(2)}, u32[]{:S(2)}) %all-to-all-start) | async-done | bytes 327712 | tf_op jit(solution)/shard_map/all_to_all | solution.py:515
  26.0 2.0 %shard_map.78 = bf16[16,8,1152]{2,1,0:T(8,128)(2,1)} custom-call(bf16[32,8,640]{2,1,0:T(8,128)(2,1)S(1)} %all-to-all-done.refs_0_, bf16[768,768]{1,0:T(8,128)(2,1)S(1)} %get-tuple-element.12.refs_1_, f32[192,1]{1,0:T(8,128)S(1)} %broadcast_in_dim_reshape.4.refs_2_), custom_call_target="tpu_custom_call" | custom-call | tf_op jit(solution)/shard_map/pallas_call | solution.py:24
  28.1 0.0 copy-done.4
  28.1 0.0 copy-done
  28.1 11.7 %all-to-all-start.1 = ((bf16[16,8,1152]{2,1,0:T(8,128)(2,1)}), bf16[16,8,1152]{2,1,0:T(8,128)(2,1)}, u32[]{:S(2)}, u32[]{:S(2)}) async-start(bf16[16,8,1152]{2,1,0:T(8,128)(2,1)} %shard_map.78), calls=%async_computation.1 | async-start | bytes 589824 | tf_op jit(solution)/shard_map/all_to_all | solution.py:536
  39.9 0.1 multiply_add_fusion.diag_ref
  40.0 0.0 copy-start.9
  40.0 6.1 %shard_map.79.table_ref = bf16[192,6144]{1,0:T(8,128)(2,1)S(1)} custom-call(f32[8,192]{1,0:T(8,128)S(1)} %broadcast_in_dim.17.cos_ref, f32[24,192]{1,0:T(8,128)S(1)} %multiply_add_fusion.diag_ref), custom_call_target="tpu_custom_call" | custom-call | flops 40000000 | bytes 6000000 | tf_op jit(solution)/shard_map/pallas_call | solution.py:24
  46.0 4.1 %all-to-all-done.1.x_ref = bf16[16,8,1152]{2,1,0:T(8,128)(2,1)} async-done(((bf16[16,8,1152]{2,1,0:T(8,128)(2,1)}), bf16[16,8,1152]{2,1,0:T(8,128)(2,1)}, u32[]{:S(2)}, u32[]{:S(2)}) %all-to-all-start.1) | async-done | bytes 294944 | tf_op jit(solution)/shard_map/all_to_all | solution.py:536
  50.2 0.0 copy-done.9
  50.2 3.4 %shard_map.80 = bf16[16,8,1152]{2,1,0:T(8,128)(2,1)S(1)} custom-call(bf16[16,8,1152]{2,1,0:T(8,128)(2,1)} %all-to-all-done.1.x_ref, f32[8,384]{1,0:T(8,128)S(1)} %bitcast.7, bf16[192,6144]{1,0:T(8,128)(2,1)S(1)} %shard_map.79.table_ref), custom_call_target="tpu_custom_call" | custom-call | tf_op jit(solution)/shard_map/pallas_call | solution.py:24
  53.6 15.1 %all_to_all.40.refs_0_ = bf16[16,8,1152]{2,1,0:T(8,128)(2,1)S(1)} all-to-all(bf16[16,8,1152]{2,1,0:T(8,128)(2,1)S(1)} %shard_map.80), channel_id=1, replica_groups=mesh['lat'=16,'lon'=32] {'lat'}, dimensions={0} | all-to-all | bytes 589824 | tf_op jit(solution)/shard_map/all_to_all | solution.py:536
  68.6 0.0 copy-start.3
  68.6 0.0 copy-start.7
  68.7 0.0 copy-start.8
  68.7 1.3 shard_map.81
  70.0 22.0 %all_to_all.41.recv_ref = bf16[32,8,640]{2,1,0:T(8,128)(2,1)S(1)} all-to-all(bf16[32,8,640]{2,1,0:T(8,128)(2,1)S(1)} %shard_map.81), channel_id=1, replica_groups=mesh['lat'=16,'lon'=32] {'lon'}, dimensions={0} | all-to-all | bytes 655360 | tf_op jit(solution)/shard_map/all_to_all | solution.py:559
  91.9 0.0 copy-done.3
  92.0 0.0 copy-done.6
  92.0 0.0 copy-done.7
  92.0 0.0 copy-done.8
  92.0 3.6 %shard_map.82 = (bf16[32,8,1664]{2,1,0:T(8,128)(2,1)S(1)}, f32[576,256]{1,0:T(8,128)S(1)}) custom-call(bf16[32,8,640]{2,1,0:T(8,128)(2,1)S(1)} %all_to_all.41.recv_ref, bf16[24,24,256]{2,1,0:T(8,128)(2,1)S(1)} %bitcast.5, bf16[24,24,256]{2,1,0:T(8,128)(2,1)S(1)} %bitcast.6, bf16[256,512]{1,0:T(8,128)(2,1)S(1)} %copy-done.7, bf16[256,512]{1,0:T(8,128)(2,1)S(1)} %copy-done.8), custom_call_target="tpu_custom_call" | custom-call | tf_op jit(solution)/shard_map/pallas_call | solution.py:24
  95.6 0.0 copy-start.1
  95.6 27.1 %all_to_all.42.refs_0_ = bf16[32,8,1664]{2,1,0:T(8,128)(2,1)S(1)} all-to-all(bf16[32,8,1664]{2,1,0:T(8,128)(2,1)S(1)} %get-tuple-element.14), channel_id=1, replica_groups=mesh['lat'=16,'lon'=32] {'lon'}, dimensions={0} | all-to-all | bytes 1703936 | tf_op jit(solution)/shard_map/all_to_all | solution.py:579
  122.8 0.0 copy-done.1
  122.8 1.4 shard_map.83
  124.1 13.9 %all_to_all.43.x_ref = bf16[16,8,1280]{2,1,0:T(8,128)(2,1)S(1)} all-to-all(bf16[16,8,1280]{2,1,0:T(8,128)(2,1)S(1)} %shard_map.83), channel_id=1, replica_groups=mesh['lat'=16,'lon'=32] {'lat'}, dimensions={0} | all-to-all | bytes 655360 | tf_op jit(solution)/shard_map/all_to_all | solution.py:536
  138.0 0.0 copy-start.5
  138.0 2.4 %shard_map.84 = (bf16[16,8,1152]{2,1,0:T(8,128)(2,1)S(1)}, f32[8,128]{1,0:T(8,128)S(1)}) custom-call(bf16[16,8,1280]{2,1,0:T(8,128)(2,1)S(1)} %all_to_all.43.x_ref, f32[8,384]{1,0:T(8,128)S(1)} %bitcast.8, bf16[192,6144]{1,0:T(8,128)(2,1)S(1)} %shard_map.79.table_ref), custom_call_target="tpu_custom_call" | custom-call | tf_op jit(solution)/shard_map/pallas_call | solution.py:24
  140.5 15.7 %all_to_all.44.refs_0_ = bf16[16,8,1152]{2,1,0:T(8,128)(2,1)S(1)} all-to-all(bf16[16,8,1152]{2,1,0:T(8,128)(2,1)S(1)} %get-tuple-element.15), channel_id=1, replica_groups=mesh['lat'=16,'lon'=32] {'lat'}, dimensions={0} | all-to-all | bytes 589824 | tf_op jit(solution)/shard_map/all_to_all | solution.py:536
  156.2 0.0 copy-done.5
  156.2 1.3 shard_map.85
  157.5 22.8 %all_to_all.45.recv_ref = bf16[32,8,640]{2,1,0:T(8,128)(2,1)S(1)} all-to-all(bf16[32,8,640]{2,1,0:T(8,128)(2,1)S(1)} %shard_map.85), channel_id=1, replica_groups=mesh['lat'=16,'lon'=32] {'lon'}, dimensions={0} | all-to-all | bytes 655360 | tf_op jit(solution)/shard_map/all_to_all | solution.py:582
  180.3 0.9 shard_map.86
  (10 shorter events, 0.2 us)
Async XLA Ops:
  0.6 1.0 copy-start.2
  2.5 23.5 %all-to-all-start = ((bf16[32,8,640]{2,1,0:T(8,128)(2,1)}), bf16[32,8,640]{2,1,0:T(8,128)(2,1)S(1)}, u32[]{:S(2)}, u32[]{:S(2)}) async-start(bf16[32,8,640]{2,1,0:T(8,128)(2,1)} %shard_map.76), calls=%async_computation | async-start | bytes 655360 | tf_op jit(solution)/shard_map/all_to_all | solution.py:515
  14.6 13.4 %copy-start.4 = (f32[192,1]{1,0:T(8,128)}, f32[192,1]{1,0:T(8,128)S(1)}, u32[]{:S(2)}) copy-start(f32[192,1]{1,0:T(8,128)S(1)} %broadcast_in_dim_reshape.4.refs_2_) | copy-start | bytes 2308
  16.5 11.6 %copy-start = (bf16[768,768]{1,0:T(8,128)(2,1)}, bf16[768,768]{1,0:T(8,128)(2,1)S(1)}, u32[]{:S(2)}) copy-start(bf16[768,768]{1,0:T(8,128)(2,1)S(1)} %get-tuple-element.12.refs_1_) | copy-start | bytes 3538948
  28.1 22.1 %all-to-all-start.1 = ((bf16[16,8,1152]{2,1,0:T(8,128)(2,1)}), bf16[16,8,1152]{2,1,0:T(8,128)(2,1)}, u32[]{:S(2)}, u32[]{:S(2)}) async-start(bf16[16,8,1152]{2,1,0:T(8,128)(2,1)} %shard_map.78), calls=%async_computation.1 | async-start | bytes 589824 | tf_op jit(solution)/shard_map/all_to_all | solution.py:536
  40.0 10.2 %copy-start.9 = (f32[384,8]{0,1:T(8,128)S(1)}, f32[384,8]{0,1:T(8,128)}, u32[]{:S(2)}) copy-start(f32[384,8]{0,1:T(8,128)} %param.6) | copy-start | bytes 36868
  68.6 23.3 %copy-start.3 = (bf16[1,24,24,256]{3,2,1,0:T(8,128)(2,1)S(1)}, bf16[1,24,24,256]{3,2,1,0:T(8,128)(2,1)}, u32[]{:S(2)}) copy-start(bf16[1,24,24,256]{3,2,1,0:T(8,128)(2,1)} %param.5) | copy-start | bytes 884740
  68.6 23.3 %copy-start.6 = (bf16[1,24,24,256]{3,2,1,0:T(8,128)(2,1)S(1)}, bf16[1,24,24,256]{3,2,1,0:T(8,128)(2,1)}, u32[]{:S(2)}) copy-start(bf16[1,24,24,256]{3,2,1,0:T(8,128)(2,1)} %param.9) | copy-start | bytes 884740
  68.6 23.3 %copy-start.7 = (bf16[256,512]{1,0:T(8,128)(2,1)S(1)}, bf16[256,512]{1,0:T(8,128)(2,1)}, u32[]{:S(2)}) copy-start(bf16[256,512]{1,0:T(8,128)(2,1)} %up_ref.1) | copy-start | bytes 786436
  68.7 23.3 %copy-start.8 = (bf16[256,512]{1,0:T(8,128)(2,1)S(1)}, bf16[256,512]{1,0:T(8,128)(2,1)}, u32[]{:S(2)}) copy-start(bf16[256,512]{1,0:T(8,128)(2,1)} %down_ref.1) | copy-start | bytes 786436
  95.6 27.2 %copy-start.1 = (bf16[768,768]{1,0:T(8,128)(2,1)S(1)}, bf16[768,768]{1,0:T(8,128)(2,1)}, u32[]{:S(2)}) copy-start(bf16[768,768]{1,0:T(8,128)(2,1)} %copy-done) | copy-start | bytes 3538948
  138.0 18.1 %copy-start.5 = (f32[192,1]{1,0:T(8,128)S(1)}, f32[192,1]{1,0:T(8,128)}, u32[]{:S(2)}) copy-start(f32[192,1]{1,0:T(8,128)} %copy-done.4) | copy-start | bytes 2308

commit v4 on v3

--- a/solution.py
+++ b/solution.py
@@ -102,7 +102,7 @@
     return jnp.where(part == 1, -sine, cosine), jnp.where(part == 1, cosine, sine)
 
 
-def fourier_kernel(bands, orders, table_out, turned_out, table_ref, turned_ref, sems):
+def fourier_kernel(bands, orders, start_ref, table_ref, turned_ref):
     lon_total, modes = table_ref.shape
     per = 2 * orders
 
@@ -121,8 +121,6 @@
         return rotate(later, turn)
 
     lax.fori_loop(0, lon_total // (2 * TILE), step, phased(row * order, rank % 2, lon_total))
-    first = pltpu.make_async_copy(table_ref, table_out, sems.at[0])
-    first.start()
 
     shape = (TILE, lon_total)
     lon_index = lax.broadcasted_iota(jnp.int32, shape, 1).astype(F32)
@@ -141,23 +139,18 @@
         return rotate(pair, outer)
 
     lax.fori_loop(0, modes // per, group_step, start)
-    second = pltpu.make_async_copy(turned_ref, turned_out, sems.at[1])
-    second.start()
-    first.wait()
-    second.wait()
-
-
-def fourier_tables(lon_total, bands, orders):
+
+
+def fourier_tables(start, lon_total, bands, orders):
     modes = 2 * bands * orders
     shapes = [(lon_total, modes), (modes, lon_total)]
     return call(
         functools.partial(fourier_kernel, bands, orders),
         [shaped(shape, BF16) for shape in shapes],
-        scratch=[pltpu.VMEM(shape, BF16) for shape in shapes] + [pltpu.SemaphoreType.DMA((2,))],
+        start,
         cost=pl.CostEstimate(
             flops=30 * modes * lon_total, bytes_accessed=8 * modes * lon_total, transcendentals=0
         ),
-        in_hbm=(0, 1),
     )
 
 
@@ -410,12 +403,8 @@
         out_ref[b] = jnp.concatenate(parts + [rest], axis=1).astype(BF16)
 
 
-def erf(values):
-    return lax.erf(values)
-
-
 def mlp_kernel(
-    block, grad_scale,
+    grad_scale,
     recv_ref, state_ref, cot_ref, up_ref, down_ref,
     send_ref, back_out,
     mixed, cots, active_all, back_pre_all, grads, back_ref, sem,
@@ -430,24 +419,20 @@
         mixed[at, :] = mixed[at, :] + state_ref[row].astype(F32)
         cots[at, :] = cot_ref[row].astype(F32)
 
-    def step(index, _):
-        at = pl.ds(pl.multiple_of(index * block, block), block)
-        up = up_ref[...]
-        pre = dot(mixed[at, :].astype(BF16), up)
-        back_active = dot(cots[at, :].astype(BF16), down_ref[...])
-        cdf = 0.5 * (1.0 + erf(pre * (1.0 / math.sqrt(2.0))))
-        density = jnp.exp(-0.5 * pre * pre) * (1.0 / math.sqrt(2.0 * math.pi))
-        active_all[at, :] = (pre * cdf).astype(BF16)
-        back_pre = (back_active * (cdf + pre * density)).astype(BF16)
-        back_pre_all[at, :] = back_pre
-        back_ref[at, :] = cots[at, :] + dot(back_pre, up, ((1,), (1,)))
-        return 0
-
-    lax.fori_loop(0, points // block, step, 0)
+    up = up_ref[...]
+    mixed_low = mixed[...].astype(BF16)
+    cot_low = cots[...].astype(BF16)
+    pre = dot(mixed_low, up)
+    back_active = dot(cot_low, down_ref[...])
+    cdf = 0.5 * (1.0 + lax.erf(pre * (1.0 / math.sqrt(2.0))))
+    density = jnp.exp(-0.5 * pre * pre) * (1.0 / math.sqrt(2.0 * math.pi))
+    active_all[...] = (pre * cdf).astype(BF16)
+    back_pre_all[...] = (back_active * (cdf + pre * density)).astype(BF16)
+    back_ref[...] = cots[...] + dot(back_pre_all[...], up, ((1,), (1,)))
     kept = pltpu.make_async_copy(back_ref, back_out, sem)
     kept.start()
-    up_part = dot(mixed[...].astype(BF16), back_pre_all[...], ((0,), (0,)))
-    down_part = dot(cots[...].astype(BF16), active_all[...], ((0,), (0,)))
+    up_part = dot(mixed_low, back_pre_all[...], ((0,), (0,)))
+    down_part = dot(cot_low, active_all[...], ((0,), (0,)))
     place(grads, up_part * grad_scale, lead=(0,))
     place(grads, down_part * grad_scale, lead=(1,))
 
@@ -514,8 +499,9 @@
     )
     whole = lax.all_to_all(sent, "lon", 0, 0, tiled=True)
 
-    table, turned = fourier_tables(lon_total, bands, orders)
     legendre = legendre_tables(bands, orders, lat_total, degrees)
+    start, legendre = lax.optimization_barrier((jnp.zeros((TILE, 128), F32), legendre))
+    table, turned = fourier_tables(start, lon_total, bands, orders)
     gains = spectral_filter.T
     own = lax.dynamic_slice_in_dim(row_scale(lat_total, lon_total), band * rows, rows)
     own = jnp.where(band * 2 >= bands, jnp.flip(own), own)
@@ -559,7 +545,7 @@
     smooth = lax.all_to_all(inverse(waves, True), "lon", 0, 0, tiled=True)
 
     sent, back_mixed = call(
-        functools.partial(mlp_kernel, points // 6, 1.0 / math.sqrt(lat_total * lon_total)),
+        functools.partial(mlp_kernel, 1.0 / math.sqrt(lat_total * lon_total)),
         [
             shaped((chunks, TILE, used + bands // TILE * hidden), BF16),
             shaped((points, channels), F32),

time: 182 us -> 184 us (1.011)
  blocking collectives: 117 us -> 140 us
  waiting for transfers between devices: 13.4 us -> 2.18 us
  starting transfers between devices: 22.3 us -> 11.1 us
  local copies, waits for them, and re-layouts: 1.33 us -> 5.15 us
  Pallas kernels: 25.1 us -> 22.5 us
    all_to_all x3 -> x4, blocking collectives: 44.7 us -> 66.3 us  [turn(): return lax.all_to_all(x, 'lat', 0, 0, tiled=True)]
    all_to_all x1 -> x0, starting transfers between devices: 11.7 us -> none  [turn(): return lax.all_to_all(x, 'lat', 0, 0, tiled=True)]
    all_to_all x1, waiting for transfers between devices: 9.29 us -> 2.18 us  [body(): whole = lax.all_to_all(sent, 'lon', 0, 0, tiled=True)]
    all_to_all x1 -> x0, waiting for transfers between devices: 4.12 us -> none  [turn(): return lax.all_to_all(x, 'lat', 0, 0, tiled=True)]
    unnamed x20 -> x22, local copies, waits for them, and re-layouts: 0.99 us -> 4.16 us
    pallas_call x11, Pallas kernels: 25.1 us -> 22.5 us  [call(): pl.pallas_call(kernel, out_shape=shapes, in_specs=[pl.BlockSpec(memory_sp...]
    all_to_all x1, blocking collectives: 22 us -> 24 us  [body(): smooth = lax.all_to_all(inverse(waves, True), 'lon', 0, 0, tiled=True)]
  transfers between devices with their start and end apart: 2 -> 1, of which waited for: 2 -> 1; matrix products, arithmetic and copies ran while one was open for 1% -> 1% of each run, Pallas kernels for 4% -> 4%
where the time goes in v4:
time: 184 us; the launch traced here: 183 us
  blocking collectives  140 us (76%)
  Pallas kernels  22.5 us (12%)
  starting transfers between devices  11.1 us (6%)
  local copies, waits for them, and re-layouts  5.15 us (3%)
  waiting for transfers between devices  2.18 us (1%)
    all_to_all x4, blocking collectives, turn(): return lax.all_to_all(x, 'lat', 0, 0, tiled=True)  66.3 us
    all_to_all x1, blocking collectives, body(): whole = lax.all_to_all(sent, 'lon', 0, 0, tiled=True)  27.1 us
    all_to_all x1, blocking collectives, body(): smooth = lax.all_to_all(inverse(waves, True), 'lon', 0, 0, tiled=True)  24 us
    all_to_all x1, blocking collectives, body(): lax.all_to_all(inverse(back_waves, False, scale, piece), 'lon', 0, 0, til...  22.8 us
    pallas_call x11, Pallas kernels, call(): pl.pallas_call(kernel, out_shape=shapes, in_specs=[pl.BlockSpec(memory_sp...  22.5 us
    all_to_all x1, starting transfers between devices, body(): whole = lax.all_to_all(sent, 'lon', 0, 0, tiled=True)  11.1 us
    unnamed x22, local copies, waits for them, and re-layouts  4.16 us
  transfers between devices with their start and end apart: 1, of which 1 were waited for; matrix products, arithmetic and copies ran while one was open for 1% of the time, Pallas kernels for 4%

profile of v4, /device:TPU:1, one launch (start us, length us, event | category | flops | bytes accessed | tf_op | source)
XLA Modules:
  0.0 183.5 jit_solution(1664430835463477715)
XLA Ops:
  0.6 0.0 copy-start.3
  0.6 1.0 copy-done.3
  1.6 0.9 shard_map.76
  2.5 11.1 %all-to-all-start = ((bf16[32,8,640]{2,1,0:T(8,128)(2,1)}), bf16[32,8,640]{2,1,0:T(8,128)(2,1)}, u32[]{:S(2)}, u32[]{:S(2)}) async-start(bf16[32,8,640]{2,1,0:T(8,128)(2,1)} %shard_map.76), calls=%async_computation | async-start | bytes 655360 | tf_op jit(solution)/shard_map/all_to_all | solution.py:500
  13.7 1.1 fusion
  14.8 0.1 dynamic_slice.3
  14.9 0.1 rev.4
  15.0 0.1 broadcast_select_fusion
  15.1 0.1 broadcast_in_dim.22
  15.1 0.7 broadcast_in_dim_reshape.4.refs_2_
  15.9 0.2 select_reduce_fusion
  16.1 0.1 multiply_add_fusion.diag_ref
  16.2 6.1 %shard_map.77.table_ref = bf16[192,6144]{1,0:T(8,128)(2,1)S(1)} custom-call(f32[8,192]{1,0:T(8,128)S(1)} %broadcast_in_dim.19.cos_ref, f32[24,192]{1,0:T(8,128)S(1)} %multiply_add_fusion.diag_ref), custom_call_target="tpu_custom_call" | custom-call | flops 40000000 | bytes 6000000 | tf_op jit(solution)/shard_map/pallas_call | solution.py:24
  22.2 1.3 shard_map.78
  23.5 0.0 copy-start
  23.5 1.0 copy-done
  24.5 2.2 %all-to-all-done.refs_0_ = bf16[32,8,640]{2,1,0:T(8,128)(2,1)} async-done(((bf16[32,8,640]{2,1,0:T(8,128)(2,1)}), bf16[32,8,640]{2,1,0:T(8,128)(2,1)}, u32[]{:S(2)}, u32[]{:S(2)}) %all-to-all-start) | async-done | bytes 327712 | tf_op jit(solution)/shard_map/all_to_all | solution.py:500
  26.7 0.0 copy-start.1
  26.7 1.3 copy-done.1
  28.0 0.0 copy-start.5
  28.0 0.9 copy-done.5
  28.9 0.0 copy-start.10
  28.9 2.3 %shard_map.79 = bf16[16,8,1152]{2,1,0:T(8,128)(2,1)S(1)} custom-call(bf16[32,8,640]{2,1,0:T(8,128)(2,1)} %all-to-all-done.refs_0_, bf16[768,768]{1,0:T(8,128)(2,1)S(1)} %copy-done.1, f32[192,1]{1,0:T(8,128)S(1)} %copy-done.5), custom_call_target="tpu_custom_call" | custom-call | tf_op jit(solution)/shard_map/pallas_call | solution.py:24
  31.2 21.2 %all_to_all.40.x_ref = bf16[16,8,1152]{2,1,0:T(8,128)(2,1)S(1)} all-to-all(bf16[16,8,1152]{2,1,0:T(8,128)(2,1)S(1)} %shard_map.79), channel_id=1, replica_groups=mesh['lat'=16,'lon'=32] {'lat'}, dimensions={0} | all-to-all | bytes 589824 | tf_op jit(solution)/shard_map/all_to_all | solution.py:522
  52.4 0.0 copy-done.10
  52.4 2.4 %shard_map.80 = bf16[16,8,1152]{2,1,0:T(8,128)(2,1)S(1)} custom-call(bf16[16,8,1152]{2,1,0:T(8,128)(2,1)S(1)} %all_to_all.40.x_ref, f32[8,384]{1,0:T(8,128)S(1)} %bitcast.7, bf16[192,6144]{1,0:T(8,128)(2,1)S(1)} %shard_map.77.table_ref), custom_call_target="tpu_custom_call" | custom-call | tf_op jit(solution)/shard_map/pallas_call | solution.py:24
  54.8 15.1 %all_to_all.41.refs_0_ = bf16[16,8,1152]{2,1,0:T(8,128)(2,1)S(1)} all-to-all(bf16[16,8,1152]{2,1,0:T(8,128)(2,1)S(1)} %shard_map.80), channel_id=1, replica_groups=mesh['lat'=16,'lon'=32] {'lat'}, dimensions={0} | all-to-all | bytes 589824 | tf_op jit(solution)/shard_map/all_to_all | solution.py:522
  69.9 0.0 copy-start.4
  69.9 0.0 copy-start.7
  69.9 0.0 copy-start.8
  69.9 1.3 shard_map.81
  71.2 24.0 %all_to_all.42.recv_ref = bf16[32,8,640]{2,1,0:T(8,128)(2,1)S(1)} all-to-all(bf16[32,8,640]{2,1,0:T(8,128)(2,1)S(1)} %shard_map.81), channel_id=1, replica_groups=mesh['lat'=16,'lon'=32] {'lon'}, dimensions={0} | all-to-all | bytes 655360 | tf_op jit(solution)/shard_map/all_to_all | solution.py:545
  95.2 0.0 copy-done.4
  95.2 0.0 copy-done.7
  95.2 0.0 copy-done.8
  95.2 0.0 copy-done.9
  95.2 2.2 %shard_map.82 = (bf16[32,8,1664]{2,1,0:T(8,128)(2,1)S(1)}, f32[576,256]{1,0:T(8,128)S(1)}) custom-call(bf16[32,8,640]{2,1,0:T(8,128)(2,1)S(1)} %all_to_all.42.recv_ref, bf16[24,24,256]{2,1,0:T(8,128)(2,1)S(1)} %bitcast.5, bf16[24,24,256]{2,1,0:T(8,128)(2,1)S(1)} %bitcast.6, bf16[256,512]{1,0:T(8,128)(2,1)S(1)} %copy-done.8, bf16[256,512]{1,0:T(8,128)(2,1)S(1)} %copy-done.9), custom_call_target="tpu_custom_call" | custom-call | tf_op jit(solution)/shard_map/pallas_call | solution.py:24
  97.4 0.0 copy-start.2
  97.4 27.1 %all_to_all.43.refs_0_ = bf16[32,8,1664]{2,1,0:T(8,128)(2,1)S(1)} all-to-all(bf16[32,8,1664]{2,1,0:T(8,128)(2,1)S(1)} %get-tuple-element.18), channel_id=1, replica_groups=mesh['lat'=16,'lon'=32] {'lon'}, dimensions={0} | all-to-all | bytes 1703936 | tf_op jit(solution)/shard_map/all_to_all | solution.py:565
  124.6 0.0 copy-done.2
  124.6 1.4 shard_map.83
  125.9 14.3 %all_to_all.44.x_ref = bf16[16,8,1280]{2,1,0:T(8,128)(2,1)S(1)} all-to-all(bf16[16,8,1280]{2,1,0:T(8,128)(2,1)S(1)} %shard_map.83), channel_id=1, replica_groups=mesh['lat'=16,'lon'=32] {'lat'}, dimensions={0} | all-to-all | bytes 655360 | tf_op jit(solution)/shard_map/all_to_all | solution.py:522
  140.3 2.4 %shard_map.84 = (bf16[16,8,1152]{2,1,0:T(8,128)(2,1)S(1)}, f32[8,128]{1,0:T(8,128)S(1)}) custom-call(bf16[16,8,1280]{2,1,0:T(8,128)(2,1)S(1)} %all_to_all.44.x_ref, f32[8,384]{1,0:T(8,128)S(1)} %bitcast.8, bf16[192,6144]{1,0:T(8,128)(2,1)S(1)} %shard_map.77.table_ref), custom_call_target="tpu_custom_call" | custom-call | tf_op jit(solution)/shard_map/pallas_call | solution.py:24
  142.7 15.7 %all_to_all.45.refs_0_ = bf16[16,8,1152]{2,1,0:T(8,128)(2,1)S(1)} all-to-all(bf16[16,8,1152]{2,1,0:T(8,128)(2,1)S(1)} %get-tuple-element.19), channel_id=1, replica_groups=mesh['lat'=16,'lon'=32] {'lat'}, dimensions={0} | all-to-all | bytes 589824 | tf_op jit(solution)/shard_map/all_to_all | solution.py:522
  158.4 0.0 copy-done.6
  158.4 1.3 shard_map.85
  159.7 22.8 %all_to_all.46.recv_ref = bf16[32,8,640]{2,1,0:T(8,128)(2,1)S(1)} all-to-all(bf16[32,8,640]{2,1,0:T(8,128)(2,1)S(1)} %shard_map.85), channel_id=1, replica_groups=mesh['lat'=16,'lon'=32] {'lon'}, dimensions={0} | all-to-all | bytes 655360 | tf_op jit(solution)/shard_map/all_to_all | solution.py:568
  182.6 0.9 shard_map.86
  (12 shorter events, 0.2 us)
Async XLA Ops:
  0.6 1.0 copy-start.3
  2.5 24.2 %all-to-all-start = ((bf16[32,8,640]{2,1,0:T(8,128)(2,1)}), bf16[32,8,640]{2,1,0:T(8,128)(2,1)}, u32[]{:S(2)}, u32[]{:S(2)}) async-start(bf16[32,8,640]{2,1,0:T(8,128)(2,1)} %shard_map.76), calls=%async_computation | async-start | bytes 655360 | tf_op jit(solution)/shard_map/all_to_all | solution.py:500
  23.5 1.0 copy-start
  26.7 1.3 copy-start.1
  28.0 0.9 copy-start.5
  28.9 23.5 %copy-start.10 = (f32[384,8]{0,1:T(8,128)S(1)}, f32[384,8]{0,1:T(8,128)}, u32[]{:S(2)}) copy-start(f32[384,8]{0,1:T(8,128)} %param.6) | copy-start | bytes 36868
  69.9 25.3 %copy-start.4 = (bf16[1,24,24,256]{3,2,1,0:T(8,128)(2,1)S(1)}, bf16[1,24,24,256]{3,2,1,0:T(8,128)(2,1)}, u32[]{:S(2)}) copy-start(bf16[1,24,24,256]{3,2,1,0:T(8,128)(2,1)} %param.5) | copy-start | bytes 884740
  69.9 25.3 %copy-start.7 = (bf16[1,24,24,256]{3,2,1,0:T(8,128)(2,1)S(1)}, bf16[1,24,24,256]{3,2,1,0:T(8,128)(2,1)}, u32[]{:S(2)}) copy-start(bf16[1,24,24,256]{3,2,1,0:T(8,128)(2,1)} %param.9) | copy-start | bytes 884740
  69.9 25.3 %copy-start.8 = (bf16[256,512]{1,0:T(8,128)(2,1)S(1)}, bf16[256,512]{1,0:T(8,128)(2,1)}, u32[]{:S(2)}) copy-start(bf16[256,512]{1,0:T(8,128)(2,1)} %up_ref.1) | copy-start | bytes 786436
  69.9 25.3 %copy-start.9 = (bf16[256,512]{1,0:T(8,128)(2,1)S(1)}, bf16[256,512]{1,0:T(8,128)(2,1)}, u32[]{:S(2)}) copy-start(bf16[256,512]{1,0:T(8,128)(2,1)} %down_ref.1) | copy-start | bytes 786436
  97.4 27.2 %copy-start.2 = (bf16[768,768]{1,0:T(8,128)(2,1)S(1)}, bf16[768,768]{1,0:T(8,128)(2,1)}, u32[]{:S(2)}) copy-start(bf16[768,768]{1,0:T(8,128)(2,1)} %copy-done) | copy-start | bytes 3538948
  140.3 18.2 %copy-start.6 = (f32[192,1]{1,0:T(8,128)S(1)}, f32[192,1]{1,0:T(8,128)}, u32[]{:S(2)}) copy-start(f32[192,1]{1,0:T(8,128)} %broadcast_in_dim_reshape.4.refs_2_) | copy-start | bytes 2308

commit v5 on v4

--- a/solution.py
+++ b/solution.py
@@ -102,7 +102,7 @@
     return jnp.where(part == 1, -sine, cosine), jnp.where(part == 1, cosine, sine)
 
 
-def fourier_kernel(bands, orders, start_ref, table_ref, turned_ref):
+def fourier_kernel(bands, orders, table_out, turned_out, table_ref, turned_ref, sems):
     lon_total, modes = table_ref.shape
     per = 2 * orders
 
@@ -121,6 +121,8 @@
         return rotate(later, turn)
 
     lax.fori_loop(0, lon_total // (2 * TILE), step, phased(row * order, rank % 2, lon_total))
+    first = pltpu.make_async_copy(table_ref, table_out, sems.at[0])
+    first.start()
 
     shape = (TILE, lon_total)
     lon_index = lax.broadcasted_iota(jnp.int32, shape, 1).astype(F32)
@@ -139,18 +141,23 @@
         return rotate(pair, outer)
 
     lax.fori_loop(0, modes // per, group_step, start)
-
-
-def fourier_tables(start, lon_total, bands, orders):
+    second = pltpu.make_async_copy(turned_ref, turned_out, sems.at[1])
+    second.start()
+    first.wait()
+    second.wait()
+
+
+def fourier_tables(lon_total, bands, orders):
     modes = 2 * bands * orders
     shapes = [(lon_total, modes), (modes, lon_total)]
     return call(
         functools.partial(fourier_kernel, bands, orders),
         [shaped(shape, BF16) for shape in shapes],
-        start,
+        scratch=[pltpu.VMEM(shape, BF16) for shape in shapes] + [pltpu.SemaphoreType.DMA((2,))],
         cost=pl.CostEstimate(
             flops=30 * modes * lon_total, bytes_accessed=8 * modes * lon_total, transcendentals=0
         ),
+        in_hbm=(0, 1),
     )
 
 
@@ -334,18 +341,23 @@
             ]
             place(x_all, jnp.concatenate(parts, axis=0).T, h * 128, 128)
         sign, gain = signs[:, degrees - depth :], gains[:, degrees - depth :]
+        held = []
         for r in range(TILE):
             starts = [h * 128 + 2 * r + p for h in range(2) for p in range(2)]
             modes = [pick(x_all, half, start, TILE, 2 * TILE) for start in starts]
-            table = table_ref[:, at : at + depth]
-            at += depth
-            both = dot(jnp.concatenate(modes, axis=0).astype(BF16), table)
+            both = dot(
+                jnp.concatenate(modes, axis=0).astype(BF16), table_ref[:, at + r * depth : at + (r + 1) * depth]
+            )
             spectrum = both[: 2 * TILE] + sign * both[2 * TILE :]
             filtered = spectrum * gain
-            filtered = jnp.concatenate([filtered, sign * filtered], axis=0).astype(BF16)
-            waves = dot(filtered, table, ((1,), (1,)))
-            for i, start in enumerate(starts):
-                place(out_all, waves[i * TILE : (i + 1) * TILE], start, TILE, 2 * TILE)
+            held.append(jnp.concatenate([filtered, sign * filtered], axis=0).astype(BF16))
+        for r in range(TILE):
+            waves = dot(held[r], table_ref[:, at + r * depth : at + (r + 1) * depth], ((1,), (1,)))
+            for h in range(2):
+                for p in range(2):
+                    i = 2 * h + p
+                    place(out_all, waves[i * TILE : (i + 1) * TILE], h * 128 + 2 * r + p, TILE, 2 * TILE)
+        at += TILE * depth
         for h, order in enumerate((north, south)):
             waves = pick(out_all, half, h * 128, 128).T.astype(BF16)
             for n, t in enumerate(order):
@@ -499,9 +511,8 @@
     )
     whole = lax.all_to_all(sent, "lon", 0, 0, tiled=True)
 
+    table, turned = fourier_tables(lon_total, bands, orders)
     legendre = legendre_tables(bands, orders, lat_total, degrees)
-    start, legendre = lax.optimization_barrier((jnp.zeros((TILE, 128), F32), legendre))
-    table, turned = fourier_tables(start, lon_total, bands, orders)
     gains = spectral_filter.T
     own = lax.dynamic_slice_in_dim(row_scale(lat_total, lon_total), band * rows, rows)
     own = jnp.where(band * 2 >= bands, jnp.flip(own), own)

time: 184 us -> 179 us (0.973)
  blocking collectives: 140 us -> 117 us
  waiting for transfers between devices: 2.18 us -> 13.4 us
  starting transfers between devices: 11.1 us -> 22.3 us
  local copies, waits for them, and re-layouts: 5.15 us -> 1.33 us
    all_to_all x4 -> x3, blocking collectives: 66.3 us -> 44.7 us  [turn(): return lax.all_to_all(x, 'lat', 0, 0, tiled=True)]
    all_to_all x0 -> x1, starting transfers between devices: none -> 11.7 us  [turn(): return lax.all_to_all(x, 'lat', 0, 0, tiled=True)]
    all_to_all x1, waiting for transfers between devices: 2.18 us -> 9.29 us  [body(): whole = lax.all_to_all(sent, 'lon', 0, 0, tiled=True)]
    all_to_all x0 -> x1, waiting for transfers between devices: none -> 4.12 us  [turn(): return lax.all_to_all(x, 'lat', 0, 0, tiled=True)]
    unnamed x22 -> x20, local copies, waits for them, and re-layouts: 4.16 us -> 0.99 us
    all_to_all x1, blocking collectives: 24 us -> 22 us  [body(): smooth = lax.all_to_all(inverse(waves, True), 'lon', 0, 0, tiled=True)]
  transfers between devices with their start and end apart: 1 -> 2, of which waited for: 1 -> 2; matrix products, arithmetic and copies ran while one was open for 1% -> 1% of each run, Pallas kernels for 4% -> 4%
where the time goes in v5:
time: 179 us
  blocking collectives  117 us (65%)
  Pallas kernels  22.7 us (13%)
  starting transfers between devices  22.3 us (12%)
  waiting for transfers between devices  13.4 us (7%)
    all_to_all x3, blocking collectives, turn(): return lax.all_to_all(x, 'lat', 0, 0, tiled=True)  44.7 us
    all_to_all x1, blocking collectives, body(): whole = lax.all_to_all(sent, 'lon', 0, 0, tiled=True)  27.1 us
    all_to_all x1, blocking collectives, body(): lax.all_to_all(inverse(back_waves, False, scale, piece), 'lon', 0, 0, til...  22.9 us
    pallas_call x11, Pallas kernels, call(): pl.pallas_call(kernel, out_shape=shapes, in_specs=[pl.BlockSpec(memory_sp...  22.7 us
    all_to_all x1, blocking collectives, body(): smooth = lax.all_to_all(inverse(waves, True), 'lon', 0, 0, tiled=True)  22 us
    all_to_all x1, starting transfers between devices, turn(): return lax.all_to_all(x, 'lat', 0, 0, tiled=True)  11.7 us
    all_to_all x1, starting transfers between devices, body(): whole = lax.all_to_all(sent, 'lon', 0, 0, tiled=True)  10.6 us
    all_to_all x1, waiting for transfers between devices, body(): whole = lax.all_to_all(sent, 'lon', 0, 0, tiled=True)  9.29 us
  transfers between devices with their start and end apart: 2, of which 2 were waited for; matrix products, arithmetic and copies ran while one was open for 1% of the time, Pallas kernels for 4%

profile of v5, /device:TPU:1, one launch (start us, length us, event | category | flops | bytes accessed | tf_op | source)
XLA Modules:
  0.0 178.8 jit_solution(15200775944407684800)
XLA Ops:
  0.6 0.0 copy-start.2
  0.6 1.0 copy-done.2
  1.6 0.9 shard_map.76
  2.5 10.6 %all-to-all-start = ((bf16[32,8,640]{2,1,0:T(8,128)(2,1)}), bf16[32,8,640]{2,1,0:T(8,128)(2,1)S(1)}, u32[]{:S(2)}, u32[]{:S(2)}) async-start(bf16[32,8,640]{2,1,0:T(8,128)(2,1)} %shard_map.76), calls=%async_computation | async-start | bytes 655360 | tf_op jit(solution)/shard_map/all_to_all | solution.py:512
  13.1 1.1 fusion
  14.2 0.1 dynamic_slice.3
  14.3 0.1 rev.4
  14.4 0.1 broadcast_select_fusion
  14.5 0.1 broadcast_in_dim.16
  14.5 0.1 broadcast_in_dim_reshape.4.refs_2_
  14.6 0.0 copy-start.4
  14.6 1.8 %shard_map.77 = (bf16[768,768]{1,0:T(8,128)(2,1)S(1)}, bf16[768,768]{1,0:T(8,128)(2,1)S(1)}) custom-call(), custom_call_target="tpu_custom_call" | custom-call | flops 17694720 | bytes 4718592 | tf_op jit(solution)/shard_map/pallas_call | solution.py:24
  16.5 0.0 copy-start
  16.6 0.2 select_reduce_fusion
  16.8 9.3 %all-to-all-done.refs_0_ = bf16[32,8,640]{2,1,0:T(8,128)(2,1)S(1)} async-done(((bf16[32,8,640]{2,1,0:T(8,128)(2,1)}), bf16[32,8,640]{2,1,0:T(8,128)(2,1)S(1)}, u32[]{:S(2)}, u32[]{:S(2)}) %all-to-all-start) | async-done | bytes 327712 | tf_op jit(solution)/shard_map/all_to_all | solution.py:512
  26.0 2.0 %shard_map.78 = bf16[16,8,1152]{2,1,0:T(8,128)(2,1)} custom-call(bf16[32,8,640]{2,1,0:T(8,128)(2,1)S(1)} %all-to-all-done.refs_0_, bf16[768,768]{1,0:T(8,128)(2,1)S(1)} %get-tuple-element.12.refs_1_, f32[192,1]{1,0:T(8,128)S(1)} %broadcast_in_dim_reshape.4.refs_2_), custom_call_target="tpu_custom_call" | custom-call | tf_op jit(solution)/shard_map/pallas_call | solution.py:24
  28.1 0.0 copy-done.4
  28.1 0.0 copy-done
  28.1 11.7 %all-to-all-start.1 = ((bf16[16,8,1152]{2,1,0:T(8,128)(2,1)}), bf16[16,8,1152]{2,1,0:T(8,128)(2,1)}, u32[]{:S(2)}, u32[]{:S(2)}) async-start(bf16[16,8,1152]{2,1,0:T(8,128)(2,1)} %shard_map.78), calls=%async_computation.1 | async-start | bytes 589824 | tf_op jit(solution)/shard_map/all_to_all | solution.py:533
  39.9 0.1 multiply_add_fusion.diag_ref
  40.0 0.0 copy-start.9
  40.0 6.1 %shard_map.79.table_ref = bf16[192,6144]{1,0:T(8,128)(2,1)S(1)} custom-call(f32[8,192]{1,0:T(8,128)S(1)} %broadcast_in_dim.17.cos_ref, f32[24,192]{1,0:T(8,128)S(1)} %multiply_add_fusion.diag_ref), custom_call_target="tpu_custom_call" | custom-call | flops 40000000 | bytes 6000000 | tf_op jit(solution)/shard_map/pallas_call | solution.py:24
  46.0 4.1 %all-to-all-done.1.x_ref = bf16[16,8,1152]{2,1,0:T(8,128)(2,1)} async-done(((bf16[16,8,1152]{2,1,0:T(8,128)(2,1)}), bf16[16,8,1152]{2,1,0:T(8,128)(2,1)}, u32[]{:S(2)}, u32[]{:S(2)}) %all-to-all-start.1) | async-done | bytes 294944 | tf_op jit(solution)/shard_map/all_to_all | solution.py:533
  50.2 0.0 copy-done.9
  50.2 2.9 %shard_map.80 = bf16[16,8,1152]{2,1,0:T(8,128)(2,1)S(1)} custom-call(bf16[16,8,1152]{2,1,0:T(8,128)(2,1)} %all-to-all-done.1.x_ref, f32[8,384]{1,0:T(8,128)S(1)} %bitcast.7, bf16[192,6144]{1,0:T(8,128)(2,1)S(1)} %shard_map.79.table_ref), custom_call_target="tpu_custom_call" | custom-call | tf_op jit(solution)/shard_map/pallas_call | solution.py:24
  53.1 15.1 %all_to_all.40.refs_0_ = bf16[16,8,1152]{2,1,0:T(8,128)(2,1)S(1)} all-to-all(bf16[16,8,1152]{2,1,0:T(8,128)(2,1)S(1)} %shard_map.80), channel_id=1, replica_groups=mesh['lat'=16,'lon'=32] {'lat'}, dimensions={0} | all-to-all | bytes 589824 | tf_op jit(solution)/shard_map/all_to_all | solution.py:533
  68.2 0.0 copy-start.3
  68.2 0.0 copy-start.6
  68.2 0.0 copy-start.7
  68.2 0.0 copy-start.8
  68.2 1.3 shard_map.81
  69.5 22.0 %all_to_all.41.recv_ref = bf16[32,8,640]{2,1,0:T(8,128)(2,1)S(1)} all-to-all(bf16[32,8,640]{2,1,0:T(8,128)(2,1)S(1)} %shard_map.81), channel_id=1, replica_groups=mesh['lat'=16,'lon'=32] {'lon'}, dimensions={0} | all-to-all | bytes 655360 | tf_op jit(solution)/shard_map/all_to_all | solution.py:556
  91.5 0.0 copy-done.3
  91.5 0.0 copy-done.6
  91.5 0.0 copy-done.7
  91.5 0.0 copy-done.8
  91.5 2.2 %shard_map.82 = (bf16[32,8,1664]{2,1,0:T(8,128)(2,1)S(1)}, f32[576,256]{1,0:T(8,128)S(1)}) custom-call(bf16[32,8,640]{2,1,0:T(8,128)(2,1)S(1)} %all_to_all.41.recv_ref, bf16[24,24,256]{2,1,0:T(8,128)(2,1)S(1)} %bitcast.5, bf16[24,24,256]{2,1,0:T(8,128)(2,1)S(1)} %bitcast.6, bf16[256,512]{1,0:T(8,128)(2,1)S(1)} %copy-done.7, bf16[256,512]{1,0:T(8,128)(2,1)S(1)} %copy-done.8), custom_call_target="tpu_custom_call" | custom-call | tf_op jit(solution)/shard_map/pallas_call | solution.py:24
  93.7 0.0 copy-start.1
  93.7 27.1 %all_to_all.42.refs_0_ = bf16[32,8,1664]{2,1,0:T(8,128)(2,1)S(1)} all-to-all(bf16[32,8,1664]{2,1,0:T(8,128)(2,1)S(1)} %get-tuple-element.14), channel_id=1, replica_groups=mesh['lat'=16,'lon'=32] {'lon'}, dimensions={0} | all-to-all | bytes 1703936 | tf_op jit(solution)/shard_map/all_to_all | solution.py:576
  120.8 0.0 copy-done.1
  120.8 1.4 shard_map.83
  122.2 13.9 %all_to_all.43.x_ref = bf16[16,8,1280]{2,1,0:T(8,128)(2,1)S(1)} all-to-all(bf16[16,8,1280]{2,1,0:T(8,128)(2,1)S(1)} %shard_map.83), channel_id=1, replica_groups=mesh['lat'=16,'lon'=32] {'lat'}, dimensions={0} | all-to-all | bytes 655360 | tf_op jit(solution)/shard_map/all_to_all | solution.py:533
  136.1 2.0 %shard_map.84 = (bf16[16,8,1152]{2,1,0:T(8,128)(2,1)S(1)}, f32[8,128]{1,0:T(8,128)S(1)}) custom-call(bf16[16,8,1280]{2,1,0:T(8,128)(2,1)S(1)} %all_to_all.43.x_ref, f32[8,384]{1,0:T(8,128)S(1)} %bitcast.8, bf16[192,6144]{1,0:T(8,128)(2,1)S(1)} %shard_map.79.table_ref), custom_call_target="tpu_custom_call" | custom-call | tf_op jit(solution)/shard_map/pallas_call | solution.py:24
  138.1 15.7 %all_to_all.44.refs_0_ = bf16[16,8,1152]{2,1,0:T(8,128)(2,1)S(1)} all-to-all(bf16[16,8,1152]{2,1,0:T(8,128)(2,1)S(1)} %get-tuple-element.15), channel_id=1, replica_groups=mesh['lat'=16,'lon'=32] {'lat'}, dimensions={0} | all-to-all | bytes 589824 | tf_op jit(solution)/shard_map/all_to_all | solution.py:533
  153.8 0.0 copy-done.5
  153.8 1.3 shard_map.85
  155.1 22.9 %all_to_all.45.recv_ref = bf16[32,8,640]{2,1,0:T(8,128)(2,1)S(1)} all-to-all(bf16[32,8,640]{2,1,0:T(8,128)(2,1)S(1)} %shard_map.85), channel_id=1, replica_groups=mesh['lat'=16,'lon'=32] {'lon'}, dimensions={0} | all-to-all | bytes 655360 | tf_op jit(solution)/shard_map/all_to_all | solution.py:579
  177.9 0.9 shard_map.86
  (10 shorter events, 0.2 us)
Async XLA Ops:
  0.6 1.0 copy-start.2
  2.5 23.5 %all-to-all-start = ((bf16[32,8,640]{2,1,0:T(8,128)(2,1)}), bf16[32,8,640]{2,1,0:T(8,128)(2,1)S(1)}, u32[]{:S(2)}, u32[]{:S(2)}) async-start(bf16[32,8,640]{2,1,0:T(8,128)(2,1)} %shard_map.76), calls=%async_computation | async-start | bytes 655360 | tf_op jit(solution)/shard_map/all_to_all | solution.py:512
  14.6 13.4 %copy-start.4 = (f32[192,1]{1,0:T(8,128)}, f32[192,1]{1,0:T(8,128)S(1)}, u32[]{:S(2)}) copy-start(f32[192,1]{1,0:T(8,128)S(1)} %broadcast_in_dim_reshape.4.refs_2_) | copy-start | bytes 2308
  16.5 11.6 %copy-start = (bf16[768,768]{1,0:T(8,128)(2,1)}, bf16[768,768]{1,0:T(8,128)(2,1)S(1)}, u32[]{:S(2)}) copy-start(bf16[768,768]{1,0:T(8,128)(2,1)S(1)} %get-tuple-element.12.refs_1_) | copy-start | bytes 3538948
  28.1 22.1 %all-to-all-start.1 = ((bf16[16,8,1152]{2,1,0:T(8,128)(2,1)}), bf16[16,8,1152]{2,1,0:T(8,128)(2,1)}, u32[]{:S(2)}, u32[]{:S(2)}) async-start(bf16[16,8,1152]{2,1,0:T(8,128)(2,1)} %shard_map.78), calls=%async_computation.1 | async-start | bytes 589824 | tf_op jit(solution)/shard_map/all_to_all | solution.py:533
  40.0 10.2 %copy-start.9 = (f32[384,8]{0,1:T(8,128)S(1)}, f32[384,8]{0,1:T(8,128)}, u32[]{:S(2)}) copy-start(f32[384,8]{0,1:T(8,128)} %param.6) | copy-start | bytes 36868
  68.2 23.3 %copy-start.3 = (bf16[1,24,24,256]{3,2,1,0:T(8,128)(2,1)S(1)}, bf16[1,24,24,256]{3,2,1,0:T(8,128)(2,1)}, u32[]{:S(2)}) copy-start(bf16[1,24,24,256]{3,2,1,0:T(8,128)(2,1)} %param.5) | copy-start | bytes 884740
  68.2 23.3 %copy-start.6 = (bf16[1,24,24,256]{3,2,1,0:T(8,128)(2,1)S(1)}, bf16[1,24,24,256]{3,2,1,0:T(8,128)(2,1)}, u32[]{:S(2)}) copy-start(bf16[1,24,24,256]{3,2,1,0:T(8,128)(2,1)} %param.9) | copy-start | bytes 884740
  68.2 23.3 %copy-start.7 = (bf16[256,512]{1,0:T(8,128)(2,1)S(1)}, bf16[256,512]{1,0:T(8,128)(2,1)}, u32[]{:S(2)}) copy-start(bf16[256,512]{1,0:T(8,128)(2,1)} %up_ref.1) | copy-start | bytes 786436
  68.2 23.3 %copy-start.8 = (bf16[256,512]{1,0:T(8,128)(2,1)S(1)}, bf16[256,512]{1,0:T(8,128)(2,1)}, u32[]{:S(2)}) copy-start(bf16[256,512]{1,0:T(8,128)(2,1)} %down_ref.1) | copy-start | bytes 786436
  93.7 27.1 %copy-start.1 = (bf16[768,768]{1,0:T(8,128)(2,1)S(1)}, bf16[768,768]{1,0:T(8,128)(2,1)}, u32[]{:S(2)}) copy-start(bf16[768,768]{1,0:T(8,128)(2,1)} %copy-done) | copy-start | bytes 3538948
  136.1 17.7 %copy-start.5 = (f32[192,1]{1,0:T(8,128)S(1)}, f32[192,1]{1,0:T(8,128)}, u32[]{:S(2)}) copy-start(f32[192,1]{1,0:T(8,128)} %copy-done.4) | copy-start | bytes 2308

commit v6 on v5

--- a/solution.py
+++ b/solution.py
@@ -289,14 +289,12 @@
     lines = [pick(out_all, modes, c, rows, TILE) for c in range(TILE)]
     bands = out_ref.shape[0]
     per = modes // bands
-    share = 2 * TILE
+    line_lanes = TILE * per
     for t in range(bands):
-        for g in range(per // share):
-            at = t * per + g * share
-            tile = jnp.concatenate([line[:, at : at + share] for line in lines], axis=1).astype(BF16)
-            for i in range(rows // TILE):
-                lane = i * TILE * per + g * 128
-                out_ref[t, :, lane : lane + 128] = tile[i * TILE : (i + 1) * TILE]
+        tile = jnp.concatenate([line[:, t * per : (t + 1) * per] for line in lines], axis=1)
+        tile = tile.astype(BF16)
+        for i in range(rows // TILE):
+            out_ref[t, :, i * line_lanes : (i + 1) * line_lanes] = tile[i * TILE : (i + 1) * TILE]
     if skip:
         total = x_ref[0, :, used:].astype(F32)
         for b in range(1, chunks):
@@ -330,36 +328,36 @@
     gains = jnp.concatenate([filter_ref[...], filter_ref[...]], axis=0)
     north = list(range(bands // 2))
     south = [bands - 1 - t for t in north]
-    at = 0
-    for g in range(tiles):
-        depth = degrees - bands * TILE * g
-        for h, order in enumerate((north, south)):
+    for h, order in enumerate((north, south)):
+        for g in range(tiles):
             parts = [
                 x_ref[t, :, i * stride + g * 128 : i * stride + (g + 1) * 128].astype(F32)
                 for t in order
                 for i in range(blocks)
             ]
-            place(x_all, jnp.concatenate(parts, axis=0).T, h * 128, 128)
+            place(x_all, jnp.concatenate(parts, axis=0).T, h * stride + g * 128, 128)
+    step = stride // TILE
+    at = 0
+    for g in range(tiles):
+        depth = degrees - bands * TILE * g
         sign, gain = signs[:, degrees - depth :], gains[:, degrees - depth :]
         held = []
         for r in range(TILE):
-            starts = [h * 128 + 2 * r + p for h in range(2) for p in range(2)]
-            modes = [pick(x_all, half, start, TILE, 2 * TILE) for start in starts]
-            both = dot(
-                jnp.concatenate(modes, axis=0).astype(BF16), table_ref[:, at + r * depth : at + (r + 1) * depth]
-            )
-            spectrum = both[: 2 * TILE] + sign * both[2 * TILE :]
-            filtered = spectrum * gain
-            held.append(jnp.concatenate([filtered, sign * filtered], axis=0).astype(BF16))
-        for r in range(TILE):
-            waves = dot(held[r], table_ref[:, at + r * depth : at + (r + 1) * depth], ((1,), (1,)))
-            for h in range(2):
-                for p in range(2):
-                    i = 2 * h + p
-                    place(out_all, waves[i * TILE : (i + 1) * TILE], h * 128 + 2 * r + p, TILE, 2 * TILE)
-        at += TILE * depth
-        for h, order in enumerate((north, south)):
-            waves = pick(out_all, half, h * 128, 128).T.astype(BF16)
+            starts = [h * stride + 2 * (g * TILE + r) + p for h in range(2) for p in range(2)]
+            modes = [pick(x_all, half, start, TILE, step) for start in starts]
+            table = table_ref[:, at : at + depth]
+            both = dot(jnp.concatenate(modes, axis=0).astype(BF16), table)
+            filtered = (both[: 2 * TILE] + sign * both[2 * TILE :]) * gain
+            filtered = jnp.concatenate([filtered, sign * filtered], axis=0).astype(BF16)
+            held.append((at, starts, filtered))
+            at += depth
+        for first, starts, filtered in held:
+            waves = dot(filtered, table_ref[:, first : first + depth], ((1,), (1,)))
+            for i, start in enumerate(starts):
+                place(out_all, waves[i * TILE : (i + 1) * TILE], start, TILE, step)
+    for h, order in enumerate((north, south)):
+        for g in range(tiles):
+            waves = pick(out_all, half, h * stride + g * 128, 128).T.astype(BF16)
             for n, t in enumerate(order):
                 for i in range(blocks):
                     lane = i * stride + g * 128
@@ -375,24 +373,15 @@
     bands = x_ref.shape[0]
     blocks = rows // TILE
     stride = x_ref.shape[2] // blocks
-    share = 2 * TILE
+    share = stride // TILE
     held = [
-        [
-            jnp.concatenate(
-                [
-                    x_ref[t, :, i * stride + g * 128 : i * stride + (g + 1) * 128].astype(F32)
-                    for i in range(blocks)
-                ],
-                axis=0,
-            )
-            for g in range(stride // 128)
-        ]
+        jnp.concatenate(
+            [x_ref[t, :, i * stride : (i + 1) * stride].astype(F32) for i in range(blocks)], axis=0
+        )
         for t in range(bands)
     ]
     for c in range(TILE):
-        line = jnp.concatenate(
-            [tile[:, c * share : (c + 1) * share] for one in held for tile in one], axis=1
-        )
+        line = jnp.concatenate([one[:, c * share : (c + 1) * share] for one in held], axis=1)
         place(x_all, line, c, rows, TILE)
     modes = table_ref.shape[0]
     x = pick(x_all, modes)
@@ -540,7 +529,7 @@
             functools.partial(spectral_kernel, rows, tiles, has_piece),
             outs,
             x, gains, legendre,
-            scratch=[tiles_of(256, lat_total // 2)] * 2,
+            scratch=[tiles_of(2 * line, lat_total // 2)] * 2,
         )
 
     def inverse(x, doubled, *extra):

time: 179 us -> 179 us (level)
  no operation moved by 1% of the time
where the time goes in v6:
time: 179 us; the launch traced here: 178 us
  blocking collectives  117 us (65%)
  starting transfers between devices  22.3 us (12%)
  Pallas kernels  21.8 us (12%)
  waiting for transfers between devices  13.4 us (7%)
    all_to_all x3, blocking collectives, turn(): return lax.all_to_all(x, 'lat', 0, 0, tiled=True)  44.6 us
    all_to_all x1, blocking collectives, body(): whole = lax.all_to_all(sent, 'lon', 0, 0, tiled=True)  27.1 us
    all_to_all x1, blocking collectives, body(): lax.all_to_all(inverse(back_waves, False, scale, piece), 'lon', 0, 0, til...  23 us
    all_to_all x1, blocking collectives, body(): smooth = lax.all_to_all(inverse(waves, True), 'lon', 0, 0, tiled=True)  22 us
    pallas_call x11, Pallas kernels, call(): pl.pallas_call(kernel, out_shape=shapes, in_specs=[pl.BlockSpec(memory_sp...  21.8 us
    all_to_all x1, starting transfers between devices, turn(): return lax.all_to_all(x, 'lat', 0, 0, tiled=True)  11.7 us
    all_to_all x1, starting transfers between devices, body(): whole = lax.all_to_all(sent, 'lon', 0, 0, tiled=True)  10.6 us
    all_to_all x1, waiting for transfers between devices, body(): whole = lax.all_to_all(sent, 'lon', 0, 0, tiled=True)  9.29 us
  transfers between devices with their start and end apart: 2, of which 2 were waited for; matrix products, arithmetic and copies ran while one was open for 1% of the time, Pallas kernels for 4%

profile of v6, /device:TPU:1, one launch (start us, length us, event | category | flops | bytes accessed | tf_op | source)
XLA Modules:
  0.0 178.0 jit_solution(233408945539582840)
XLA Ops:
  0.6 0.0 copy-start.2
  0.6 1.0 copy-done.2
  1.6 0.9 shard_map.76
  2.5 10.6 %all-to-all-start = ((bf16[32,8,640]{2,1,0:T(8,128)(2,1)}), bf16[32,8,640]{2,1,0:T(8,128)(2,1)S(1)}, u32[]{:S(2)}, u32[]{:S(2)}) async-start(bf16[32,8,640]{2,1,0:T(8,128)(2,1)} %shard_map.76), calls=%async_computation | async-start | bytes 655360 | tf_op jit(solution)/shard_map/all_to_all | solution.py:501
  13.1 1.1 fusion
  14.2 0.1 dynamic_slice.3
  14.3 0.1 rev.4
  14.4 0.1 broadcast_select_fusion
  14.5 0.1 broadcast_in_dim.16
  14.5 0.1 broadcast_in_dim_reshape.4.refs_2_
  14.6 0.0 copy-start.4
  14.6 1.8 %shard_map.77 = (bf16[768,768]{1,0:T(8,128)(2,1)S(1)}, bf16[768,768]{1,0:T(8,128)(2,1)S(1)}) custom-call(), custom_call_target="tpu_custom_call" | custom-call | flops 17694720 | bytes 4718592 | tf_op jit(solution)/shard_map/pallas_call | solution.py:24
  16.5 0.0 copy-start
  16.6 0.2 select_reduce_fusion
  16.8 9.3 %all-to-all-done.refs_0_ = bf16[32,8,640]{2,1,0:T(8,128)(2,1)S(1)} async-done(((bf16[32,8,640]{2,1,0:T(8,128)(2,1)}), bf16[32,8,640]{2,1,0:T(8,128)(2,1)S(1)}, u32[]{:S(2)}, u32[]{:S(2)}) %all-to-all-start) | async-done | bytes 327712 | tf_op jit(solution)/shard_map/all_to_all | solution.py:501
  26.0 1.7 shard_map.78
  27.8 0.0 copy-done.4
  27.8 0.0 copy-done
  27.8 11.7 %all-to-all-start.1 = ((bf16[16,8,1152]{2,1,0:T(8,128)(2,1)}), bf16[16,8,1152]{2,1,0:T(8,128)(2,1)}, u32[]{:S(2)}, u32[]{:S(2)}) async-start(bf16[16,8,1152]{2,1,0:T(8,128)(2,1)} %shard_map.78), calls=%async_computation.1 | async-start | bytes 589824 | tf_op jit(solution)/shard_map/all_to_all | solution.py:522
  39.6 0.1 multiply_add_fusion.diag_ref
  39.7 0.0 copy-start.9
  39.7 6.1 %shard_map.79.table_ref = bf16[192,6144]{1,0:T(8,128)(2,1)S(1)} custom-call(f32[8,192]{1,0:T(8,128)S(1)} %broadcast_in_dim.17.cos_ref, f32[24,192]{1,0:T(8,128)S(1)} %multiply_add_fusion.diag_ref), custom_call_target="tpu_custom_call" | custom-call | flops 40000000 | bytes 6000000 | tf_op jit(solution)/shard_map/pallas_call | solution.py:24
  45.8 4.1 %all-to-all-done.1.x_ref = bf16[16,8,1152]{2,1,0:T(8,128)(2,1)} async-done(((bf16[16,8,1152]{2,1,0:T(8,128)(2,1)}), bf16[16,8,1152]{2,1,0:T(8,128)(2,1)}, u32[]{:S(2)}, u32[]{:S(2)}) %all-to-all-start.1) | async-done | bytes 294944 | tf_op jit(solution)/shard_map/all_to_all | solution.py:522
  49.9 0.0 copy-done.9
  49.9 3.0 %shard_map.80 = bf16[16,8,1152]{2,1,0:T(8,128)(2,1)S(1)} custom-call(bf16[16,8,1152]{2,1,0:T(8,128)(2,1)} %all-to-all-done.1.x_ref, f32[8,384]{1,0:T(8,128)S(1)} %bitcast.7, bf16[192,6144]{1,0:T(8,128)(2,1)S(1)} %shard_map.79.table_ref), custom_call_target="tpu_custom_call" | custom-call | tf_op jit(solution)/shard_map/pallas_call | solution.py:24
  52.9 15.1 %all_to_all.40.refs_0_ = bf16[16,8,1152]{2,1,0:T(8,128)(2,1)S(1)} all-to-all(bf16[16,8,1152]{2,1,0:T(8,128)(2,1)S(1)} %shard_map.80), channel_id=1, replica_groups=mesh['lat'=16,'lon'=32] {'lat'}, dimensions={0} | all-to-all | bytes 589824 | tf_op jit(solution)/shard_map/all_to_all | solution.py:522
  68.0 0.0 copy-start.3
  68.0 0.0 copy-start.6
  68.0 0.0 copy-start.7
  68.0 0.0 copy-start.8
  68.0 1.0 shard_map.81
  69.0 22.0 %all_to_all.41.recv_ref = bf16[32,8,640]{2,1,0:T(8,128)(2,1)S(1)} all-to-all(bf16[32,8,640]{2,1,0:T(8,128)(2,1)S(1)} %shard_map.81), channel_id=1, replica_groups=mesh['lat'=16,'lon'=32] {'lon'}, dimensions={0} | all-to-all | bytes 655360 | tf_op jit(solution)/shard_map/all_to_all | solution.py:545
  91.0 0.0 copy-done.3
  91.0 0.0 copy-done.6
  91.0 0.0 copy-done.7
  91.0 0.0 copy-done.8
  91.0 2.2 %shard_map.82 = (bf16[32,8,1664]{2,1,0:T(8,128)(2,1)S(1)}, f32[576,256]{1,0:T(8,128)S(1)}) custom-call(bf16[32,8,640]{2,1,0:T(8,128)(2,1)S(1)} %all_to_all.41.recv_ref, bf16[24,24,256]{2,1,0:T(8,128)(2,1)S(1)} %bitcast.5, bf16[24,24,256]{2,1,0:T(8,128)(2,1)S(1)} %bitcast.6, bf16[256,512]{1,0:T(8,128)(2,1)S(1)} %copy-done.7, bf16[256,512]{1,0:T(8,128)(2,1)S(1)} %copy-done.8), custom_call_target="tpu_custom_call" | custom-call | tf_op jit(solution)/shard_map/pallas_call | solution.py:24
  93.2 0.0 copy-start.1
  93.2 27.1 %all_to_all.42.refs_0_ = bf16[32,8,1664]{2,1,0:T(8,128)(2,1)S(1)} all-to-all(bf16[32,8,1664]{2,1,0:T(8,128)(2,1)S(1)} %get-tuple-element.14), channel_id=1, replica_groups=mesh['lat'=16,'lon'=32] {'lon'}, dimensions={0} | all-to-all | bytes 1703936 | tf_op jit(solution)/shard_map/all_to_all | solution.py:565
  120.3 0.0 copy-done.1
  120.3 1.1 shard_map.83
  121.4 13.9 %all_to_all.43.x_ref = bf16[16,8,1280]{2,1,0:T(8,128)(2,1)S(1)} all-to-all(bf16[16,8,1280]{2,1,0:T(8,128)(2,1)S(1)} %shard_map.83), channel_id=1, replica_groups=mesh['lat'=16,'lon'=32] {'lat'}, dimensions={0} | all-to-all | bytes 655360 | tf_op jit(solution)/shard_map/all_to_all | solution.py:522
  135.4 2.0 %shard_map.84 = (bf16[16,8,1152]{2,1,0:T(8,128)(2,1)S(1)}, f32[8,128]{1,0:T(8,128)S(1)}) custom-call(bf16[16,8,1280]{2,1,0:T(8,128)(2,1)S(1)} %all_to_all.43.x_ref, f32[8,384]{1,0:T(8,128)S(1)} %bitcast.8, bf16[192,6144]{1,0:T(8,128)(2,1)S(1)} %shard_map.79.table_ref), custom_call_target="tpu_custom_call" | custom-call | tf_op jit(solution)/shard_map/pallas_call | solution.py:24
  137.4 15.6 %all_to_all.44.refs_0_ = bf16[16,8,1152]{2,1,0:T(8,128)(2,1)S(1)} all-to-all(bf16[16,8,1152]{2,1,0:T(8,128)(2,1)S(1)} %get-tuple-element.15), channel_id=1, replica_groups=mesh['lat'=16,'lon'=32] {'lat'}, dimensions={0} | all-to-all | bytes 589824 | tf_op jit(solution)/shard_map/all_to_all | solution.py:522
  153.0 0.0 copy-done.5
  153.0 1.0 shard_map.85
  154.0 23.0 %all_to_all.45.recv_ref = bf16[32,8,640]{2,1,0:T(8,128)(2,1)S(1)} all-to-all(bf16[32,8,640]{2,1,0:T(8,128)(2,1)S(1)} %shard_map.85), channel_id=1, replica_groups=mesh['lat'=16,'lon'=32] {'lon'}, dimensions={0} | all-to-all | bytes 655360 | tf_op jit(solution)/shard_map/all_to_all | solution.py:568
  177.1 0.9 shard_map.86
  (10 shorter events, 0.2 us)
Async XLA Ops:
  0.6 1.0 copy-start.2
  2.5 23.5 %all-to-all-start = ((bf16[32,8,640]{2,1,0:T(8,128)(2,1)}), bf16[32,8,640]{2,1,0:T(8,128)(2,1)S(1)}, u32[]{:S(2)}, u32[]{:S(2)}) async-start(bf16[32,8,640]{2,1,0:T(8,128)(2,1)} %shard_map.76), calls=%async_computation | async-start | bytes 655360 | tf_op jit(solution)/shard_map/all_to_all | solution.py:501
  14.6 13.2 %copy-start.4 = (f32[192,1]{1,0:T(8,128)}, f32[192,1]{1,0:T(8,128)S(1)}, u32[]{:S(2)}) copy-start(f32[192,1]{1,0:T(8,128)S(1)} %broadcast_in_dim_reshape.4.refs_2_) | copy-start | bytes 2308
  16.5 11.3 %copy-start = (bf16[768,768]{1,0:T(8,128)(2,1)}, bf16[768,768]{1,0:T(8,128)(2,1)S(1)}, u32[]{:S(2)}) copy-start(bf16[768,768]{1,0:T(8,128)(2,1)S(1)} %get-tuple-element.12.refs_1_) | copy-start | bytes 3538948
  27.8 22.1 %all-to-all-start.1 = ((bf16[16,8,1152]{2,1,0:T(8,128)(2,1)}), bf16[16,8,1152]{2,1,0:T(8,128)(2,1)}, u32[]{:S(2)}, u32[]{:S(2)}) async-start(bf16[16,8,1152]{2,1,0:T(8,128)(2,1)} %shard_map.78), calls=%async_computation.1 | async-start | bytes 589824 | tf_op jit(solution)/shard_map/all_to_all | solution.py:522
  39.7 10.2 %copy-start.9 = (f32[384,8]{0,1:T(8,128)S(1)}, f32[384,8]{0,1:T(8,128)}, u32[]{:S(2)}) copy-start(f32[384,8]{0,1:T(8,128)} %param.6) | copy-start | bytes 36868
  68.0 23.0 %copy-start.3 = (bf16[1,24,24,256]{3,2,1,0:T(8,128)(2,1)S(1)}, bf16[1,24,24,256]{3,2,1,0:T(8,128)(2,1)}, u32[]{:S(2)}) copy-start(bf16[1,24,24,256]{3,2,1,0:T(8,128)(2,1)} %param.5) | copy-start | bytes 884740
  68.0 23.0 %copy-start.6 = (bf16[1,24,24,256]{3,2,1,0:T(8,128)(2,1)S(1)}, bf16[1,24,24,256]{3,2,1,0:T(8,128)(2,1)}, u32[]{:S(2)}) copy-start(bf16[1,24,24,256]{3,2,1,0:T(8,128)(2,1)} %param.9) | copy-start | bytes 884740
  68.0 23.0 %copy-start.7 = (bf16[256,512]{1,0:T(8,128)(2,1)S(1)}, bf16[256,512]{1,0:T(8,128)(2,1)}, u32[]{:S(2)}) copy-start(bf16[256,512]{1,0:T(8,128)(2,1)} %up_ref.1) | copy-start | bytes 786436
  68.0 23.0 %copy-start.8 = (bf16[256,512]{1,0:T(8,128)(2,1)S(1)}, bf16[256,512]{1,0:T(8,128)(2,1)}, u32[]{:S(2)}) copy-start(bf16[256,512]{1,0:T(8,128)(2,1)} %down_ref.1) | copy-start | bytes 786436
  93.2 27.2 %copy-start.1 = (bf16[768,768]{1,0:T(8,128)(2,1)S(1)}, bf16[768,768]{1,0:T(8,128)(2,1)}, u32[]{:S(2)}) copy-start(bf16[768,768]{1,0:T(8,128)(2,1)} %copy-done) | copy-start | bytes 3538948
  135.4 17.6 %copy-start.5 = (f32[192,1]{1,0:T(8,128)S(1)}, f32[192,1]{1,0:T(8,128)}, u32[]{:S(2)}) copy-start(f32[192,1]{1,0:T(8,128)} %copy-done.4) | copy-start | bytes 2308
